TPU v7x, 32 devices: a whole 2x2x4 slice. The times are simulated.
32 devices in a mesh: seq: 8 (over z, x), kv: 4 (over y, core).
Axes of the slice: x: 2, y: 2, z: 4, core: 2. Of those that a mesh axis runs over, the one named last changes fastest.
Arguments:
- queries: bfloat16 [4096, 1024], P('seq'), may hold values from -88 to 88
- keys: bfloat16 [64, 64, 1024], P('seq', 'kv'), may hold values from -4 to 4
- values: bfloat16 [64, 64, 1024], P('seq', 'kv'), may hold values from -6 to 6
- layout: int32 [64, 15], replicated, may hold values from -1 to 63, as said below
- grad_out: bfloat16 [4096, 1024], P('seq'), may hold values from -6 to 6
Outputs:
- attended: bfloat16 [4096, 1024], P('seq')
- grad_q: bfloat16 [4096, 1024], P('seq')
- grad_k: bfloat16 [64, 64, 1024], P('seq', 'kv')
- grad_v: bfloat16 [64, 64, 1024], P('seq', 'kv')
Inputs may be any that keep to these rules, and one draw needn't show every extreme that they name: `layout`: write query block b as 8 w + i with 0 <= i < 8. Row b lists the summary block of each window 0 .. w - 1 in order of windows, then the blocks 8 w .. 8 w + i in order, then -1 in the remaining entries. The summary block of window u is one of the blocks 8 u .. 8 u + 7 and is the same in every row.
All inputs are finite; a program needn't handle non-finite values.
Results may differ from a plain program's by a relative error of at most 0.038.
Values may be sent and summed in bfloat16 or wider, within the bound.
No kernel may reach another device: no remote copies, remote signals or barrier semaphores. Data moves between devices by JAX's collectives and lax.ppermute only.
A program may use at most 128 MiB of HBM per device.

v0:
```python
import functools
import math

import jax
import jax.numpy as jnp
from jax import lax
from jax.experimental import pallas as pl
from jax.experimental.pallas import tpu as pltpu
from jax.sharding import PartitionSpec as P

HEADS = 8
COLUMNS = 2
HIDDEN = -1e30
NT = (((1,), (1,)), ((), ()))
NN = (((1,), (0,)), ((), ()))
TN = (((0,), (0,)), ((), ()))
WHOLE = pl.BlockSpec(memory_space=pltpu.VMEM)
LIMIT = pltpu.CompilerParams(vmem_limit_bytes=28 * 1024 * 1024)


def dot(a, b, dims):
    return lax.dot_general(a, b, dims, preferred_element_type=jnp.float32)


def base2_scale(head_dim):
    return math.log2(math.e) / math.sqrt(head_dim)


def pick_kernel(table_ref, keys_ref, values_ref, pair_ref, both_ref):
    window = lax.axis_index("seq")
    blocks = keys_ref.shape[0]
    pick = jnp.minimum(window, lax.axis_size("seq") - 2)
    block = table_ref[pick, table_ref.shape[1] - 1] - window * blocks
    block = jnp.clip(block, 0, blocks - 1)
    pair_ref[0] = keys_ref[block]
    pair_ref[1] = values_ref[block]
    both_ref[0] = keys_ref[...]
    both_ref[1] = values_ref[...]


def pick_pair(table, keys, values):
    _, part_tok, feat_width = keys.shape
    return pl.pallas_call(
        pick_kernel,
        in_specs=[pl.BlockSpec(memory_space=pltpu.SMEM), WHOLE, WHOLE],
        out_specs=[WHOLE, WHOLE],
        out_shape=[
            jax.ShapeDtypeStruct((2, part_tok, feat_width), keys.dtype),
            jax.ShapeDtypeStruct((2,) + keys.shape, keys.dtype),
        ],
    )(table, keys, values)


def near_tiles(rows, near):
    half = rows // 2
    return [(0, half, near // 2), (half, half, near)]


def fill_near_bias(bias_ref, members, near, blk_len, part_tok):
    member = lax.axis_index("kv")
    shift = part_tok.bit_length() - 1
    for start, count, used in near_tiles(bias_ref.shape[0], near):
        row = start + lax.broadcasted_iota(jnp.int32, (count, 1), 0)
        col = lax.broadcasted_iota(jnp.int32, (1, used), 1)
        key_tok = (col >> shift) * blk_len + (col & (part_tok - 1))
        for j in range(members):
            key_pos = key_tok + (member ^ j) * part_tok
            bias_ref[start : start + count, j * used : (j + 1) * used] = jnp.where(
                key_pos <= row, 0.0, HIDDEN
            )


def head_columns(head, feat_width):
    head_dim = feat_width // HEADS
    return pl.ds(pl.multiple_of(head * head_dim, head_dim), head_dim)


def near_forward_kernel(members, blk_len, part_tok, q_ref, *refs):
    parts = refs[:members]
    out_ref, stat_ref, bias_ref = refs[members:]
    rows, feat_width = q_ref.shape
    head_dim = feat_width // HEADS
    near = parts[0].shape[1]
    fill_near_bias(bias_ref, members, near, blk_len, part_tok)

    @pl.loop(0, HEADS)
    def _(head):
        cols = head_columns(head, feat_width)
        for start, count, used in near_tiles(rows, near):
            here = pl.ds(start, count)
            keys = jnp.concatenate([ref[0, :used, cols] for ref in parts], axis=0)
            values = jnp.concatenate([ref[1, :used, cols] for ref in parts], axis=0)
            raw = dot(q_ref[here, cols], keys, NT) * base2_scale(head_dim)
            raw += bias_ref[here, : members * used]
            peak = jnp.max(raw, axis=1, keepdims=True)
            weight = jnp.exp2(raw - peak)
            total = jnp.sum(weight, axis=1, keepdims=True)
            stat_ref[here, cols] = jnp.broadcast_to(peak + jnp.log2(total), (count, head_dim))
            out_ref[here, cols] = dot(weight.astype(jnp.bfloat16), values, NN) * (1.0 / total)


def far_kernel(members, tile, q_ref, g_ref, sum_ref, stat_ref, *refs):
    parts = refs[: COLUMNS * members]
    att_ref, gq_ref, stat_out_ref = refs[COLUMNS * members : COLUMNS * members + 3]
    grad_refs = refs[COLUMNS * members + 3 :]
    rows, feat_width = q_ref.shape
    head_dim = feat_width // HEADS
    steps, _, part_tok, _ = parts[0].shape
    span = steps * part_tok
    width = COLUMNS * span
    score_scale = 1.0 / math.sqrt(head_dim)
    window = lax.axis_index("seq")
    level, side = window // COLUMNS, window % COLUMNS
    step = lax.broadcasted_iota(jnp.int32, (1, span), 1) >> (part_tok.bit_length() - 1)
    valid = [(step >= 1) & (step <= level), (step >= 1 - side) & (step <= level)]
    bias = jnp.concatenate([jnp.where(ok, 0.0, HIDDEN) for ok in valid] * members, axis=1)
    lane = lax.broadcasted_iota(jnp.int32, (tile, head_dim), 1)

    @pl.loop(0, HEADS)
    def _(head):
        cols = head_columns(head, feat_width)
        keys = jnp.concatenate([ref[:, 0, :, cols].reshape(span, head_dim) for ref in parts], axis=0)
        values = jnp.concatenate([ref[:, 1, :, cols].reshape(span, head_dim) for ref in parts], axis=0)
        key_grad = jnp.zeros((width, head_dim), jnp.float32)
        value_grad = jnp.zeros((width, head_dim), jnp.float32)
        for start in range(0, rows, tile):
            here = pl.ds(start, tile)
            query = q_ref[here, cols]
            grad = g_ref[here, cols]
            raw = dot(query, keys, NT) * base2_scale(head_dim) + bias
            near_level = stat_ref[here, cols][:, 0:1]
            peak = jnp.maximum(near_level, jnp.max(raw, axis=1, keepdims=True))
            near_weight = jnp.exp2(near_level - peak)
            weight = jnp.exp2(raw - peak)
            total = near_weight + jnp.sum(weight, axis=1, keepdims=True)
            inverse = 1.0 / total
            summed = sum_ref[here, cols] * near_weight
            summed += dot(weight.astype(jnp.bfloat16), values, NN)
            attended = (summed * inverse).astype(jnp.bfloat16)
            att_ref[here, cols] = attended
            drift = jnp.sum(
                grad.astype(jnp.float32) * attended.astype(jnp.float32), axis=1, keepdims=True
            )
            stat_out_ref[here, cols] = jnp.where(
                lane < head_dim // 2, peak + jnp.log2(total), drift
            )
            moved = weight * (dot(grad, values, NT) - drift)
            gq_ref[here, cols] = dot(moved.astype(jnp.bfloat16), keys, NN) * (inverse * score_scale)
            own_score = (moved[:, :width] * (inverse * score_scale)).astype(jnp.bfloat16)
            own_prob = (weight[:, :width] * inverse).astype(jnp.bfloat16)
            key_grad += dot(own_score, query, TN)
            value_grad += dot(own_prob, grad, TN)
        for c, ref in enumerate(grad_refs):
            shape = (steps, part_tok, head_dim)
            used = slice(c * span, (c + 1) * span)
            ref[:, 0, :, cols] = key_grad[used].astype(jnp.bfloat16).reshape(shape)
            ref[:, 1, :, cols] = value_grad[used].astype(jnp.bfloat16).reshape(shape)


def near_backward_kernel(members, blk_len, part_tok, q_ref, g_ref, stat_ref, far_gq_ref, *refs):
    parts = refs[:members]
    gq_ref, gk_ref, gv_ref, bias_ref = refs[members:]
    rows, feat_width = q_ref.shape
    head_dim = feat_width // HEADS
    near = parts[0].shape[1]
    score_scale = 1.0 / math.sqrt(head_dim)
    fill_near_bias(bias_ref, members, near, blk_len, part_tok)

    @pl.loop(0, HEADS)
    def _(head):
        cols = head_columns(head, feat_width)
        for start, count, used in reversed(near_tiles(rows, near)):
            here = pl.ds(start, count)
            query = q_ref[here, cols]
            grad = g_ref[here, cols]
            keys = jnp.concatenate([ref[0, :used, cols] for ref in parts], axis=0)
            values = jnp.concatenate([ref[1, :used, cols] for ref in parts], axis=0)
            stat = stat_ref[here, cols]
            level = stat[:, 0:1]
            drift = stat[:, head_dim // 2 : head_dim // 2 + 1]
            raw = dot(query, keys, NT) * base2_scale(head_dim)
            raw += bias_ref[here, : members * used]
            prob = jnp.exp2(raw - level)
            moved = prob * (dot(grad, values, NT) - drift)
            gq_ref[here, cols] = (
                dot(moved.astype(jnp.bfloat16), keys, NN) * score_scale + far_gq_ref[here, cols]
            ).astype(jnp.bfloat16)
            key_grad = dot((moved[:, :used] * score_scale).astype(jnp.bfloat16), query, TN)
            value_grad = dot(prob[:, :used].astype(jnp.bfloat16), grad, TN)
            if used == near:
                gk_ref[:, cols] = key_grad
                gv_ref[:, cols] = value_grad
            else:
                gk_ref[:used, cols] += key_grad
                gv_ref[:used, cols] += value_grad


def call(kernel, operands, outs, scratch, pairs, products, head_dim):
    moved_bytes = sum(a.size * a.dtype.itemsize for a in operands)
    return pl.pallas_call(
        kernel,
        in_specs=[WHOLE] * len(operands),
        out_specs=[WHOLE] * len(outs),
        scratch_shapes=scratch,
        out_shape=outs,
        compiler_params=LIMIT,
        cost_estimate=pl.CostEstimate(
            flops=4 * products * pairs * head_dim, bytes_accessed=moved_bytes, transcendentals=pairs
        ),
    )(*operands)


def shards(queries, keys, values, layout, grad_out):
    seq_count = lax.axis_size("seq")
    seq_index = lax.axis_index("seq")
    members = lax.axis_size("kv")
    tok_rows, feat_width = queries.shape
    blocks, part_tok = (keys.shape[0], keys.shape[1])
    blk_len = part_tok * members
    near = blocks * part_tok
    head_dim = feat_width // HEADS
    levels = seq_count // COLUMNS
    pick_window = jnp.minimum(seq_index, seq_count - 2)
    last_row = layout[layout.shape[0] - 1]
    summary_local = jnp.clip(last_row[pick_window] - seq_index * blocks, 0, blocks - 1)

    def hop(part, column_step, member_step):
        pairs = [
            (s * members + m, (s ^ column_step) * members + (m ^ member_step))
            for s in range(seq_count)
            for m in range(members)
        ]
        return lax.ppermute(part, ("seq", "kv"), pairs)

    def climb(part, d):
        return lax.ppermute(
            part, "seq", [(s, s + COLUMNS * d) for s in range(seq_count - COLUMNS * d)]
        )

    def sink(part, d):
        return lax.ppermute(
            part, "seq", [(s, s - COLUMNS * d) for s in range(COLUMNS * d, seq_count)]
        )

    own_pair, both = pick_pair(layout.T, keys, values)
    both = both.reshape(2, near, feat_width)
    near_parts = [both] + [hop(both, 0, step) for step in range(2, members, 2)]
    near_parts = [p for part in near_parts for p in (part, hop(part, 0, 1))]
    column = jnp.stack([own_pair] + [climb(own_pair, d) for d in range(1, levels)])
    far_parts = []
    for step in range(0, members, 2):
        group = [
            column if (c, step) == (0, 0) else hop(column, c, step) for c in range(COLUMNS)
        ]
        far_parts += group + [hop(part, 0, 1) for part in group]

    def rows_out(dtype):
        return jax.ShapeDtypeStruct((tok_rows, feat_width), dtype)

    near_out = jax.ShapeDtypeStruct((near, feat_width), jnp.float32)
    far_out = jax.ShapeDtypeStruct(column.shape, jnp.bfloat16)
    bias_scratch = [pltpu.VMEM((tok_rows, members * near), jnp.float32)]
    near_pairs = HEADS * tok_rows * members * near
    far_pairs = HEADS * tok_rows * members * seq_count * part_tok
    tile = min(256, max(64, 2**18 // (members * seq_count * part_tok)))

    near_sum, near_stat = call(
        functools.partial(near_forward_kernel, members, blk_len, part_tok),
        [queries] + near_parts,
        [rows_out(jnp.float32), rows_out(jnp.float32)],
        bias_scratch,
        near_pairs,
        2,
        head_dim,
    )
    attended, far_gq, stat, own_grad, cross_grad = call(
        functools.partial(far_kernel, members, tile),
        [queries, grad_out, near_sum, near_stat] + far_parts,
        [rows_out(jnp.bfloat16), rows_out(jnp.float32), rows_out(jnp.float32), far_out, far_out],
        [],
        far_pairs,
        5,
        head_dim,
    )
    crossed = hop(cross_grad, 1, 0)
    returned = [crossed[0].astype(jnp.float32)]
    for d in range(1, levels):
        summed = own_grad[d].astype(jnp.float32) + crossed[d].astype(jnp.float32)
        returned.append(sink(summed.astype(jnp.bfloat16), d).astype(jnp.float32))
    grad_q, near_k, near_v = call(
        functools.partial(near_backward_kernel, members, blk_len, part_tok),
        [queries, grad_out, stat, far_gq] + near_parts,
        [rows_out(jnp.bfloat16), near_out, near_out],
        bias_scratch,
        near_pairs,
        4,
        head_dim,
    )
    extra = functools.reduce(lambda a, b: a + b, returned)
    chosen = (jnp.arange(blocks) == summary_local)[:, None, None]

    def finish(near_term, far_term):
        near_term = near_term.reshape(blocks, part_tok, feat_width)
        return (near_term + jnp.where(chosen, far_term[None], 0.0)).astype(jnp.bfloat16)

    return (attended, grad_q, finish(near_k, extra[0]), finish(near_v, extra[1]))


def solution(mesh):
    return jax.shard_map(
        shards,
        mesh=mesh,
        in_specs=(P("seq", None), P("seq", "kv", None), P("seq", "kv", None), P(), P("seq", None)),
        out_specs=(P("seq", None), P("seq", None), P("seq", "kv", None), P("seq", "kv", None)),
        check_vma=False,
    )
```

profile of v0, /device:TPU:0, one launch (start us, length us, event | category | flops | bytes accessed | tf_op | source)
XLA Modules:
  0.0 99.2 jit_solution(5233692274146089477)
XLA Ops:
  0.6 1.9 %shard_map.84 = (bf16[2,16,1024]{2,1,0:T(8,128)(2,1)}, bf16[2,8,16,1024]{3,2,1,0:T(8,128)(2,1)}) custom-call(s32[15,64]{1,0:T(8,128)} %bitcast.34, bf16[8,16,1024]{2,1,0:T(8,128)(2,1)} %keys_ref.1, bf16[8,16,1024]{2,1,0:T(8,128)(2,1)} %values_ref.1), custom_call_target="tpu_custom_call" | custom-call | tf_op jit(solution)/shard_map/pallas_call | solution.py:43
  2.5 3.0 %collective-permute-start.1 = (bf16[2,128,1024]{2,1,0:T(8,128)(2,1)}, bf16[2,128,1024]{2,1,0:T(8,128)(2,1)S(1)}, u32[]{:S(2)}, u32[]{:S(2)}) collective-permute-start(bf16[2,128,1024]{2,1,0:T(8,128)(2,1)} %bitcast.26), channel_id=1, source_target_pairs={{0,2},{1,3},{2,0},{3,1},{4,6},{5,7},{6,4},{7,5},{8,10},{9,11},{10,... | collective-permute-start | bytes 1572872 | tf_op jit(solution)/shard_map/ppermute | solution.py:233
  5.5 12.1 %collective-permute-done.1.refs_2_ = bf16[2,128,1024]{2,1,0:T(8,128)(2,1)S(1)} collective-permute-done((bf16[2,128,1024]{2,1,0:T(8,128)(2,1)}, bf16[2,128,1024]{2,1,0:T(8,128)(2,1)S(1)}, u32[]{:S(2)}, u32[]{:S(2)}) %collective-permute-start.1) | collective-permute-done | bytes 524320 | tf_op jit(solution)/shard_map/ppermute | solution.py:233
  17.6 3.7 %collective-permute-start.3 = (bf16[2,16,1024]{2,1,0:T(8,128)(2,1)}, bf16[2,16,1024]{2,1,0:T(8,128)(2,1)S(1)}, u32[]{:S(2)}, u32[]{:S(2)}) collective-permute-start(bf16[2,16,1024]{2,1,0:T(8,128)(2,1)} %get-tuple-element.19), channel_id=1, source_target_pairs={{0,8},{4,12},{8,16},{12,20},{16,24},{20,28},{1,9},{5,13},{9,17},{1... | collective-permute-start | bytes 196616 | tf_op jit(solution)/shard_map/ppermute | solution.py:236
  21.3 4.5 %collective-permute-start.4 = (bf16[2,16,1024]{2,1,0:T(8,128)(2,1)}, bf16[2,16,1024]{2,1,0:T(8,128)(2,1)S(1)}, u32[]{:S(2)}, u32[]{:S(2)}) collective-permute-start(bf16[2,16,1024]{2,1,0:T(8,128)(2,1)} %get-tuple-element.19), channel_id=1, source_target_pairs={{0,16},{4,20},{8,24},{12,28},{1,17},{5,21},{9,25},{13,29},{2,18},{... | collective-permute-start | bytes 196616 | tf_op jit(solution)/shard_map/ppermute | solution.py:236
  25.8 1.3 %collective-permute-start.5 = (bf16[2,16,1024]{2,1,0:T(8,128)(2,1)}, bf16[2,16,1024]{2,1,0:T(8,128)(2,1)S(1)}, u32[]{:S(2)}, u32[]{:S(2)}) collective-permute-start(bf16[2,16,1024]{2,1,0:T(8,128)(2,1)} %get-tuple-element.19), channel_id=1, source_target_pairs={{0,24},{4,28},{1,25},{5,29},{2,26},{6,30},{3,27},{7,31}} | collective-permute-start | bytes 196616 | tf_op jit(solution)/shard_map/ppermute | solution.py:236
  27.1 1.0 collective-permute-done.4
  28.1 1.2 %collective-permute-done.5 = bf16[2,16,1024]{2,1,0:T(8,128)(2,1)S(1)} collective-permute-done((bf16[2,16,1024]{2,1,0:T(8,128)(2,1)}, bf16[2,16,1024]{2,1,0:T(8,128)(2,1)S(1)}, u32[]{:S(2)}, u32[]{:S(2)}) %collective-permute-start.5) | collective-permute-done | bytes 65568 | tf_op jit(solution)/shard_map/ppermute | solution.py:236
  29.3 0.9 pad_maximum_fusion.refs_0_
  30.2 1.6 %collective-permute-start.9 = (bf16[4,2,16,1024]{3,2,1,0:T(8,128)(2,1)S(1)}, bf16[4,2,16,1024]{3,2,1,0:T(8,128)(2,1)S(1)}, u32[]{:S(2)}, u32[]{:S(2)}) collective-permute-start(bf16[4,2,16,1024]{3,2,1,0:T(8,128)(2,1)S(1)} %pad_maximum_fusion.refs_0_), channel_id=1, source_target_pairs={{0,2},{1,3},{2,0},{3,1},{4,6},{5,7},{6,4},{7,5},{8,10},{9,11},{10,... | collective-permute-start | bytes 786440 | tf_op jit(solution)/shard_map/ppermute | solution.py:233
  31.8 1.4 %collective-permute-start.10 = (bf16[4,2,16,1024]{3,2,1,0:T(8,128)(2,1)S(1)}, bf16[4,2,16,1024]{3,2,1,0:T(8,128)(2,1)S(1)}, u32[]{:S(2)}, u32[]{:S(2)}) collective-permute-start(bf16[4,2,16,1024]{3,2,1,0:T(8,128)(2,1)S(1)} %pad_maximum_fusion.refs_0_), channel_id=1, source_target_pairs={{0,6},{1,7},{2,4},{3,5},{4,2},{5,3},{6,0},{7,1},{8,14},{9,15},{10,... | collective-permute-start | bytes 786440 | tf_op jit(solution)/shard_map/ppermute | solution.py:233
  33.8 9.7 %collective-permute-done.9.refs_4_ = bf16[4,2,16,1024]{3,2,1,0:T(8,128)(2,1)S(1)} collective-permute-done((bf16[4,2,16,1024]{3,2,1,0:T(8,128)(2,1)S(1)}, bf16[4,2,16,1024]{3,2,1,0:T(8,128)(2,1)S(1)}, u32[]{:S(2)}, u32[]{:S(2)}) %collective-permute-start.9) | collective-permute-done | bytes 262176 | tf_op jit(solution)/shard_map/ppermute | solution.py:233
  44.0 0.7 collective-permute-done.6.refs_1_
  45.3 1.2 %copy-done = bf16[512,1024]{1,0:T(8,128)(2,1)S(1)} copy-done((bf16[512,1024]{1,0:T(8,128)(2,1)S(1)}, bf16[512,1024]{1,0:T(8,128)(2,1)}, u32[]{:S(2)}) %copy-start) | copy-done | bytes 1048600
  46.5 1.0 %copy-done.3 = bf16[2,8,16,1024]{3,2,1,0:T(8,128)(2,1)S(1)} copy-done((bf16[2,8,16,1024]{3,2,1,0:T(8,128)(2,1)S(1)}, bf16[2,8,16,1024]{3,2,1,0:T(8,128)(2,1)}, u32[]{:S(2)}) %copy-start.3) | copy-done | bytes 524312
  47.5 6.2 %shard_map.85 = (f32[512,1024]{1,0:T(8,128)S(1)}, f32[512,1024]{1,0:T(8,128)S(1)}) custom-call(bf16[512,1024]{1,0:T(8,128)(2,1)S(1)} %copy-done, bf16[2,128,1024]{2,1,0:T(8,128)(2,1)S(1)} %bitcast.28, bf16[2,128,1024]{2,1,0:T(8,128)(2,1)S(1)} %collective-permute-done.refs_1_, bf16[2,128,1024]{2,1,0:T(8,128)(2,1)S(1)} %collective-permute-done.1.refs_2_, ...), custom_call_target="tpu_custom_call" | custom-call | flops 2147483648 | bytes 3145728 | tf_op jit(solution)/shard_map/pallas_call | solution.py:200
  53.8 14.2 %shard_map.86 = (bf16[512,1024]{1,0:T(8,128)(2,1)}, f32[512,1024]{1,0:T(8,128)S(1)}, f32[512,1024]{1,0:T(8,128)S(1)}, bf16[4,2,16,1024]{3,2,1,0:T(8,128)(2,1)S(1)}, bf16[4,2,16,1024]{3,2,1,0:T(8,128)(2,1)}) custom-call(bf16[512,1024]{1,0:T(8,128)(2,1)S(1)} %copy-done.1, bf16[512,1024]{1,0:T(8,128)(2,1)S(1)} %copy-done.2, ...), custom_call_target="tpu_custom_call" | custom-call | flops 5368709120 | bytes 8388608 | tf_op jit(solution)/shard_map/pallas_call | solution.py:200
  68.1 1.3 %copy-done.9 = f32[512,1024]{1,0:T(8,128)} copy-done((f32[512,1024]{1,0:T(8,128)}, f32[512,1024]{1,0:T(8,128)S(1)}, u32[]{:S(2)}) %copy-start.9) | copy-done | bytes 2097176
  69.4 1.4 %copy-done.11 = f32[512,1024]{1,0:T(8,128)} copy-done((f32[512,1024]{1,0:T(8,128)}, f32[512,1024]{1,0:T(8,128)S(1)}, u32[]{:S(2)}) %copy-start.11) | copy-done | bytes 2097176
  70.8 1.5 %collective-permute-start.13 = (bf16[4,2,16,1024]{3,2,1,0:T(8,128)(2,1)}, bf16[4,2,16,1024]{3,2,1,0:T(8,128)(2,1)}, u32[]{:S(2)}, u32[]{:S(2)}) collective-permute-start(bf16[4,2,16,1024]{3,2,1,0:T(8,128)(2,1)} %get-tuple-element.25), channel_id=1, source_target_pairs={{0,4},{1,5},{2,6},{3,7},{4,0},{5,1},{6,2},{7,3},{8,12},{9,13},{10,... | collective-permute-start | bytes 786440 | tf_op jit(solution)/shard_map/ppermute | solution.py:233
  73.5 6.0 %collective-permute-done.13 = bf16[4,2,16,1024]{3,2,1,0:T(8,128)(2,1)} collective-permute-done((bf16[4,2,16,1024]{3,2,1,0:T(8,128)(2,1)}, bf16[4,2,16,1024]{3,2,1,0:T(8,128)(2,1)}, u32[]{:S(2)}, u32[]{:S(2)}) %collective-permute-start.13) | collective-permute-done | bytes 262176 | tf_op jit(solution)/shard_map/ppermute | solution.py:233
  79.5 1.0 fusion.2
  80.5 1.3 %collective-permute-start.14 = (bf16[2,16,1024]{2,1,0:T(8,128)(2,1)S(1)}, bf16[2,16,1024]{2,1,0:T(8,128)(2,1)S(1)}, u32[]{:S(2)}, u32[]{:S(2)}) collective-permute-start(bf16[2,16,1024]{2,1,0:T(8,128)(2,1)S(1)} %get-tuple-element.28), channel_id=1, source_target_pairs={{8,0},{12,4},{16,8},{20,12},{24,16},{28,20},{9,1},{13,5},{17,9},{2... | collective-permute-start | bytes 196616 | tf_op jit(solution)/shard_map/ppermute | solution.py:241
  81.8 1.3 %collective-permute-start.15 = (bf16[2,16,1024]{2,1,0:T(8,128)(2,1)S(1)}, bf16[2,16,1024]{2,1,0:T(8,128)(2,1)S(1)}, u32[]{:S(2)}, u32[]{:S(2)}) collective-permute-start(bf16[2,16,1024]{2,1,0:T(8,128)(2,1)S(1)} %get-tuple-element.30), channel_id=1, source_target_pairs={{16,0},{20,4},{24,8},{28,12},{17,1},{21,5},{25,9},{29,13},{18,2},{... | collective-permute-start | bytes 196616 | tf_op jit(solution)/shard_map/ppermute | solution.py:241
  83.0 1.3 %collective-permute-start.16 = (bf16[2,16,1024]{2,1,0:T(8,128)(2,1)S(1)}, bf16[2,16,1024]{2,1,0:T(8,128)(2,1)S(1)}, u32[]{:S(2)}, u32[]{:S(2)}) collective-permute-start(bf16[2,16,1024]{2,1,0:T(8,128)(2,1)S(1)} %get-tuple-element.29), channel_id=1, source_target_pairs={{24,0},{28,4},{25,1},{29,5},{26,2},{30,6},{27,3},{31,7}} | collective-permute-start | bytes 196616 | tf_op jit(solution)/shard_map/ppermute | solution.py:241
  84.4 1.0 %copy-done.6 = bf16[2,128,1024]{2,1,0:T(8,128)(2,1)S(1)} copy-done((bf16[2,128,1024]{2,1,0:T(8,128)(2,1)S(1)}, bf16[2,128,1024]{2,1,0:T(8,128)(2,1)}, u32[]{:S(2)}) %copy-start.6) | copy-done | bytes 524312
  85.4 1.0 %copy-done.8 = bf16[2,128,1024]{2,1,0:T(8,128)(2,1)S(1)} copy-done((bf16[2,128,1024]{2,1,0:T(8,128)(2,1)S(1)}, bf16[2,128,1024]{2,1,0:T(8,128)(2,1)}, u32[]{:S(2)}) %copy-start.8) | copy-done | bytes 524312
  86.4 1.6 %copy-done.10 = f32[512,1024]{1,0:T(8,128)S(1)} copy-done((f32[512,1024]{1,0:T(8,128)S(1)}, f32[512,1024]{1,0:T(8,128)}, u32[]{:S(2)}) %copy-start.10) | copy-done | bytes 2097176
  88.0 1.6 %copy-done.12 = f32[512,1024]{1,0:T(8,128)S(1)} copy-done((f32[512,1024]{1,0:T(8,128)S(1)}, f32[512,1024]{1,0:T(8,128)}, u32[]{:S(2)}) %copy-start.12) | copy-done | bytes 2097176
  89.6 7.7 %shard_map.87 = (bf16[512,1024]{1,0:T(8,128)(2,1)}, f32[128,1024]{1,0:T(8,128)S(1)}, f32[128,1024]{1,0:T(8,128)S(1)}) custom-call(bf16[512,1024]{1,0:T(8,128)(2,1)S(1)} %copy-done.1, bf16[512,1024]{1,0:T(8,128)(2,1)S(1)} %copy-done.2, f32[512,1024]{1,0:T(8,128)S(1)} %copy-done.12, f32[512,1024]{1,0:T(8,128)S(1)} %copy-done.10, ...), custom_call_target="tpu_custom_call" | custom-call | flops 4294967296 | bytes 8388608 | tf_op jit(solution)/shard_map/pallas_call | solution.py:200
  97.3 0.9 fusion.1
  98.2 1.0 add_convert_fusion
  (42 shorter events, 2.2 us)
Async XLA Ops:
  2.5 15.1 %collective-permute-start.1 = (bf16[2,128,1024]{2,1,0:T(8,128)(2,1)}, bf16[2,128,1024]{2,1,0:T(8,128)(2,1)S(1)}, u32[]{:S(2)}, u32[]{:S(2)}) collective-permute-start(bf16[2,128,1024]{2,1,0:T(8,128)(2,1)} %bitcast.26), channel_id=1, source_target_pairs={{0,2},{1,3},{2,0},{3,1},{4,6},{5,7},{6,4},{7,5},{8,10},{9,11},{10,... | collective-permute-start | bytes 1572872 | tf_op jit(solution)/shard_map/ppermute | solution.py:233
  5.5 39.2 %collective-permute-start = (bf16[2,128,1024]{2,1,0:T(8,128)(2,1)}, bf16[2,128,1024]{2,1,0:T(8,128)(2,1)S(1)}, u32[]{:S(2)}, u32[]{:S(2)}) collective-permute-start(bf16[2,128,1024]{2,1,0:T(8,128)(2,1)} %bitcast.27), channel_id=1, source_target_pairs={{0,1},{1,0},{2,3},{3,2},{4,5},{5,4},{6,7},{7,6},{8,9},{9,8},{10,11... | collective-permute-start | bytes 1572872 | tf_op jit(solution)/shard_map/ppermute | solution.py:233
  17.6 27.6 %collective-permute-start.2 = (bf16[2,128,1024]{2,1,0:T(8,128)(2,1)S(1)}, bf16[2,128,1024]{2,1,0:T(8,128)(2,1)S(1)}, u32[]{:S(2)}, u32[]{:S(2)}) collective-permute-start(bf16[2,128,1024]{2,1,0:T(8,128)(2,1)S(1)} %collective-permute-done.1.refs_2_), channel_id=1, source_target_pairs={{0,1},{1,0},{2,3},{3,2},{4,5},{5,4},{6,7},{7,6},{8,9},{9,8},{10,11... | collective-permute-start | bytes 1572872 | tf_op jit(solution)/shard_map/ppermute | solution.py:233
  17.6 9.5 %collective-permute-start.3 = (bf16[2,16,1024]{2,1,0:T(8,128)(2,1)}, bf16[2,16,1024]{2,1,0:T(8,128)(2,1)S(1)}, u32[]{:S(2)}, u32[]{:S(2)}) collective-permute-start(bf16[2,16,1024]{2,1,0:T(8,128)(2,1)} %get-tuple-element.19), channel_id=1, source_target_pairs={{0,8},{4,12},{8,16},{12,20},{16,24},{20,28},{1,9},{5,13},{9,17},{1... | collective-permute-start | bytes 196616 | tf_op jit(solution)/shard_map/ppermute | solution.py:236
  21.3 6.8 %collective-permute-start.4 = (bf16[2,16,1024]{2,1,0:T(8,128)(2,1)}, bf16[2,16,1024]{2,1,0:T(8,128)(2,1)S(1)}, u32[]{:S(2)}, u32[]{:S(2)}) collective-permute-start(bf16[2,16,1024]{2,1,0:T(8,128)(2,1)} %get-tuple-element.19), channel_id=1, source_target_pairs={{0,16},{4,20},{8,24},{12,28},{1,17},{5,21},{9,25},{13,29},{2,18},{... | collective-permute-start | bytes 196616 | tf_op jit(solution)/shard_map/ppermute | solution.py:236
  25.8 3.5 %collective-permute-start.5 = (bf16[2,16,1024]{2,1,0:T(8,128)(2,1)}, bf16[2,16,1024]{2,1,0:T(8,128)(2,1)S(1)}, u32[]{:S(2)}, u32[]{:S(2)}) collective-permute-start(bf16[2,16,1024]{2,1,0:T(8,128)(2,1)} %get-tuple-element.19), channel_id=1, source_target_pairs={{0,24},{4,28},{1,25},{5,29},{2,26},{6,30},{3,27},{7,31}} | collective-permute-start | bytes 196616 | tf_op jit(solution)/shard_map/ppermute | solution.py:236
  30.2 13.3 %collective-permute-start.9 = (bf16[4,2,16,1024]{3,2,1,0:T(8,128)(2,1)S(1)}, bf16[4,2,16,1024]{3,2,1,0:T(8,128)(2,1)S(1)}, u32[]{:S(2)}, u32[]{:S(2)}) collective-permute-start(bf16[4,2,16,1024]{3,2,1,0:T(8,128)(2,1)S(1)} %pad_maximum_fusion.refs_0_), channel_id=1, source_target_pairs={{0,2},{1,3},{2,0},{3,1},{4,6},{5,7},{6,4},{7,5},{8,10},{9,11},{10,... | collective-permute-start | bytes 786440 | tf_op jit(solution)/shard_map/ppermute | solution.py:233
  31.8 11.7 %collective-permute-start.10 = (bf16[4,2,16,1024]{3,2,1,0:T(8,128)(2,1)S(1)}, bf16[4,2,16,1024]{3,2,1,0:T(8,128)(2,1)S(1)}, u32[]{:S(2)}, u32[]{:S(2)}) collective-permute-start(bf16[4,2,16,1024]{3,2,1,0:T(8,128)(2,1)S(1)} %pad_maximum_fusion.refs_0_), channel_id=1, source_target_pairs={{0,6},{1,7},{2,4},{3,5},{4,2},{5,3},{6,0},{7,1},{8,14},{9,15},{10,... | collective-permute-start | bytes 786440 | tf_op jit(solution)/shard_map/ppermute | solution.py:233
  33.2 11.5 %collective-permute-start.6 = (bf16[4,2,16,1024]{3,2,1,0:T(8,128)(2,1)S(1)}, bf16[4,2,16,1024]{3,2,1,0:T(8,128)(2,1)S(1)}, u32[]{:S(2)}, u32[]{:S(2)}) collective-permute-start(bf16[4,2,16,1024]{3,2,1,0:T(8,128)(2,1)S(1)} %pad_maximum_fusion.refs_0_), channel_id=1, source_target_pairs={{0,4},{1,5},{2,6},{3,7},{4,0},{5,1},{6,2},{7,3},{8,12},{9,13},{10,... | collective-permute-start | bytes 786440 | tf_op jit(solution)/shard_map/ppermute | solution.py:233
  43.5 10.2 %collective-permute-start.7 = (bf16[4,2,16,1024]{3,2,1,0:T(8,128)(2,1)S(1)}, bf16[4,2,16,1024]{3,2,1,0:T(8,128)(2,1)S(1)}, u32[]{:S(2)}, u32[]{:S(2)}) collective-permute-start(bf16[4,2,16,1024]{3,2,1,0:T(8,128)(2,1)S(1)} %pad_maximum_fusion.refs_0_), channel_id=1, source_target_pairs={{0,1},{1,0},{2,3},{3,2},{4,5},{5,4},{6,7},{7,6},{8,9},{9,8},{10,11... | collective-permute-start | bytes 786440 | tf_op jit(solution)/shard_map/ppermute | solution.py:233
  43.5 10.3 %collective-permute-start.11 = (bf16[4,2,16,1024]{3,2,1,0:T(8,128)(2,1)S(1)}, bf16[4,2,16,1024]{3,2,1,0:T(8,128)(2,1)S(1)}, u32[]{:S(2)}, u32[]{:S(2)}) collective-permute-start(bf16[4,2,16,1024]{3,2,1,0:T(8,128)(2,1)S(1)} %collective-permute-done.9.refs_4_), channel_id=1, source_target_pairs={{0,1},{1,0},{2,3},{3,2},{4,5},{5,4},{6,7},{7,6},{8,9},{9,8},{10,11... | collective-permute-start | bytes 786440 | tf_op jit(solution)/shard_map/ppermute | solution.py:233
  44.7 9.0 %collective-permute-start.12 = (bf16[4,2,16,1024]{3,2,1,0:T(8,128)(2,1)S(1)}, bf16[4,2,16,1024]{3,2,1,0:T(8,128)(2,1)S(1)}, u32[]{:S(2)}, u32[]{:S(2)}) collective-permute-start(bf16[4,2,16,1024]{3,2,1,0:T(8,128)(2,1)S(1)} %collective-permute-done.10.refs_5_), channel_id=1, source_target_pairs={{0,1},{1,0},{2,3},{3,2},{4,5},{5,4},{6,7},{7,6},{8,9},{9,8},{10,11... | collective-permute-start | bytes 786440 | tf_op jit(solution)/shard_map/ppermute | solution.py:233
  44.7 9.0 %copy-start.5 = (bf16[2,128,1024]{2,1,0:T(8,128)(2,1)}, bf16[2,128,1024]{2,1,0:T(8,128)(2,1)S(1)}, u32[]{:S(2)}) copy-start(bf16[2,128,1024]{2,1,0:T(8,128)(2,1)S(1)} %collective-permute-done.refs_1_) | copy-start | bytes 1572868
  44.7 9.0 %collective-permute-start.8 = (bf16[4,2,16,1024]{3,2,1,0:T(8,128)(2,1)S(1)}, bf16[4,2,16,1024]{3,2,1,0:T(8,128)(2,1)S(1)}, u32[]{:S(2)}, u32[]{:S(2)}) collective-permute-start(bf16[4,2,16,1024]{3,2,1,0:T(8,128)(2,1)S(1)} %collective-permute-done.6.refs_1_), channel_id=1, source_target_pairs={{0,1},{1,0},{2,3},{3,2},{4,5},{5,4},{6,7},{7,6},{8,9},{9,8},{10,11... | collective-permute-start | bytes 786440 | tf_op jit(solution)/shard_map/ppermute | solution.py:233
  45.3 1.2 %copy-start = (bf16[512,1024]{1,0:T(8,128)(2,1)S(1)}, bf16[512,1024]{1,0:T(8,128)(2,1)}, u32[]{:S(2)}) copy-start(bf16[512,1024]{1,0:T(8,128)(2,1)} %q_ref.5) | copy-start | bytes 3145732
  46.5 1.0 %copy-start.3 = (bf16[2,8,16,1024]{3,2,1,0:T(8,128)(2,1)S(1)}, bf16[2,8,16,1024]{3,2,1,0:T(8,128)(2,1)}, u32[]{:S(2)}) copy-start(bf16[2,8,16,1024]{3,2,1,0:T(8,128)(2,1)} %get-tuple-element.16) | copy-start | bytes 1572868
  47.5 6.2 %copy-start.7 = (bf16[2,128,1024]{2,1,0:T(8,128)(2,1)}, bf16[2,128,1024]{2,1,0:T(8,128)(2,1)S(1)}, u32[]{:S(2)}) copy-start(bf16[2,128,1024]{2,1,0:T(8,128)(2,1)S(1)} %collective-permute-done.2.refs_3_) | copy-start | bytes 1572868
  47.5 6.3 %copy-start.1 = (bf16[512,1024]{1,0:T(8,128)(2,1)S(1)}, bf16[512,1024]{1,0:T(8,128)(2,1)}, u32[]{:S(2)}) copy-start(bf16[512,1024]{1,0:T(8,128)(2,1)} %q_ref.5) | copy-start | bytes 3145732
  47.5 6.3 %copy-start.2 = (bf16[512,1024]{1,0:T(8,128)(2,1)S(1)}, bf16[512,1024]{1,0:T(8,128)(2,1)}, u32[]{:S(2)}) copy-start(bf16[512,1024]{1,0:T(8,128)(2,1)} %g_ref.3) | copy-start | bytes 3145732
  53.8 18.4 %copy-start.13 = (s32[64,15]{0,1:T(8,128)S(1)}, s32[64,15]{0,1:T(8,128)}, u32[]{:S(2)}) copy-start(s32[64,15]{0,1:T(8,128)} %param.8) | copy-start | bytes 11524
  53.8 30.5 %copy-start.4 = (bf16[2,8,16,1024]{3,2,1,0:T(8,128)(2,1)S(1)}, bf16[2,8,16,1024]{3,2,1,0:T(8,128)(2,1)}, u32[]{:S(2)}) copy-start(bf16[2,8,16,1024]{3,2,1,0:T(8,128)(2,1)} %get-tuple-element.16) | copy-start | bytes 1572868
  68.1 1.3 %copy-start.9 = (f32[512,1024]{1,0:T(8,128)}, f32[512,1024]{1,0:T(8,128)S(1)}, u32[]{:S(2)}) copy-start(f32[512,1024]{1,0:T(8,128)S(1)} %get-tuple-element.22.far_gq_ref) | copy-start | bytes 6291460
  69.4 1.4 %copy-start.11 = (f32[512,1024]{1,0:T(8,128)}, f32[512,1024]{1,0:T(8,128)S(1)}, u32[]{:S(2)}) copy-start(f32[512,1024]{1,0:T(8,128)S(1)} %get-tuple-element.21.stat_ref) | copy-start | bytes 6291460
  70.8 8.7 %collective-permute-start.13 = (bf16[4,2,16,1024]{3,2,1,0:T(8,128)(2,1)}, bf16[4,2,16,1024]{3,2,1,0:T(8,128)(2,1)}, u32[]{:S(2)}, u32[]{:S(2)}) collective-permute-start(bf16[4,2,16,1024]{3,2,1,0:T(8,128)(2,1)} %get-tuple-element.25), channel_id=1, source_target_pairs={{0,4},{1,5},{2,6},{3,7},{4,0},{5,1},{6,2},{7,3},{8,12},{9,13},{10,... | collective-permute-start | bytes 786440 | tf_op jit(solution)/shard_map/ppermute | solution.py:233
  80.5 16.9 %collective-permute-start.14 = (bf16[2,16,1024]{2,1,0:T(8,128)(2,1)S(1)}, bf16[2,16,1024]{2,1,0:T(8,128)(2,1)S(1)}, u32[]{:S(2)}, u32[]{:S(2)}) collective-permute-start(bf16[2,16,1024]{2,1,0:T(8,128)(2,1)S(1)} %get-tuple-element.28), channel_id=1, source_target_pairs={{8,0},{12,4},{16,8},{20,12},{24,16},{28,20},{9,1},{13,5},{17,9},{2... | collective-permute-start | bytes 196616 | tf_op jit(solution)/shard_map/ppermute | solution.py:241
  81.8 15.6 %collective-permute-start.15 = (bf16[2,16,1024]{2,1,0:T(8,128)(2,1)S(1)}, bf16[2,16,1024]{2,1,0:T(8,128)(2,1)S(1)}, u32[]{:S(2)}, u32[]{:S(2)}) collective-permute-start(bf16[2,16,1024]{2,1,0:T(8,128)(2,1)S(1)} %get-tuple-element.30), channel_id=1, source_target_pairs={{16,0},{20,4},{24,8},{28,12},{17,1},{21,5},{25,9},{29,13},{18,2},{... | collective-permute-start | bytes 196616 | tf_op jit(solution)/shard_map/ppermute | solution.py:241
  83.0 14.3 %collective-permute-start.16 = (bf16[2,16,1024]{2,1,0:T(8,128)(2,1)S(1)}, bf16[2,16,1024]{2,1,0:T(8,128)(2,1)S(1)}, u32[]{:S(2)}, u32[]{:S(2)}) collective-permute-start(bf16[2,16,1024]{2,1,0:T(8,128)(2,1)S(1)} %get-tuple-element.29), channel_id=1, source_target_pairs={{24,0},{28,4},{25,1},{29,5},{26,2},{30,6},{27,3},{31,7}} | collective-permute-start | bytes 196616 | tf_op jit(solution)/shard_map/ppermute | solution.py:241
  84.4 1.0 %copy-start.6 = (bf16[2,128,1024]{2,1,0:T(8,128)(2,1)S(1)}, bf16[2,128,1024]{2,1,0:T(8,128)(2,1)}, u32[]{:S(2)}) copy-start(bf16[2,128,1024]{2,1,0:T(8,128)(2,1)} %copy-done.5) | copy-start | bytes 1572868
  85.4 1.0 %copy-start.8 = (bf16[2,128,1024]{2,1,0:T(8,128)(2,1)S(1)}, bf16[2,128,1024]{2,1,0:T(8,128)(2,1)}, u32[]{:S(2)}) copy-start(bf16[2,128,1024]{2,1,0:T(8,128)(2,1)} %copy-done.7) | copy-start | bytes 1572868
  86.4 1.6 %copy-start.10 = (f32[512,1024]{1,0:T(8,128)S(1)}, f32[512,1024]{1,0:T(8,128)}, u32[]{:S(2)}) copy-start(f32[512,1024]{1,0:T(8,128)} %copy-done.9) | copy-start | bytes 6291460
  88.0 1.6 %copy-start.12 = (f32[512,1024]{1,0:T(8,128)S(1)}, f32[512,1024]{1,0:T(8,128)}, u32[]{:S(2)}) copy-start(f32[512,1024]{1,0:T(8,128)} %copy-done.11) | copy-start | bytes 6291460
where the time goes:
time: 100 us; the launch traced here: 99.2 us
  waiting for transfers between devices  30.8 us (31%)
  Pallas kernels  30 us (30%)
  starting transfers between devices  22.4 us (22%)
  local copies, waits for them, and re-layouts  10.8 us (11%)
  other arithmetic  3.68 us (4%)
  between operations  1.5 us (2%)
    ppermute x11, waiting for transfers between devices, hop(): return lax.ppermute(part, ('seq', 'kv'), pairs)  28.6 us
    pallas_call x3, Pallas kernels, call(): pl.pallas_call(kernel, in_specs=[WHOLE] * len(operands), out_specs=[WHOLE...  28.1 us
    unnamed x28, local copies, waits for them, and re-layouts  10.2 us
    ppermute x3, starting transfers between devices, climb(): lax.ppermute(part, 'seq', [(s, s + COLUMNS * d) for s in range(seq_count...  9.49 us
    ppermute x11, starting transfers between devices, hop(): return lax.ppermute(part, ('seq', 'kv'), pairs)  9.02 us
    ppermute x3, starting transfers between devices, sink(): lax.ppermute(part, 'seq', [(s, s - COLUMNS * d) for s in range(COLUMNS *...  3.88 us
    ppermute x3, waiting for transfers between devices, climb(): lax.ppermute(part, 'seq', [(s, s + COLUMNS * d) for s in range(seq_count...  2.19 us
  transfers between devices with their start and end apart: 17, of which 6 were waited for; matrix products, arithmetic and copies ran while one was open for 1% of the time, Pallas kernels for 14%

commit v1 on v0

--- a/solution.py
+++ b/solution.py
@@ -10,12 +10,13 @@
 
 HEADS = 8
 COLUMNS = 2
+GROUP = 2
 HIDDEN = -1e30
 NT = (((1,), (1,)), ((), ()))
 NN = (((1,), (0,)), ((), ()))
 TN = (((0,), (0,)), ((), ()))
 WHOLE = pl.BlockSpec(memory_space=pltpu.VMEM)
-LIMIT = pltpu.CompilerParams(vmem_limit_bytes=28 * 1024 * 1024)
+LIMIT = pltpu.CompilerParams(vmem_limit_bytes=20 * 1024 * 1024)
 
 
 def dot(a, b, dims):
@@ -75,6 +76,10 @@
     return pl.ds(pl.multiple_of(head * head_dim, head_dim), head_dim)
 
 
+def near_rows(parts, which, used, cols):
+    return jnp.concatenate([ref[which, :used, cols] for ref in parts], axis=0)
+
+
 def near_forward_kernel(members, blk_len, part_tok, q_ref, *refs):
     parts = refs[:members]
     out_ref, stat_ref, bias_ref = refs[members:]
@@ -83,23 +88,39 @@
     near = parts[0].shape[1]
     fill_near_bias(bias_ref, members, near, blk_len, part_tok)
 
-    @pl.loop(0, HEADS)
-    def _(head):
-        cols = head_columns(head, feat_width)
-        for start, count, used in near_tiles(rows, near):
-            here = pl.ds(start, count)
-            keys = jnp.concatenate([ref[0, :used, cols] for ref in parts], axis=0)
-            values = jnp.concatenate([ref[1, :used, cols] for ref in parts], axis=0)
-            raw = dot(q_ref[here, cols], keys, NT) * base2_scale(head_dim)
-            raw += bias_ref[here, : members * used]
-            peak = jnp.max(raw, axis=1, keepdims=True)
-            weight = jnp.exp2(raw - peak)
-            total = jnp.sum(weight, axis=1, keepdims=True)
-            stat_ref[here, cols] = jnp.broadcast_to(peak + jnp.log2(total), (count, head_dim))
-            out_ref[here, cols] = dot(weight.astype(jnp.bfloat16), values, NN) * (1.0 / total)
-
-
-def far_kernel(members, tile, q_ref, g_ref, sum_ref, stat_ref, *refs):
+    @pl.loop(0, HEADS // GROUP)
+    def _(group):
+        units = [
+            (head_columns(group * GROUP + i, feat_width), pl.ds(start, count), used)
+            for i in range(GROUP)
+            for start, count, used in near_tiles(rows, near)
+        ]
+        raws = [
+            dot(q_ref[here, cols], near_rows(parts, 0, used, cols), NT) * base2_scale(head_dim)
+            + bias_ref[here, : members * used]
+            for cols, here, used in units
+        ]
+        peaks = [jnp.max(raw, axis=1, keepdims=True) for raw in raws]
+        weights = [jnp.exp2(raw - peak) for raw, peak in zip(raws, peaks)]
+        totals = [jnp.sum(weight, axis=1, keepdims=True) for weight in weights]
+        sums = [
+            dot(weight.astype(jnp.bfloat16), near_rows(parts, 1, used, cols), NN)
+            for weight, (cols, here, used) in zip(weights, units)
+        ]
+        for (cols, here, used), peak, total, summed in zip(units, peaks, totals, sums):
+            level = peak + jnp.log2(total)
+            stat_ref[here, cols] = jnp.broadcast_to(level, summed.shape)
+            out_ref[here, cols] = summed * (1.0 / total)
+
+
+def far_rows(parts, which, cols):
+    steps, _, part_tok, _ = parts[0].shape
+    return jnp.concatenate(
+        [ref[:, which, :, cols].reshape(steps * part_tok, cols.size) for ref in parts], axis=0
+    )
+
+
+def far_kernel(members, tile, heads, batch, q_ref, g_ref, sum_ref, stat_ref, *refs):
     parts = refs[: COLUMNS * members]
     att_ref, gq_ref, stat_out_ref = refs[COLUMNS * members : COLUMNS * members + 3]
     grad_refs = refs[COLUMNS * members + 3 :]
@@ -116,45 +137,75 @@
     bias = jnp.concatenate([jnp.where(ok, 0.0, HIDDEN) for ok in valid] * members, axis=1)
     lane = lax.broadcasted_iota(jnp.int32, (tile, head_dim), 1)
 
-    @pl.loop(0, HEADS)
-    def _(head):
-        cols = head_columns(head, feat_width)
-        keys = jnp.concatenate([ref[:, 0, :, cols].reshape(span, head_dim) for ref in parts], axis=0)
-        values = jnp.concatenate([ref[:, 1, :, cols].reshape(span, head_dim) for ref in parts], axis=0)
-        key_grad = jnp.zeros((width, head_dim), jnp.float32)
-        value_grad = jnp.zeros((width, head_dim), jnp.float32)
-        for start in range(0, rows, tile):
-            here = pl.ds(start, tile)
-            query = q_ref[here, cols]
-            grad = g_ref[here, cols]
-            raw = dot(query, keys, NT) * base2_scale(head_dim) + bias
-            near_level = stat_ref[here, cols][:, 0:1]
-            peak = jnp.maximum(near_level, jnp.max(raw, axis=1, keepdims=True))
-            near_weight = jnp.exp2(near_level - peak)
-            weight = jnp.exp2(raw - peak)
-            total = near_weight + jnp.sum(weight, axis=1, keepdims=True)
-            inverse = 1.0 / total
-            summed = sum_ref[here, cols] * near_weight
-            summed += dot(weight.astype(jnp.bfloat16), values, NN)
-            attended = (summed * inverse).astype(jnp.bfloat16)
+    def work(units, keys, values, key_grads, value_grads):
+        raws = [
+            dot(q_ref[here, cols], keys[i], NT) * base2_scale(head_dim) + bias
+            for i, cols, here in units
+        ]
+        grad_probs = [dot(g_ref[here, cols], values[i], NT) for i, cols, here in units]
+        near_levels = [stat_ref[here, cols][:, 0:1] for i, cols, here in units]
+        peaks = [
+            jnp.maximum(near_level, jnp.max(raw, axis=1, keepdims=True))
+            for near_level, raw in zip(near_levels, raws)
+        ]
+        near_weights = [jnp.exp2(near_level - peak) for near_level, peak in zip(near_levels, peaks)]
+        weights = [jnp.exp2(raw - peak) for raw, peak in zip(raws, peaks)]
+        totals = [
+            near_weight + jnp.sum(weight, axis=1, keepdims=True)
+            for near_weight, weight in zip(near_weights, weights)
+        ]
+        inverses = [1.0 / total for total in totals]
+        sums = [
+            dot(weight.astype(jnp.bfloat16), values[i], NN)
+            for weight, (i, cols, here) in zip(weights, units)
+        ]
+        drifts = []
+        for u, (i, cols, here) in enumerate(units):
+            summed = sum_ref[here, cols] * near_weights[u] + sums[u]
+            attended = (summed * inverses[u]).astype(jnp.bfloat16)
             att_ref[here, cols] = attended
-            drift = jnp.sum(
-                grad.astype(jnp.float32) * attended.astype(jnp.float32), axis=1, keepdims=True
+            product = g_ref[here, cols].astype(jnp.float32) * attended.astype(jnp.float32)
+            drifts.append(jnp.sum(product, axis=1, keepdims=True))
+            stat_out_ref[here, cols] = jnp.where(
+                lane < head_dim // 2, peaks[u] + jnp.log2(totals[u]), drifts[u]
             )
-            stat_out_ref[here, cols] = jnp.where(
-                lane < head_dim // 2, peak + jnp.log2(total), drift
+        moved = [
+            weight * (grad_prob - drift)
+            for weight, grad_prob, drift in zip(weights, grad_probs, drifts)
+        ]
+        own_scores = [
+            (part[:, :width] * (inverse * score_scale)).astype(jnp.bfloat16)
+            for part, inverse in zip(moved, inverses)
+        ]
+        own_probs = [
+            (weight[:, :width] * inverse).astype(jnp.bfloat16)
+            for weight, inverse in zip(weights, inverses)
+        ]
+        for u, (i, cols, here) in enumerate(units):
+            gq_ref[here, cols] = dot(moved[u].astype(jnp.bfloat16), keys[i], NN) * (
+                inverses[u] * score_scale
             )
-            moved = weight * (dot(grad, values, NT) - drift)
-            gq_ref[here, cols] = dot(moved.astype(jnp.bfloat16), keys, NN) * (inverse * score_scale)
-            own_score = (moved[:, :width] * (inverse * score_scale)).astype(jnp.bfloat16)
-            own_prob = (weight[:, :width] * inverse).astype(jnp.bfloat16)
-            key_grad += dot(own_score, query, TN)
-            value_grad += dot(own_prob, grad, TN)
-        for c, ref in enumerate(grad_refs):
-            shape = (steps, part_tok, head_dim)
-            used = slice(c * span, (c + 1) * span)
-            ref[:, 0, :, cols] = key_grad[used].astype(jnp.bfloat16).reshape(shape)
-            ref[:, 1, :, cols] = value_grad[used].astype(jnp.bfloat16).reshape(shape)
+        for u, (i, cols, here) in enumerate(units):
+            key_grads[i].append(dot(own_scores[u], q_ref[here, cols], TN))
+            value_grads[i].append(dot(own_probs[u], g_ref[here, cols], TN))
+
+    @pl.loop(0, HEADS // heads)
+    def _(group):
+        columns = [head_columns(group * heads + i, feat_width) for i in range(heads)]
+        units = [
+            (i, cols, pl.ds(r, tile)) for i, cols in enumerate(columns) for r in range(0, rows, tile)
+        ]
+        keys = [far_rows(parts, 0, cols) for cols in columns]
+        values = [far_rows(parts, 1, cols) for cols in columns]
+        grads = [[[] for _ in columns] for _ in range(2)]
+        for first in range(0, len(units), batch):
+            work(units[first : first + batch], keys, values, *grads)
+        for which, per_head in enumerate(grads):
+            for cols, terms in zip(columns, per_head):
+                total = functools.reduce(lambda a, b: a + b, terms).astype(jnp.bfloat16)
+                for c, ref in enumerate(grad_refs):
+                    piece = total[c * span : (c + 1) * span]
+                    ref[:, which, :, cols] = piece.reshape(steps, part_tok, head_dim)
 
 
 def near_backward_kernel(members, blk_len, part_tok, q_ref, g_ref, stat_ref, far_gq_ref, *refs):
@@ -166,33 +217,42 @@
     score_scale = 1.0 / math.sqrt(head_dim)
     fill_near_bias(bias_ref, members, near, blk_len, part_tok)
 
-    @pl.loop(0, HEADS)
-    def _(head):
-        cols = head_columns(head, feat_width)
-        for start, count, used in reversed(near_tiles(rows, near)):
-            here = pl.ds(start, count)
-            query = q_ref[here, cols]
-            grad = g_ref[here, cols]
-            keys = jnp.concatenate([ref[0, :used, cols] for ref in parts], axis=0)
-            values = jnp.concatenate([ref[1, :used, cols] for ref in parts], axis=0)
-            stat = stat_ref[here, cols]
-            level = stat[:, 0:1]
-            drift = stat[:, head_dim // 2 : head_dim // 2 + 1]
-            raw = dot(query, keys, NT) * base2_scale(head_dim)
-            raw += bias_ref[here, : members * used]
-            prob = jnp.exp2(raw - level)
-            moved = prob * (dot(grad, values, NT) - drift)
+    @pl.loop(0, HEADS // GROUP)
+    def _(group):
+        units = [
+            (head_columns(group * GROUP + i, feat_width), pl.ds(start, count), used)
+            for i in range(GROUP)
+            for start, count, used in reversed(near_tiles(rows, near))
+        ]
+        keys = [near_rows(parts, 0, used, cols) for cols, here, used in units]
+        values = [near_rows(parts, 1, used, cols) for cols, here, used in units]
+        raws = [
+            dot(q_ref[here, cols], key, NT) * base2_scale(head_dim)
+            + bias_ref[here, : members * used]
+            for (cols, here, used), key in zip(units, keys)
+        ]
+        grad_probs = [
+            dot(g_ref[here, cols], value, NT) for (cols, here, used), value in zip(units, values)
+        ]
+        stats = [stat_ref[here, cols] for cols, here, used in units]
+        probs = [jnp.exp2(raw - stat[:, 0:1]) for raw, stat in zip(raws, stats)]
+        moved = [
+            prob * (grad_prob - stat[:, head_dim // 2 : head_dim // 2 + 1])
+            for prob, grad_prob, stat in zip(probs, grad_probs, stats)
+        ]
+        for (cols, here, used), part, key in zip(units, moved, keys):
             gq_ref[here, cols] = (
-                dot(moved.astype(jnp.bfloat16), keys, NN) * score_scale + far_gq_ref[here, cols]
+                dot(part.astype(jnp.bfloat16), key, NN) * score_scale + far_gq_ref[here, cols]
             ).astype(jnp.bfloat16)
-            key_grad = dot((moved[:, :used] * score_scale).astype(jnp.bfloat16), query, TN)
-            value_grad = dot(prob[:, :used].astype(jnp.bfloat16), grad, TN)
-            if used == near:
-                gk_ref[:, cols] = key_grad
-                gv_ref[:, cols] = value_grad
-            else:
-                gk_ref[:used, cols] += key_grad
-                gv_ref[:used, cols] += value_grad
+        for (cols, here, used), part, prob in zip(units, moved, probs):
+            own_score = (part[:, :used] * score_scale).astype(jnp.bfloat16)
+            own_prob = prob[:, :used].astype(jnp.bfloat16)
+            for left, right_ref, ref in ((own_score, q_ref, gk_ref), (own_prob, g_ref, gv_ref)):
+                grad = dot(left, right_ref[here, cols], TN)
+                if used == near:
+                    ref[:, cols] = grad
+                else:
+                    ref[:used, cols] += grad
 
 
 def call(kernel, operands, outs, scratch, pairs, products, head_dim):
@@ -244,15 +304,15 @@
 
     own_pair, both = pick_pair(layout.T, keys, values)
     both = both.reshape(2, near, feat_width)
-    near_parts = [both] + [hop(both, 0, step) for step in range(2, members, 2)]
-    near_parts = [p for part in near_parts for p in (part, hop(part, 0, 1))]
     column = jnp.stack([own_pair] + [climb(own_pair, d) for d in range(1, levels)])
-    far_parts = []
-    for step in range(0, members, 2):
-        group = [
-            column if (c, step) == (0, 0) else hop(column, c, step) for c in range(COLUMNS)
-        ]
-        far_parts += group + [hop(part, 0, 1) for part in group]
+    crossing = [
+        [column if (c, step) == (0, 0) else hop(column, c, step) for c in range(COLUMNS)]
+        for step in range(0, members, 2)
+    ]
+    near_parts = [both, hop(both, 0, 1)]
+    for step in range(2, members, 2):
+        landed, _ = lax.optimization_barrier((hop(both, 0, step), column))
+        near_parts += [landed, hop(landed, 0, 1)]
 
     def rows_out(dtype):
         return jax.ShapeDtypeStruct((tok_rows, feat_width), dtype)
@@ -261,8 +321,10 @@
     far_out = jax.ShapeDtypeStruct(column.shape, jnp.bfloat16)
     bias_scratch = [pltpu.VMEM((tok_rows, members * near), jnp.float32)]
     near_pairs = HEADS * tok_rows * members * near
-    far_pairs = HEADS * tok_rows * members * seq_count * part_tok
-    tile = min(256, max(64, 2**18 // (members * seq_count * part_tok)))
+    far_width = members * seq_count * part_tok
+    far_pairs = HEADS * tok_rows * far_width
+    roomy = far_width <= 512
+    far_plan = (tok_rows // 2, GROUP, 2 * GROUP) if roomy else (tok_rows // 8, 1, 1)
 
     near_sum, near_stat = call(
         functools.partial(near_forward_kernel, members, blk_len, part_tok),
@@ -273,8 +335,12 @@
         2,
         head_dim,
     )
+    far_parts = []
+    for group in crossing:
+        group, _ = lax.optimization_barrier((group, near_stat))
+        far_parts += group + [hop(part, 0, 1) for part in group]
     attended, far_gq, stat, own_grad, cross_grad = call(
-        functools.partial(far_kernel, members, tile),
+        functools.partial(far_kernel, members, *far_plan),
         [queries, grad_out, near_sum, near_stat] + far_parts,
         [rows_out(jnp.bfloat16), rows_out(jnp.float32), rows_out(jnp.float32), far_out, far_out],
         [],

time: 100 us -> 85.8 us (0.86)
  waiting for transfers between devices: 30.8 us -> 15.1 us
  Pallas kernels: 30 us -> 31 us
    ppermute x11, waiting for transfers between devices: 28.6 us -> 13 us  [hop(): return lax.ppermute(part, ('seq', 'kv'), pairs)]
  transfers between devices with their start and end apart: 17 -> 17, of which waited for: 6 -> 9; matrix products, arithmetic and copies ran while one was open for 1% -> 2% of each run, Pallas kernels for 14% -> 11%
where the time goes in v1:
time: 85.8 us; the launch traced here: 84.6 us
  Pallas kernels  31 us (36%)
  starting transfers between devices  22.3 us (26%)
  waiting for transfers between devices  15.1 us (18%)
  local copies, waits for them, and re-layouts  11 us (13%)
  other arithmetic  3.68 us (4%)
  between operations  1.47 us (2%)
    pallas_call x3, Pallas kernels, call(): pl.pallas_call(kernel, in_specs=[WHOLE] * len(operands), out_specs=[WHOLE...  29.1 us
    ppermute x11, waiting for transfers between devices, hop(): return lax.ppermute(part, ('seq', 'kv'), pairs)  13 us
    unnamed x28, local copies, waits for them, and re-layouts  10.4 us
    ppermute x3, starting transfers between devices, climb(): lax.ppermute(part, 'seq', [(s, s + COLUMNS * d) for s in range(seq_count...  9.26 us
    ppermute x11, starting transfers between devices, hop(): return lax.ppermute(part, ('seq', 'kv'), pairs)  9.19 us
    ppermute x3, starting transfers between devices, sink(): lax.ppermute(part, 'seq', [(s, s - COLUMNS * d) for s in range(COLUMNS *...  3.88 us
    ppermute x3, waiting for transfers between devices, climb(): lax.ppermute(part, 'seq', [(s, s + COLUMNS * d) for s in range(seq_count...  2.11 us
    pallas_call x1, Pallas kernels, pick_pair(): pl.pallas_call(pick_kernel, in_specs=[pl.BlockSpec(memory_space=pltpu.SME...  1.89 us
  transfers between devices with their start and end apart: 17, of which 9 were waited for; matrix products, arithmetic and copies ran while one was open for 2% of the time, Pallas kernels for 11%

profile of v1, /device:TPU:0, one launch (start us, length us, event | category | flops | bytes accessed | tf_op | source)
XLA Modules:
  0.0 84.6 jit_solution(8709613971315218444)
XLA Ops:
  0.6 1.9 %shard_map.84 = (bf16[2,16,1024]{2,1,0:T(8,128)(2,1)}, bf16[2,8,16,1024]{3,2,1,0:T(8,128)(2,1)}) custom-call(s32[15,64]{1,0:T(8,128)} %bitcast.34, bf16[8,16,1024]{2,1,0:T(8,128)(2,1)} %keys_ref.1, bf16[8,16,1024]{2,1,0:T(8,128)(2,1)} %values_ref.1), custom_call_target="tpu_custom_call" | custom-call | tf_op jit(solution)/shard_map/pallas_call | solution.py:44
  2.5 3.0 %collective-permute-start.1 = (bf16[2,128,1024]{2,1,0:T(8,128)(2,1)}, bf16[2,128,1024]{2,1,0:T(8,128)(2,1)S(1)}, u32[]{:S(2)}, u32[]{:S(2)}) collective-permute-start(bf16[2,128,1024]{2,1,0:T(8,128)(2,1)} %bitcast.26), channel_id=1, source_target_pairs={{0,2},{1,3},{2,0},{3,1},{4,6},{5,7},{6,4},{7,5},{8,10},{9,11},{10,... | collective-permute-start | bytes 1572872 | tf_op jit(solution)/shard_map/ppermute | solution.py:293
  5.5 3.5 %collective-permute-start.2 = (bf16[2,16,1024]{2,1,0:T(8,128)(2,1)}, bf16[2,16,1024]{2,1,0:T(8,128)(2,1)S(1)}, u32[]{:S(2)}, u32[]{:S(2)}) collective-permute-start(bf16[2,16,1024]{2,1,0:T(8,128)(2,1)} %get-tuple-element.22), channel_id=1, source_target_pairs={{0,8},{4,12},{8,16},{12,20},{16,24},{20,28},{1,9},{5,13},{9,17},{1... | collective-permute-start | bytes 196616 | tf_op jit(solution)/shard_map/ppermute | solution.py:296
  9.0 4.5 %collective-permute-start.3 = (bf16[2,16,1024]{2,1,0:T(8,128)(2,1)}, bf16[2,16,1024]{2,1,0:T(8,128)(2,1)S(1)}, u32[]{:S(2)}, u32[]{:S(2)}) collective-permute-start(bf16[2,16,1024]{2,1,0:T(8,128)(2,1)} %get-tuple-element.22), channel_id=1, source_target_pairs={{0,16},{4,20},{8,24},{12,28},{1,17},{5,21},{9,25},{13,29},{2,18},{... | collective-permute-start | bytes 196616 | tf_op jit(solution)/shard_map/ppermute | solution.py:296
  13.5 1.3 %collective-permute-start.4 = (bf16[2,16,1024]{2,1,0:T(8,128)(2,1)}, bf16[2,16,1024]{2,1,0:T(8,128)(2,1)S(1)}, u32[]{:S(2)}, u32[]{:S(2)}) collective-permute-start(bf16[2,16,1024]{2,1,0:T(8,128)(2,1)} %get-tuple-element.22), channel_id=1, source_target_pairs={{0,24},{4,28},{1,25},{5,29},{2,26},{6,30},{3,27},{7,31}} | collective-permute-start | bytes 196616 | tf_op jit(solution)/shard_map/ppermute | solution.py:296
  14.9 1.0 %collective-permute-done.3 = bf16[2,16,1024]{2,1,0:T(8,128)(2,1)S(1)} collective-permute-done((bf16[2,16,1024]{2,1,0:T(8,128)(2,1)}, bf16[2,16,1024]{2,1,0:T(8,128)(2,1)S(1)}, u32[]{:S(2)}, u32[]{:S(2)}) %collective-permute-start.3) | collective-permute-done | bytes 65568 | tf_op jit(solution)/shard_map/ppermute | solution.py:296
  15.9 1.1 %collective-permute-done.4 = bf16[2,16,1024]{2,1,0:T(8,128)(2,1)S(1)} collective-permute-done((bf16[2,16,1024]{2,1,0:T(8,128)(2,1)}, bf16[2,16,1024]{2,1,0:T(8,128)(2,1)S(1)}, u32[]{:S(2)}, u32[]{:S(2)}) %collective-permute-start.4) | collective-permute-done | bytes 65568 | tf_op jit(solution)/shard_map/ppermute | solution.py:296
  17.0 0.9 %pad_maximum_fusion.refs_0_ = bf16[4,2,16,1024]{3,2,1,0:T(8,128)(2,1)S(1)} fusion(bf16[1,2,16,1024]{3,2,1,0:T(8,128)(2,1)S(1)} %bitcast.33, bf16[1,2,16,1024]{3,2,1,0:T(8,128)(2,1)S(1)} %bitcast.32, bf16[1,2,16,1024]{3,2,1,0:T(8,128)(2,1)S(1)} %bitcast.31, bf16[1,2,16,1024]{3,2,1,0:T(8,128)(2,1)} %bitcast.30), kind=kLoop, calls=%fused_computation.2 | loop fusion | flops 393216 | bytes 524288 | tf_op jit(solution)/shard_map/stack | solution.py:307
  17.9 2.4 %collective-permute-start.10 = (bf16[4,2,16,1024]{3,2,1,0:T(8,128)(2,1)S(1)}, bf16[4,2,16,1024]{3,2,1,0:T(8,128)(2,1)S(1)}, u32[]{:S(2)}, u32[]{:S(2)}) collective-permute-start(bf16[4,2,16,1024]{3,2,1,0:T(8,128)(2,1)S(1)} %pad_maximum_fusion.refs_0_), channel_id=1, source_target_pairs={{0,6},{1,7},{2,4},{3,5},{4,2},{5,3},{6,0},{7,1},{8,14},{9,15},{10,... | collective-permute-start | bytes 786440 | tf_op jit(solution)/shard_map/ppermute | solution.py:293
  20.3 0.7 collective-permute-start.9
  21.0 0.5 collective-permute-start.6
  21.5 1.4 %copy-done = bf16[512,1024]{1,0:T(8,128)(2,1)S(1)} copy-done((bf16[512,1024]{1,0:T(8,128)(2,1)S(1)}, bf16[512,1024]{1,0:T(8,128)(2,1)}, u32[]{:S(2)}) %copy-start) | copy-done | bytes 1048600
  22.9 1.0 %copy-done.3 = bf16[2,8,16,1024]{3,2,1,0:T(8,128)(2,1)S(1)} copy-done((bf16[2,8,16,1024]{3,2,1,0:T(8,128)(2,1)S(1)}, bf16[2,8,16,1024]{3,2,1,0:T(8,128)(2,1)}, u32[]{:S(2)}) %copy-start.3) | copy-done | bytes 524312
  24.0 3.7 %shard_map.85 = (f32[512,1024]{1,0:T(8,128)S(1)}, f32[512,1024]{1,0:T(8,128)S(1)}) custom-call(bf16[512,1024]{1,0:T(8,128)(2,1)S(1)} %copy-done, bf16[2,128,1024]{2,1,0:T(8,128)(2,1)S(1)} %bitcast.28, bf16[2,128,1024]{2,1,0:T(8,128)(2,1)S(1)} %collective-permute-done.refs_1_, bf16[2,128,1024]{2,1,0:T(8,128)(2,1)S(1)} %collective-permute-done.1.refs_2_, ...), custom_call_target="tpu_custom_call" | custom-call | flops 2147483648 | bytes 3145728 | tf_op jit(solution)/shard_map/pallas_call | solution.py:260
  28.1 5.1 %collective-permute-done.9.refs_4_ = bf16[4,2,16,1024]{3,2,1,0:T(8,128)(2,1)S(1)} collective-permute-done((bf16[4,2,16,1024]{3,2,1,0:T(8,128)(2,1)S(1)}, bf16[4,2,16,1024]{3,2,1,0:T(8,128)(2,1)S(1)}, u32[]{:S(2)}, u32[]{:S(2)}) %collective-permute-start.9) | collective-permute-done | bytes 262176 | tf_op jit(solution)/shard_map/ppermute | solution.py:293
  35.9 19.5 %shard_map.86 = (bf16[512,1024]{1,0:T(8,128)(2,1)}, f32[512,1024]{1,0:T(8,128)S(1)}, f32[512,1024]{1,0:T(8,128)S(1)}, bf16[4,2,16,1024]{3,2,1,0:T(8,128)(2,1)S(1)}, bf16[4,2,16,1024]{3,2,1,0:T(8,128)(2,1)}) custom-call(bf16[512,1024]{1,0:T(8,128)(2,1)S(1)} %copy-done.1, bf16[512,1024]{1,0:T(8,128)(2,1)S(1)} %copy-done.2, ...), custom_call_target="tpu_custom_call" | custom-call | flops 5368709120 | bytes 8388608 | tf_op jit(solution)/shard_map/pallas_call | solution.py:260
  55.3 1.3 %copy-done.9 = f32[512,1024]{1,0:T(8,128)} copy-done((f32[512,1024]{1,0:T(8,128)}, f32[512,1024]{1,0:T(8,128)S(1)}, u32[]{:S(2)}) %copy-start.9) | copy-done | bytes 2097176
  56.7 1.4 %copy-done.11 = f32[512,1024]{1,0:T(8,128)} copy-done((f32[512,1024]{1,0:T(8,128)}, f32[512,1024]{1,0:T(8,128)S(1)}, u32[]{:S(2)}) %copy-start.11) | copy-done | bytes 2097176
  58.0 1.5 %collective-permute-start.13 = (bf16[4,2,16,1024]{3,2,1,0:T(8,128)(2,1)}, bf16[4,2,16,1024]{3,2,1,0:T(8,128)(2,1)}, u32[]{:S(2)}, u32[]{:S(2)}) collective-permute-start(bf16[4,2,16,1024]{3,2,1,0:T(8,128)(2,1)} %get-tuple-element.35), channel_id=1, source_target_pairs={{0,4},{1,5},{2,6},{3,7},{4,0},{5,1},{6,2},{7,3},{8,12},{9,13},{10,... | collective-permute-start | bytes 786440 | tf_op jit(solution)/shard_map/ppermute | solution.py:293
  59.6 0.5 constant_dynamic-slice_fusion
  60.8 5.9 %collective-permute-done.13 = bf16[4,2,16,1024]{3,2,1,0:T(8,128)(2,1)} collective-permute-done((bf16[4,2,16,1024]{3,2,1,0:T(8,128)(2,1)}, bf16[4,2,16,1024]{3,2,1,0:T(8,128)(2,1)}, u32[]{:S(2)}, u32[]{:S(2)}) %collective-permute-start.13) | collective-permute-done | bytes 262176 | tf_op jit(solution)/shard_map/ppermute | solution.py:293
  66.7 1.0 %fusion.2 = (bf16[2,16,1024]{2,1,0:T(8,128)(2,1)S(1)}, bf16[2,16,1024]{2,1,0:T(8,128)(2,1)S(1)}, bf16[2,16,1024]{2,1,0:T(8,128)(2,1)S(1)}) fusion(bf16[4,2,16,1024]{3,2,1,0:T(8,128)(2,1)} %collective-permute-done.13, bf16[4,2,16,1024]{3,2,1,0:T(8,128)(2,1)S(1)} %get-tuple-element.36), kind=kLoop, calls=%fused_computation.9 | loop fusion | flops 393216 | bytes 589824 | tf_op jit(solution)/shard_map/convert_element_type | solution.py:355
  67.6 1.3 %collective-permute-start.14 = (bf16[2,16,1024]{2,1,0:T(8,128)(2,1)S(1)}, bf16[2,16,1024]{2,1,0:T(8,128)(2,1)S(1)}, u32[]{:S(2)}, u32[]{:S(2)}) collective-permute-start(bf16[2,16,1024]{2,1,0:T(8,128)(2,1)S(1)} %get-tuple-element.38), channel_id=1, source_target_pairs={{8,0},{12,4},{16,8},{20,12},{24,16},{28,20},{9,1},{13,5},{17,9},{2... | collective-permute-start | bytes 196616 | tf_op jit(solution)/shard_map/ppermute | solution.py:301
  68.9 1.3 %collective-permute-start.15 = (bf16[2,16,1024]{2,1,0:T(8,128)(2,1)S(1)}, bf16[2,16,1024]{2,1,0:T(8,128)(2,1)S(1)}, u32[]{:S(2)}, u32[]{:S(2)}) collective-permute-start(bf16[2,16,1024]{2,1,0:T(8,128)(2,1)S(1)} %get-tuple-element.40), channel_id=1, source_target_pairs={{16,0},{20,4},{24,8},{28,12},{17,1},{21,5},{25,9},{29,13},{18,2},{... | collective-permute-start | bytes 196616 | tf_op jit(solution)/shard_map/ppermute | solution.py:301
  70.2 1.3 %collective-permute-start.16 = (bf16[2,16,1024]{2,1,0:T(8,128)(2,1)S(1)}, bf16[2,16,1024]{2,1,0:T(8,128)(2,1)S(1)}, u32[]{:S(2)}, u32[]{:S(2)}) collective-permute-start(bf16[2,16,1024]{2,1,0:T(8,128)(2,1)S(1)} %get-tuple-element.39), channel_id=1, source_target_pairs={{24,0},{28,4},{25,1},{29,5},{26,2},{30,6},{27,3},{31,7}} | collective-permute-start | bytes 196616 | tf_op jit(solution)/shard_map/ppermute | solution.py:301
  71.6 1.0 %copy-done.6 = bf16[2,128,1024]{2,1,0:T(8,128)(2,1)S(1)} copy-done((bf16[2,128,1024]{2,1,0:T(8,128)(2,1)S(1)}, bf16[2,128,1024]{2,1,0:T(8,128)(2,1)}, u32[]{:S(2)}) %copy-start.6) | copy-done | bytes 524312
  72.6 1.0 %copy-done.8 = bf16[2,128,1024]{2,1,0:T(8,128)(2,1)S(1)} copy-done((bf16[2,128,1024]{2,1,0:T(8,128)(2,1)S(1)}, bf16[2,128,1024]{2,1,0:T(8,128)(2,1)}, u32[]{:S(2)}) %copy-start.8) | copy-done | bytes 524312
  73.6 1.6 %copy-done.10 = f32[512,1024]{1,0:T(8,128)S(1)} copy-done((f32[512,1024]{1,0:T(8,128)S(1)}, f32[512,1024]{1,0:T(8,128)}, u32[]{:S(2)}) %copy-start.10) | copy-done | bytes 2097176
  75.2 1.6 %copy-done.12 = f32[512,1024]{1,0:T(8,128)S(1)} copy-done((f32[512,1024]{1,0:T(8,128)S(1)}, f32[512,1024]{1,0:T(8,128)}, u32[]{:S(2)}) %copy-start.12) | copy-done | bytes 2097176
  76.8 5.9 %shard_map.87 = (bf16[512,1024]{1,0:T(8,128)(2,1)}, f32[128,1024]{1,0:T(8,128)S(1)}, f32[128,1024]{1,0:T(8,128)S(1)}) custom-call(bf16[512,1024]{1,0:T(8,128)(2,1)S(1)} %copy-done.1, bf16[512,1024]{1,0:T(8,128)(2,1)S(1)} %copy-done.2, f32[512,1024]{1,0:T(8,128)S(1)} %copy-done.12, f32[512,1024]{1,0:T(8,128)S(1)} %copy-done.10, ...), custom_call_target="tpu_custom_call" | custom-call | flops 4294967296 | bytes 8388608 | tf_op jit(solution)/shard_map/pallas_call | solution.py:260
  82.8 0.9 %fusion.1 = f32[2,16,1024]{2,1,0:T(8,128)S(1)} fusion(bf16[2,16,1024]{2,1,0:T(8,128)(2,1)S(1)} %collective-permute-done.16, bf16[2,16,1024]{2,1,0:T(8,128)(2,1)S(1)} %collective-permute-done.15, bf16[2,16,1024]{2,1,0:T(8,128)(2,1)S(1)} %collective-permute-done.14, bf16[4,2,16,1024]{3,2,1,0:T(8,128)(2,1)} %collective-permute-done.13), kind=kLoop, calls=%fused_computation.5 | loop fusion | flops 229376 | bytes 393216 | tf_op jit(solution)/shard_map/add | solution.py:365
  83.7 1.0 %add_convert_fusion = (bf16[8,16,1024]{2,1,0:T(8,128)(2,1)}, bf16[8,16,1024]{2,1,0:T(8,128)(2,1)}) fusion(f32[8,16,1024]{2,1,0:T(8,128)S(1)} %bitcast.25, f32[16,1024]{1,0:T(8,128)S(1)} %get-tuple-element.41, pred[8]{0:T(512)(128)(4,1)S(1)} %iota_compare_fusion, f32[8,16,1024]{2,1,0:T(8,128)S(1)} %bitcast.24, f32[16,1024]{1,0:T(8,128)S(1)} %get-tuple-element.42), kind=kLoop, calls=%fused_computation | loop fusion | flops 786432 | bytes 1703944 | tf_op jit(solution)/shard_map/convert_element_type | solution.py:370
  (42 shorter events, 3.3 us)
Async XLA Ops:
  2.5 15.3 %collective-permute-start.1 = (bf16[2,128,1024]{2,1,0:T(8,128)(2,1)}, bf16[2,128,1024]{2,1,0:T(8,128)(2,1)S(1)}, u32[]{:S(2)}, u32[]{:S(2)}) collective-permute-start(bf16[2,128,1024]{2,1,0:T(8,128)(2,1)} %bitcast.26), channel_id=1, source_target_pairs={{0,2},{1,3},{2,0},{3,1},{4,6},{5,7},{6,4},{7,5},{8,10},{9,11},{10,... | collective-permute-start | bytes 1572872 | tf_op jit(solution)/shard_map/ppermute | solution.py:293
  5.5 9.4 %collective-permute-start.2 = (bf16[2,16,1024]{2,1,0:T(8,128)(2,1)}, bf16[2,16,1024]{2,1,0:T(8,128)(2,1)S(1)}, u32[]{:S(2)}, u32[]{:S(2)}) collective-permute-start(bf16[2,16,1024]{2,1,0:T(8,128)(2,1)} %get-tuple-element.22), channel_id=1, source_target_pairs={{0,8},{4,12},{8,16},{12,20},{16,24},{20,28},{1,9},{5,13},{9,17},{1... | collective-permute-start | bytes 196616 | tf_op jit(solution)/shard_map/ppermute | solution.py:296
  9.0 6.9 %collective-permute-start.3 = (bf16[2,16,1024]{2,1,0:T(8,128)(2,1)}, bf16[2,16,1024]{2,1,0:T(8,128)(2,1)S(1)}, u32[]{:S(2)}, u32[]{:S(2)}) collective-permute-start(bf16[2,16,1024]{2,1,0:T(8,128)(2,1)} %get-tuple-element.22), channel_id=1, source_target_pairs={{0,16},{4,20},{8,24},{12,28},{1,17},{5,21},{9,25},{13,29},{2,18},{... | collective-permute-start | bytes 196616 | tf_op jit(solution)/shard_map/ppermute | solution.py:296
  13.5 3.5 %collective-permute-start.4 = (bf16[2,16,1024]{2,1,0:T(8,128)(2,1)}, bf16[2,16,1024]{2,1,0:T(8,128)(2,1)S(1)}, u32[]{:S(2)}, u32[]{:S(2)}) collective-permute-start(bf16[2,16,1024]{2,1,0:T(8,128)(2,1)} %get-tuple-element.22), channel_id=1, source_target_pairs={{0,24},{4,28},{1,25},{5,29},{2,26},{6,30},{3,27},{7,31}} | collective-permute-start | bytes 196616 | tf_op jit(solution)/shard_map/ppermute | solution.py:296
  14.8 6.7 %collective-permute-start = (bf16[2,128,1024]{2,1,0:T(8,128)(2,1)}, bf16[2,128,1024]{2,1,0:T(8,128)(2,1)S(1)}, u32[]{:S(2)}, u32[]{:S(2)}) collective-permute-start(bf16[2,128,1024]{2,1,0:T(8,128)(2,1)} %bitcast.27), channel_id=1, source_target_pairs={{0,1},{1,0},{2,3},{3,2},{4,5},{5,4},{6,7},{7,6},{8,9},{9,8},{10,11... | collective-permute-start | bytes 1572872 | tf_op jit(solution)/shard_map/ppermute | solution.py:293
  17.9 3.6 %collective-permute-start.5 = (bf16[2,128,1024]{2,1,0:T(8,128)(2,1)S(1)}, bf16[2,128,1024]{2,1,0:T(8,128)(2,1)S(1)}, u32[]{:S(2)}, u32[]{:S(2)}) collective-permute-start(bf16[2,128,1024]{2,1,0:T(8,128)(2,1)S(1)} %collective-permute-done.1.refs_2_), channel_id=1, source_target_pairs={{0,1},{1,0},{2,3},{3,2},{4,5},{5,4},{6,7},{7,6},{8,9},{9,8},{10,11... | collective-permute-start | bytes 1572872 | tf_op jit(solution)/shard_map/ppermute | solution.py:293
  17.9 10.1 %collective-permute-start.10 = (bf16[4,2,16,1024]{3,2,1,0:T(8,128)(2,1)S(1)}, bf16[4,2,16,1024]{3,2,1,0:T(8,128)(2,1)S(1)}, u32[]{:S(2)}, u32[]{:S(2)}) collective-permute-start(bf16[4,2,16,1024]{3,2,1,0:T(8,128)(2,1)S(1)} %pad_maximum_fusion.refs_0_), channel_id=1, source_target_pairs={{0,6},{1,7},{2,4},{3,5},{4,2},{5,3},{6,0},{7,1},{8,14},{9,15},{10,... | collective-permute-start | bytes 786440 | tf_op jit(solution)/shard_map/ppermute | solution.py:293
  20.3 12.9 %collective-permute-start.9 = (bf16[4,2,16,1024]{3,2,1,0:T(8,128)(2,1)S(1)}, bf16[4,2,16,1024]{3,2,1,0:T(8,128)(2,1)S(1)}, u32[]{:S(2)}, u32[]{:S(2)}) collective-permute-start(bf16[4,2,16,1024]{3,2,1,0:T(8,128)(2,1)S(1)} %pad_maximum_fusion.refs_0_), channel_id=1, source_target_pairs={{0,2},{1,3},{2,0},{3,1},{4,6},{5,7},{6,4},{7,5},{8,10},{9,11},{10,... | collective-permute-start | bytes 786440 | tf_op jit(solution)/shard_map/ppermute | solution.py:293
  21.0 12.7 %collective-permute-start.6 = (bf16[4,2,16,1024]{3,2,1,0:T(8,128)(2,1)S(1)}, bf16[4,2,16,1024]{3,2,1,0:T(8,128)(2,1)S(1)}, u32[]{:S(2)}, u32[]{:S(2)}) collective-permute-start(bf16[4,2,16,1024]{3,2,1,0:T(8,128)(2,1)S(1)} %pad_maximum_fusion.refs_0_), channel_id=1, source_target_pairs={{0,4},{1,5},{2,6},{3,7},{4,0},{5,1},{6,2},{7,3},{8,12},{9,13},{10,... | collective-permute-start | bytes 786440 | tf_op jit(solution)/shard_map/ppermute | solution.py:293
  21.5 6.2 %copy-start.5 = (bf16[2,128,1024]{2,1,0:T(8,128)(2,1)}, bf16[2,128,1024]{2,1,0:T(8,128)(2,1)S(1)}, u32[]{:S(2)}) copy-start(bf16[2,128,1024]{2,1,0:T(8,128)(2,1)S(1)} %collective-permute-done.refs_1_) | copy-start | bytes 1572868
  21.5 1.4 %copy-start = (bf16[512,1024]{1,0:T(8,128)(2,1)S(1)}, bf16[512,1024]{1,0:T(8,128)(2,1)}, u32[]{:S(2)}) copy-start(bf16[512,1024]{1,0:T(8,128)(2,1)} %q_ref.5) | copy-start | bytes 3145732
  22.9 1.0 %copy-start.3 = (bf16[2,8,16,1024]{3,2,1,0:T(8,128)(2,1)S(1)}, bf16[2,8,16,1024]{3,2,1,0:T(8,128)(2,1)}, u32[]{:S(2)}) copy-start(bf16[2,8,16,1024]{3,2,1,0:T(8,128)(2,1)} %get-tuple-element.21) | copy-start | bytes 1572868
  24.0 3.7 %copy-start.7 = (bf16[2,128,1024]{2,1,0:T(8,128)(2,1)}, bf16[2,128,1024]{2,1,0:T(8,128)(2,1)S(1)}, u32[]{:S(2)}) copy-start(bf16[2,128,1024]{2,1,0:T(8,128)(2,1)S(1)} %collective-permute-done.5.refs_3_) | copy-start | bytes 1572868
  24.0 11.9 %copy-start.1 = (bf16[512,1024]{1,0:T(8,128)(2,1)S(1)}, bf16[512,1024]{1,0:T(8,128)(2,1)}, u32[]{:S(2)}) copy-start(bf16[512,1024]{1,0:T(8,128)(2,1)} %q_ref.5) | copy-start | bytes 3145732
  24.0 11.9 %copy-start.2 = (bf16[512,1024]{1,0:T(8,128)(2,1)S(1)}, bf16[512,1024]{1,0:T(8,128)(2,1)}, u32[]{:S(2)}) copy-start(bf16[512,1024]{1,0:T(8,128)(2,1)} %g_ref.3) | copy-start | bytes 3145732
  33.2 1.5 %collective-permute-start.11 = (bf16[4,2,16,1024]{3,2,1,0:T(8,128)(2,1)S(1)}, bf16[4,2,16,1024]{3,2,1,0:T(8,128)(2,1)S(1)}, u32[]{:S(2)}, u32[]{:S(2)}) collective-permute-start(bf16[4,2,16,1024]{3,2,1,0:T(8,128)(2,1)S(1)} %collective-permute-done.9.refs_4_), channel_id=1, source_target_pairs={{0,1},{1,0},{2,3},{3,2},{4,5},{5,4},{6,7},{7,6},{8,9},{9,8},{10,11... | collective-permute-start | bytes 786440 | tf_op jit(solution)/shard_map/ppermute | solution.py:293
  33.2 1.9 %collective-permute-start.12 = (bf16[4,2,16,1024]{3,2,1,0:T(8,128)(2,1)S(1)}, bf16[4,2,16,1024]{3,2,1,0:T(8,128)(2,1)S(1)}, u32[]{:S(2)}, u32[]{:S(2)}) collective-permute-start(bf16[4,2,16,1024]{3,2,1,0:T(8,128)(2,1)S(1)} %collective-permute-done.10.refs_5_), channel_id=1, source_target_pairs={{0,1},{1,0},{2,3},{3,2},{4,5},{5,4},{6,7},{7,6},{8,9},{9,8},{10,11... | collective-permute-start | bytes 786440 | tf_op jit(solution)/shard_map/ppermute | solution.py:293
  33.7 1.8 %collective-permute-start.7 = (bf16[4,2,16,1024]{3,2,1,0:T(8,128)(2,1)S(1)}, bf16[4,2,16,1024]{3,2,1,0:T(8,128)(2,1)S(1)}, u32[]{:S(2)}, u32[]{:S(2)}) collective-permute-start(bf16[4,2,16,1024]{3,2,1,0:T(8,128)(2,1)S(1)} %pad_maximum_fusion.refs_0_), channel_id=1, source_target_pairs={{0,1},{1,0},{2,3},{3,2},{4,5},{5,4},{6,7},{7,6},{8,9},{9,8},{10,11... | collective-permute-start | bytes 786440 | tf_op jit(solution)/shard_map/ppermute | solution.py:293
  33.7 2.1 %collective-permute-start.8 = (bf16[4,2,16,1024]{3,2,1,0:T(8,128)(2,1)S(1)}, bf16[4,2,16,1024]{3,2,1,0:T(8,128)(2,1)S(1)}, u32[]{:S(2)}, u32[]{:S(2)}) collective-permute-start(bf16[4,2,16,1024]{3,2,1,0:T(8,128)(2,1)S(1)} %collective-permute-done.6.refs_1_), channel_id=1, source_target_pairs={{0,1},{1,0},{2,3},{3,2},{4,5},{5,4},{6,7},{7,6},{8,9},{9,8},{10,11... | collective-permute-start | bytes 786440 | tf_op jit(solution)/shard_map/ppermute | solution.py:293
  35.8 23.7 %copy-start.13 = (s32[64,15]{0,1:T(8,128)S(1)}, s32[64,15]{0,1:T(8,128)}, u32[]{:S(2)}) copy-start(s32[64,15]{0,1:T(8,128)} %param.8) | copy-start | bytes 11524
  35.8 35.7 %copy-start.4 = (bf16[2,8,16,1024]{3,2,1,0:T(8,128)(2,1)S(1)}, bf16[2,8,16,1024]{3,2,1,0:T(8,128)(2,1)}, u32[]{:S(2)}) copy-start(bf16[2,8,16,1024]{3,2,1,0:T(8,128)(2,1)} %get-tuple-element.21) | copy-start | bytes 1572868
  55.3 1.3 %copy-start.9 = (f32[512,1024]{1,0:T(8,128)}, f32[512,1024]{1,0:T(8,128)S(1)}, u32[]{:S(2)}) copy-start(f32[512,1024]{1,0:T(8,128)S(1)} %get-tuple-element.32.far_gq_ref) | copy-start | bytes 6291460
  56.7 1.4 %copy-start.11 = (f32[512,1024]{1,0:T(8,128)}, f32[512,1024]{1,0:T(8,128)S(1)}, u32[]{:S(2)}) copy-start(f32[512,1024]{1,0:T(8,128)S(1)} %get-tuple-element.31.stat_ref) | copy-start | bytes 6291460
  58.0 8.7 %collective-permute-start.13 = (bf16[4,2,16,1024]{3,2,1,0:T(8,128)(2,1)}, bf16[4,2,16,1024]{3,2,1,0:T(8,128)(2,1)}, u32[]{:S(2)}, u32[]{:S(2)}) collective-permute-start(bf16[4,2,16,1024]{3,2,1,0:T(8,128)(2,1)} %get-tuple-element.35), channel_id=1, source_target_pairs={{0,4},{1,5},{2,6},{3,7},{4,0},{5,1},{6,2},{7,3},{8,12},{9,13},{10,... | collective-permute-start | bytes 786440 | tf_op jit(solution)/shard_map/ppermute | solution.py:293
  67.6 15.1 %collective-permute-start.14 = (bf16[2,16,1024]{2,1,0:T(8,128)(2,1)S(1)}, bf16[2,16,1024]{2,1,0:T(8,128)(2,1)S(1)}, u32[]{:S(2)}, u32[]{:S(2)}) collective-permute-start(bf16[2,16,1024]{2,1,0:T(8,128)(2,1)S(1)} %get-tuple-element.38), channel_id=1, source_target_pairs={{8,0},{12,4},{16,8},{20,12},{24,16},{28,20},{9,1},{13,5},{17,9},{2... | collective-permute-start | bytes 196616 | tf_op jit(solution)/shard_map/ppermute | solution.py:301
  68.9 13.8 %collective-permute-start.15 = (bf16[2,16,1024]{2,1,0:T(8,128)(2,1)S(1)}, bf16[2,16,1024]{2,1,0:T(8,128)(2,1)S(1)}, u32[]{:S(2)}, u32[]{:S(2)}) collective-permute-start(bf16[2,16,1024]{2,1,0:T(8,128)(2,1)S(1)} %get-tuple-element.40), channel_id=1, source_target_pairs={{16,0},{20,4},{24,8},{28,12},{17,1},{21,5},{25,9},{29,13},{18,2},{... | collective-permute-start | bytes 196616 | tf_op jit(solution)/shard_map/ppermute | solution.py:301
  70.2 12.5 %collective-permute-start.16 = (bf16[2,16,1024]{2,1,0:T(8,128)(2,1)S(1)}, bf16[2,16,1024]{2,1,0:T(8,128)(2,1)S(1)}, u32[]{:S(2)}, u32[]{:S(2)}) collective-permute-start(bf16[2,16,1024]{2,1,0:T(8,128)(2,1)S(1)} %get-tuple-element.39), channel_id=1, source_target_pairs={{24,0},{28,4},{25,1},{29,5},{26,2},{30,6},{27,3},{31,7}} | collective-permute-start | bytes 196616 | tf_op jit(solution)/shard_map/ppermute | solution.py:301
  71.6 1.0 %copy-start.6 = (bf16[2,128,1024]{2,1,0:T(8,128)(2,1)S(1)}, bf16[2,128,1024]{2,1,0:T(8,128)(2,1)}, u32[]{:S(2)}) copy-start(bf16[2,128,1024]{2,1,0:T(8,128)(2,1)} %copy-done.5) | copy-start | bytes 1572868
  72.6 1.0 %copy-start.8 = (bf16[2,128,1024]{2,1,0:T(8,128)(2,1)S(1)}, bf16[2,128,1024]{2,1,0:T(8,128)(2,1)}, u32[]{:S(2)}) copy-start(bf16[2,128,1024]{2,1,0:T(8,128)(2,1)} %copy-done.7) | copy-start | bytes 1572868
  73.6 1.6 %copy-start.10 = (f32[512,1024]{1,0:T(8,128)S(1)}, f32[512,1024]{1,0:T(8,128)}, u32[]{:S(2)}) copy-start(f32[512,1024]{1,0:T(8,128)} %copy-done.9) | copy-start | bytes 6291460
  75.2 1.6 %copy-start.12 = (f32[512,1024]{1,0:T(8,128)S(1)}, f32[512,1024]{1,0:T(8,128)}, u32[]{:S(2)}) copy-start(f32[512,1024]{1,0:T(8,128)} %copy-done.11) | copy-start | bytes 6291460

commit v2 on v1

--- a/solution.py
+++ b/solution.py
@@ -21,6 +21,10 @@
 
 def dot(a, b, dims):
     return lax.dot_general(a, b, dims, preferred_element_type=jnp.float32)
+
+
+def wide(rows, width):
+    return jnp.concatenate([rows] * (width // rows.shape[1]), axis=1)
 
 
 def base2_scale(head_dim):
@@ -57,7 +61,7 @@
     return [(0, half, near // 2), (half, half, near)]
 
 
-def fill_near_bias(bias_ref, members, near, blk_len, part_tok):
+def mask_kernel(members, near, blk_len, part_tok, pair_ref, q_ref, g_ref, bias_ref):
     member = lax.axis_index("kv")
     shift = part_tok.bit_length() - 1
     for start, count, used in near_tiles(bias_ref.shape[0], near):
@@ -80,13 +84,12 @@
     return jnp.concatenate([ref[which, :used, cols] for ref in parts], axis=0)
 
 
-def near_forward_kernel(members, blk_len, part_tok, q_ref, *refs):
+def near_forward_kernel(members, bias_ref, q_ref, *refs):
     parts = refs[:members]
-    out_ref, stat_ref, bias_ref = refs[members:]
+    out_ref, stat_ref = refs[members:]
     rows, feat_width = q_ref.shape
     head_dim = feat_width // HEADS
     near = parts[0].shape[1]
-    fill_near_bias(bias_ref, members, near, blk_len, part_tok)
 
     @pl.loop(0, HEADS // GROUP)
     def _(group):
@@ -122,8 +125,8 @@
 
 def far_kernel(members, tile, heads, batch, q_ref, g_ref, sum_ref, stat_ref, *refs):
     parts = refs[: COLUMNS * members]
-    att_ref, gq_ref, stat_out_ref = refs[COLUMNS * members : COLUMNS * members + 3]
-    grad_refs = refs[COLUMNS * members + 3 :]
+    att_ref, gq_ref, level_ref, drift_ref = refs[COLUMNS * members : COLUMNS * members + 4]
+    grad_refs = refs[COLUMNS * members + 4 :]
     rows, feat_width = q_ref.shape
     head_dim = feat_width // HEADS
     steps, _, part_tok, _ = parts[0].shape
@@ -135,7 +138,7 @@
     step = lax.broadcasted_iota(jnp.int32, (1, span), 1) >> (part_tok.bit_length() - 1)
     valid = [(step >= 1) & (step <= level), (step >= 1 - side) & (step <= level)]
     bias = jnp.concatenate([jnp.where(ok, 0.0, HIDDEN) for ok in valid] * members, axis=1)
-    lane = lax.broadcasted_iota(jnp.int32, (tile, head_dim), 1)
+    total_width = members * width
 
     def work(units, keys, values, key_grads, value_grads):
         raws = [
@@ -143,13 +146,13 @@
             for i, cols, here in units
         ]
         grad_probs = [dot(g_ref[here, cols], values[i], NT) for i, cols, here in units]
-        near_levels = [stat_ref[here, cols][:, 0:1] for i, cols, here in units]
+        near_levels = [stat_ref[here, cols] for i, cols, here in units]
         peaks = [
             jnp.maximum(near_level, jnp.max(raw, axis=1, keepdims=True))
             for near_level, raw in zip(near_levels, raws)
         ]
         near_weights = [jnp.exp2(near_level - peak) for near_level, peak in zip(near_levels, peaks)]
-        weights = [jnp.exp2(raw - peak) for raw, peak in zip(raws, peaks)]
+        weights = [jnp.exp2(raw - wide(peak, total_width)) for raw, peak in zip(raws, peaks)]
         totals = [
             near_weight + jnp.sum(weight, axis=1, keepdims=True)
             for near_weight, weight in zip(near_weights, weights)
@@ -165,26 +168,25 @@
             attended = (summed * inverses[u]).astype(jnp.bfloat16)
             att_ref[here, cols] = attended
             product = g_ref[here, cols].astype(jnp.float32) * attended.astype(jnp.float32)
-            drifts.append(jnp.sum(product, axis=1, keepdims=True))
-            stat_out_ref[here, cols] = jnp.where(
-                lane < head_dim // 2, peaks[u] + jnp.log2(totals[u]), drifts[u]
-            )
+            drift = jnp.broadcast_to(jnp.sum(product, axis=1, keepdims=True), product.shape)
+            drifts.append(drift)
+            level_ref[here, cols] = peaks[u] + jnp.log2(totals[u])
+            drift_ref[here, cols] = drift
         moved = [
-            weight * (grad_prob - drift)
+            weight * (grad_prob - wide(drift, total_width))
             for weight, grad_prob, drift in zip(weights, grad_probs, drifts)
         ]
+        factors = [inverse * score_scale for inverse in inverses]
         own_scores = [
-            (part[:, :width] * (inverse * score_scale)).astype(jnp.bfloat16)
-            for part, inverse in zip(moved, inverses)
+            (part[:, :width] * wide(factor, width)).astype(jnp.bfloat16)
+            for part, factor in zip(moved, factors)
         ]
         own_probs = [
-            (weight[:, :width] * inverse).astype(jnp.bfloat16)
+            (weight[:, :width] * wide(inverse, width)).astype(jnp.bfloat16)
             for weight, inverse in zip(weights, inverses)
         ]
         for u, (i, cols, here) in enumerate(units):
-            gq_ref[here, cols] = dot(moved[u].astype(jnp.bfloat16), keys[i], NN) * (
-                inverses[u] * score_scale
-            )
+            gq_ref[here, cols] = dot(moved[u].astype(jnp.bfloat16), keys[i], NN) * factors[u]
         for u, (i, cols, here) in enumerate(units):
             key_grads[i].append(dot(own_scores[u], q_ref[here, cols], TN))
             value_grads[i].append(dot(own_probs[u], g_ref[here, cols], TN))
@@ -208,14 +210,13 @@
                     ref[:, which, :, cols] = piece.reshape(steps, part_tok, head_dim)
 
 
-def near_backward_kernel(members, blk_len, part_tok, q_ref, g_ref, stat_ref, far_gq_ref, *refs):
+def near_backward_kernel(members, bias_ref, q_ref, g_ref, level_ref, drift_ref, far_gq_ref, *refs):
     parts = refs[:members]
-    gq_ref, gk_ref, gv_ref, bias_ref = refs[members:]
+    gq_ref, gk_ref, gv_ref = refs[members:]
     rows, feat_width = q_ref.shape
     head_dim = feat_width // HEADS
     near = parts[0].shape[1]
     score_scale = 1.0 / math.sqrt(head_dim)
-    fill_near_bias(bias_ref, members, near, blk_len, part_tok)
 
     @pl.loop(0, HEADS // GROUP)
     def _(group):
@@ -234,11 +235,13 @@
         grad_probs = [
             dot(g_ref[here, cols], value, NT) for (cols, here, used), value in zip(units, values)
         ]
-        stats = [stat_ref[here, cols] for cols, here, used in units]
-        probs = [jnp.exp2(raw - stat[:, 0:1]) for raw, stat in zip(raws, stats)]
+        probs = [
+            jnp.exp2(raw - wide(level_ref[here, cols], raw.shape[1]))
+            for raw, (cols, here, used) in zip(raws, units)
+        ]
         moved = [
-            prob * (grad_prob - stat[:, head_dim // 2 : head_dim // 2 + 1])
-            for prob, grad_prob, stat in zip(probs, grad_probs, stats)
+            prob * (grad_prob - wide(drift_ref[here, cols], prob.shape[1]))
+            for prob, grad_prob, (cols, here, used) in zip(probs, grad_probs, units)
         ]
         for (cols, here, used), part, key in zip(units, moved, keys):
             gq_ref[here, cols] = (
@@ -255,13 +258,12 @@
                     ref[:used, cols] += grad
 
 
-def call(kernel, operands, outs, scratch, pairs, products, head_dim):
+def call(kernel, operands, outs, pairs, products, head_dim):
     moved_bytes = sum(a.size * a.dtype.itemsize for a in operands)
     return pl.pallas_call(
         kernel,
         in_specs=[WHOLE] * len(operands),
         out_specs=[WHOLE] * len(outs),
-        scratch_shapes=scratch,
         out_shape=outs,
         compiler_params=LIMIT,
         cost_estimate=pl.CostEstimate(
@@ -305,6 +307,15 @@
     own_pair, both = pick_pair(layout.T, keys, values)
     both = both.reshape(2, near, feat_width)
     column = jnp.stack([own_pair] + [climb(own_pair, d) for d in range(1, levels)])
+    bias = call(
+        functools.partial(mask_kernel, members, near, blk_len, part_tok),
+        [own_pair, queries, grad_out],
+        [jax.ShapeDtypeStruct((tok_rows, members * near), jnp.float32)],
+        tok_rows * members * near,
+        0,
+        1,
+    )[0]
+    column, bias = lax.optimization_barrier((column, bias))
     crossing = [
         [column if (c, step) == (0, 0) else hop(column, c, step) for c in range(COLUMNS)]
         for step in range(0, members, 2)
@@ -319,7 +330,6 @@
 
     near_out = jax.ShapeDtypeStruct((near, feat_width), jnp.float32)
     far_out = jax.ShapeDtypeStruct(column.shape, jnp.bfloat16)
-    bias_scratch = [pltpu.VMEM((tok_rows, members * near), jnp.float32)]
     near_pairs = HEADS * tok_rows * members * near
     far_width = members * seq_count * part_tok
     far_pairs = HEADS * tok_rows * far_width
@@ -327,10 +337,9 @@
     far_plan = (tok_rows // 2, GROUP, 2 * GROUP) if roomy else (tok_rows // 8, 1, 1)
 
     near_sum, near_stat = call(
-        functools.partial(near_forward_kernel, members, blk_len, part_tok),
-        [queries] + near_parts,
+        functools.partial(near_forward_kernel, members),
+        [bias, queries] + near_parts,
         [rows_out(jnp.float32), rows_out(jnp.float32)],
-        bias_scratch,
         near_pairs,
         2,
         head_dim,
@@ -339,29 +348,27 @@
     for group in crossing:
         group, _ = lax.optimization_barrier((group, near_stat))
         far_parts += group + [hop(part, 0, 1) for part in group]
-    attended, far_gq, stat, own_grad, cross_grad = call(
+    attended, far_gq, level, drift, own_grad, cross_grad = call(
         functools.partial(far_kernel, members, *far_plan),
         [queries, grad_out, near_sum, near_stat] + far_parts,
-        [rows_out(jnp.bfloat16), rows_out(jnp.float32), rows_out(jnp.float32), far_out, far_out],
-        [],
+        [rows_out(jnp.bfloat16)] + [rows_out(jnp.float32)] * 3 + [far_out, far_out],
         far_pairs,
         5,
         head_dim,
     )
-    crossed = hop(cross_grad, 1, 0)
+    grad_q, near_k, near_v = call(
+        functools.partial(near_backward_kernel, members),
+        [bias, queries, grad_out, level, drift, far_gq] + near_parts,
+        [rows_out(jnp.bfloat16), near_out, near_out],
+        near_pairs,
+        4,
+        head_dim,
+    )
+    crossed, near_k = lax.optimization_barrier((hop(cross_grad, 1, 0), near_k))
     returned = [crossed[0].astype(jnp.float32)]
     for d in range(1, levels):
         summed = own_grad[d].astype(jnp.float32) + crossed[d].astype(jnp.float32)
         returned.append(sink(summed.astype(jnp.bfloat16), d).astype(jnp.float32))
-    grad_q, near_k, near_v = call(
-        functools.partial(near_backward_kernel, members, blk_len, part_tok),
-        [queries, grad_out, stat, far_gq] + near_parts,
-        [rows_out(jnp.bfloat16), near_out, near_out],
-        bias_scratch,
-        near_pairs,
-        4,
-        head_dim,
-    )
     extra = functools.reduce(lambda a, b: a + b, returned)
     chosen = (jnp.arange(blocks) == summary_local)[:, None, None]
 

time: 85.8 us -> 72.4 us (0.84)
  Pallas kernels: 31 us -> 22 us
  other arithmetic: 3.68 us -> 1.1 us
  local copies, waits for them, and re-layouts: 11 us -> 9.79 us
    pallas_call x3 -> x4, Pallas kernels: 29.1 us -> 20.1 us  [call(): pl.pallas_call(kernel, in_specs=[WHOLE] * len(operands), out_specs=[WHOLE...]
    ppermute x3, waiting for transfers between devices: 0.01 us -> 7.82 us  [sink(): lax.ppermute(part, 'seq', [(s, s - COLUMNS * d) for s in range(COLUMNS *...]
    ppermute x11, waiting for transfers between devices: 13 us -> 7.27 us  [hop(): return lax.ppermute(part, ('seq', 'kv'), pairs)]
    ppermute x3, waiting for transfers between devices: 2.11 us -> 0.01 us  [climb(): lax.ppermute(part, 'seq', [(s, s + COLUMNS * d) for s in range(seq_count...]
    unnamed x28 -> x36, local copies, waits for them, and re-layouts: 10.4 us -> 9.19 us
    convert_element_type x1, other arithmetic: 0.95 us -> 0.05 us  [shards(): returned.append(sink(summed.astype(jnp.bfloat16), d).astype(jnp.float32))]
  transfers between devices with their start and end apart: 17 -> 17, of which waited for: 9 -> 8; matrix products, arithmetic and copies ran while one was open for 2% -> 1% of each run, Pallas kernels for 11% -> 13%
where the time goes in v2:
time: 72.4 us; the launch traced here: 71.9 us
  starting transfers between devices  22.3 us (31%)
  Pallas kernels  22 us (30%)
  waiting for transfers between devices  15.1 us (21%)
  local copies, waits for them, and re-layouts  9.79 us (14%)
  between operations  1.56 us (2%)
  other arithmetic  1.1 us (2%)
    pallas_call x4, Pallas kernels, call(): pl.pallas_call(kernel, in_specs=[WHOLE] * len(operands), out_specs=[WHOLE...  20.1 us
    ppermute x3, starting transfers between devices, climb(): lax.ppermute(part, 'seq', [(s, s + COLUMNS * d) for s in range(seq_count...  9.26 us
    unnamed x36, local copies, waits for them, and re-layouts  9.19 us
    ppermute x11, starting transfers between devices, hop(): return lax.ppermute(part, ('seq', 'kv'), pairs)  9.19 us
    ppermute x3, waiting for transfers between devices, sink(): lax.ppermute(part, 'seq', [(s, s - COLUMNS * d) for s in range(COLUMNS *...  7.82 us
    ppermute x11, waiting for transfers between devices, hop(): return lax.ppermute(part, ('seq', 'kv'), pairs)  7.27 us
    ppermute x3, starting transfers between devices, sink(): lax.ppermute(part, 'seq', [(s, s - COLUMNS * d) for s in range(COLUMNS *...  3.88 us
    pallas_call x1, Pallas kernels, pick_pair(): pl.pallas_call(pick_kernel, in_specs=[pl.BlockSpec(memory_space=pltpu.SME...  1.89 us
  transfers between devices with their start and end apart: 17, of which 8 were waited for; matrix products, arithmetic and copies ran while one was open for 1% of the time, Pallas kernels for 13%

profile of v2, /device:TPU:0, one launch (start us, length us, event | category | flops | bytes accessed | tf_op | source)
XLA Modules:
  0.0 71.9 jit_solution(10874759750095961934)
XLA Ops:
  0.6 1.9 %shard_map.84 = (bf16[2,16,1024]{2,1,0:T(8,128)(2,1)}, bf16[2,8,16,1024]{3,2,1,0:T(8,128)(2,1)}) custom-call(s32[15,64]{1,0:T(8,128)} %bitcast.32, bf16[8,16,1024]{2,1,0:T(8,128)(2,1)} %keys_ref.1, bf16[8,16,1024]{2,1,0:T(8,128)(2,1)} %values_ref.1), custom_call_target="tpu_custom_call" | custom-call | tf_op jit(solution)/shard_map/pallas_call | solution.py:48
  2.5 3.0 %collective-permute-start.4 = (bf16[2,128,1024]{2,1,0:T(8,128)(2,1)}, bf16[2,128,1024]{2,1,0:T(8,128)(2,1)S(1)}, u32[]{:S(2)}, u32[]{:S(2)}) collective-permute-start(bf16[2,128,1024]{2,1,0:T(8,128)(2,1)} %bitcast.25), channel_id=1, source_target_pairs={{0,2},{1,3},{2,0},{3,1},{4,6},{5,7},{6,4},{7,5},{8,10},{9,11},{10,... | collective-permute-start | bytes 1572872 | tf_op jit(solution)/shard_map/ppermute | solution.py:295
  5.5 3.5 %collective-permute-start = (bf16[2,16,1024]{2,1,0:T(8,128)(2,1)}, bf16[2,16,1024]{2,1,0:T(8,128)(2,1)S(1)}, u32[]{:S(2)}, u32[]{:S(2)}) collective-permute-start(bf16[2,16,1024]{2,1,0:T(8,128)(2,1)} %get-tuple-element.26.pair_ref), channel_id=1, source_target_pairs={{0,8},{4,12},{8,16},{12,20},{16,24},{20,28},{1,9},{5,13},{9,17},{1... | collective-permute-start | bytes 196616 | tf_op jit(solution)/shard_map/ppermute | solution.py:298
  9.0 4.5 %collective-permute-start.1 = (bf16[2,16,1024]{2,1,0:T(8,128)(2,1)}, bf16[2,16,1024]{2,1,0:T(8,128)(2,1)S(1)}, u32[]{:S(2)}, u32[]{:S(2)}) collective-permute-start(bf16[2,16,1024]{2,1,0:T(8,128)(2,1)} %get-tuple-element.26.pair_ref), channel_id=1, source_target_pairs={{0,16},{4,20},{8,24},{12,28},{1,17},{5,21},{9,25},{13,29},{2,18},{... | collective-permute-start | bytes 196616 | tf_op jit(solution)/shard_map/ppermute | solution.py:298
  13.5 1.3 %collective-permute-start.2 = (bf16[2,16,1024]{2,1,0:T(8,128)(2,1)}, bf16[2,16,1024]{2,1,0:T(8,128)(2,1)S(1)}, u32[]{:S(2)}, u32[]{:S(2)}) collective-permute-start(bf16[2,16,1024]{2,1,0:T(8,128)(2,1)} %get-tuple-element.26.pair_ref), channel_id=1, source_target_pairs={{0,24},{4,28},{1,25},{5,29},{2,26},{6,30},{3,27},{7,31}} | collective-permute-start | bytes 196616 | tf_op jit(solution)/shard_map/ppermute | solution.py:298
  14.9 1.2 %copy-done = bf16[512,1024]{1,0:T(8,128)(2,1)S(1)} copy-done((bf16[512,1024]{1,0:T(8,128)(2,1)S(1)}, bf16[512,1024]{1,0:T(8,128)(2,1)}, u32[]{:S(2)}) %copy-start) | copy-done | bytes 1048600
  16.1 1.2 %copy-done.2 = bf16[512,1024]{1,0:T(8,128)(2,1)S(1)} copy-done((bf16[512,1024]{1,0:T(8,128)(2,1)S(1)}, bf16[512,1024]{1,0:T(8,128)(2,1)}, u32[]{:S(2)}) %copy-start.2) | copy-done | bytes 1048600
  17.3 0.8 %copy-done.4 = bf16[2,16,1024]{2,1,0:T(8,128)(2,1)S(1)} copy-done((bf16[2,16,1024]{2,1,0:T(8,128)(2,1)S(1)}, bf16[2,16,1024]{2,1,0:T(8,128)(2,1)}, u32[]{:S(2)}) %copy-start.4) | copy-done | bytes 65560
  18.4 0.6 collective-permute-start.5
  19.0 1.4 %collective-permute-start.10 = (bf16[4,2,16,1024]{3,2,1,0:T(8,128)(2,1)S(1)}, bf16[4,2,16,1024]{3,2,1,0:T(8,128)(2,1)}, u32[]{:S(2)}, u32[]{:S(2)}) collective-permute-start(bf16[4,2,16,1024]{3,2,1,0:T(8,128)(2,1)S(1)} %pad_maximum_fusion.refs_0_), channel_id=1, source_target_pairs={{0,6},{1,7},{2,4},{3,5},{4,2},{5,3},{6,0},{7,1},{8,14},{9,15},{10,... | collective-permute-start | bytes 786440 | tf_op jit(solution)/shard_map/ppermute | solution.py:295
  20.4 1.5 %collective-permute-start.9 = (bf16[4,2,16,1024]{3,2,1,0:T(8,128)(2,1)S(1)}, bf16[4,2,16,1024]{3,2,1,0:T(8,128)(2,1)}, u32[]{:S(2)}, u32[]{:S(2)}) collective-permute-start(bf16[4,2,16,1024]{3,2,1,0:T(8,128)(2,1)S(1)} %pad_maximum_fusion.refs_0_), channel_id=1, source_target_pairs={{0,2},{1,3},{2,0},{3,1},{4,6},{5,7},{6,4},{7,5},{8,10},{9,11},{10,... | collective-permute-start | bytes 786440 | tf_op jit(solution)/shard_map/ppermute | solution.py:295
  22.0 0.5 collective-permute-start.6
  22.5 3.5 %shard_map.86 = (f32[512,1024]{1,0:T(8,128)S(1)}, f32[512,1024]{1,0:T(8,128)S(1)}) custom-call(f32[512,512]{1,0:T(8,128)S(1)} %shard_map.85.bias_ref, bf16[512,1024]{1,0:T(8,128)(2,1)S(1)} %copy-done.1, bf16[2,128,1024]{2,1,0:T(8,128)(2,1)S(1)} %bitcast.27, bf16[2,128,1024]{2,1,0:T(8,128)(2,1)S(1)} %collective-permute-done.3.refs_1_, ...), custom_call_target="tpu_custom_call" | custom-call | flops 2147483648 | bytes 4194304 | tf_op jit(solution)/shard_map/pallas_call | solution.py:263
  26.1 1.3 %copy-done.13 = f32[512,1024]{1,0:T(8,128)} copy-done((f32[512,1024]{1,0:T(8,128)}, f32[512,1024]{1,0:T(8,128)S(1)}, u32[]{:S(2)}) %copy-start.13) | copy-done | bytes 2097176
  27.5 1.3 %copy-done.15 = f32[512,1024]{1,0:T(8,128)} copy-done((f32[512,1024]{1,0:T(8,128)}, f32[512,1024]{1,0:T(8,128)S(1)}, u32[]{:S(2)}) %copy-start.15) | copy-done | bytes 2097176
  29.2 4.7 %collective-permute-done.9.refs_4_ = bf16[4,2,16,1024]{3,2,1,0:T(8,128)(2,1)} collective-permute-done((bf16[4,2,16,1024]{3,2,1,0:T(8,128)(2,1)S(1)}, bf16[4,2,16,1024]{3,2,1,0:T(8,128)(2,1)}, u32[]{:S(2)}, u32[]{:S(2)}) %collective-permute-start.9) | collective-permute-done | bytes 262176 | tf_op jit(solution)/shard_map/ppermute | solution.py:295
  33.9 0.5 collective-permute-start.12
  35.0 0.5 constant_dynamic-slice_fusion
  36.2 0.5 collective-permute-done.7.refs_2_
  36.9 1.6 %copy-done.14 = f32[512,1024]{1,0:T(8,128)S(1)} copy-done((f32[512,1024]{1,0:T(8,128)S(1)}, f32[512,1024]{1,0:T(8,128)}, u32[]{:S(2)}) %copy-start.14) | copy-done | bytes 2097176
  38.5 1.6 %copy-done.16 = f32[512,1024]{1,0:T(8,128)S(1)} copy-done((f32[512,1024]{1,0:T(8,128)S(1)}, f32[512,1024]{1,0:T(8,128)}, u32[]{:S(2)}) %copy-start.16) | copy-done | bytes 2097176
  40.1 10.6 %shard_map.87 = (bf16[512,1024]{1,0:T(8,128)(2,1)}, f32[512,1024]{1,0:T(8,128)S(1)}, f32[512,1024]{1,0:T(8,128)S(1)}, f32[512,1024]{1,0:T(8,128)S(1)}, bf16[4,2,...) custom-call(bf16[512,1024]{1,0:T(8,128)(2,1)S(1)} %copy-done.1, bf16[512,1024]{1,0:T(8,128)(2,1)S(1)} %copy-done.3, ...), custom_call_target="tpu_custom_call" | custom-call | flops 5368709120 | bytes 8388608 | tf_op jit(solution)/shard_map/pallas_call | solution.py:263
  50.8 1.1 %collective-permute-start.13 = (bf16[4,2,16,1024]{3,2,1,0:T(8,128)(2,1)S(1)}, bf16[4,2,16,1024]{3,2,1,0:T(8,128)(2,1)S(1)}, u32[]{:S(2)}, u32[]{:S(2)}) collective-permute-start(bf16[4,2,16,1024]{3,2,1,0:T(8,128)(2,1)S(1)} %get-tuple-element.42), channel_id=1, source_target_pairs={{0,4},{1,5},{2,6},{3,7},{4,0},{5,1},{6,2},{7,3},{8,12},{9,13},{10,... | collective-permute-start | bytes 786440 | tf_op jit(solution)/shard_map/ppermute | solution.py:295
  51.8 5.8 %shard_map.88 = (bf16[512,1024]{1,0:T(8,128)(2,1)}, f32[128,1024]{1,0:T(8,128)S(1)}, f32[128,1024]{1,0:T(8,128)S(1)}) custom-call(f32[512,512]{1,0:T(8,128)S(1)} %shard_map.85.bias_ref, bf16[512,1024]{1,0:T(8,128)(2,1)S(1)} %copy-done.1, bf16[512,1024]{1,0:T(8,128)(2,1)S(1)} %copy-done.3, f32[512,1024]{1,0:T(8,128)S(1)} %get-tuple-element.38.level_ref, ...), custom_call_target="tpu_custom_call" | custom-call | flops 4294967296 | bytes 11534336 | tf_op jit(solution)/shard_map/pallas_call | solution.py:263
  57.7 1.4 %collective-permute-done.13 = bf16[4,2,16,1024]{3,2,1,0:T(8,128)(2,1)S(1)} collective-permute-done((bf16[4,2,16,1024]{3,2,1,0:T(8,128)(2,1)S(1)}, bf16[4,2,16,1024]{3,2,1,0:T(8,128)(2,1)S(1)}, u32[]{:S(2)}, u32[]{:S(2)}) %collective-permute-start.13) | collective-permute-done | bytes 262176 | tf_op jit(solution)/shard_map/ppermute | solution.py:295
  59.1 1.3 %collective-permute-start.14 = (bf16[2,16,1024]{2,1,0:T(8,128)(2,1)S(1)}, bf16[2,16,1024]{2,1,0:T(8,128)(2,1)S(1)}, u32[]{:S(2)}, u32[]{:S(2)}) collective-permute-start(bf16[2,16,1024]{2,1,0:T(8,128)(2,1)S(1)} %get-tuple-element.48), channel_id=1, source_target_pairs={{8,0},{12,4},{16,8},{20,12},{24,16},{28,20},{9,1},{13,5},{17,9},{2... | collective-permute-start | bytes 196616 | tf_op jit(solution)/shard_map/ppermute | solution.py:303
  60.5 1.3 %collective-permute-start.15 = (bf16[2,16,1024]{2,1,0:T(8,128)(2,1)S(1)}, bf16[2,16,1024]{2,1,0:T(8,128)(2,1)S(1)}, u32[]{:S(2)}, u32[]{:S(2)}) collective-permute-start(bf16[2,16,1024]{2,1,0:T(8,128)(2,1)S(1)} %get-tuple-element.50), channel_id=1, source_target_pairs={{16,0},{20,4},{24,8},{28,12},{17,1},{21,5},{25,9},{29,13},{18,2},{... | collective-permute-start | bytes 196616 | tf_op jit(solution)/shard_map/ppermute | solution.py:303
  61.8 1.3 %collective-permute-start.16 = (bf16[2,16,1024]{2,1,0:T(8,128)(2,1)S(1)}, bf16[2,16,1024]{2,1,0:T(8,128)(2,1)S(1)}, u32[]{:S(2)}, u32[]{:S(2)}) collective-permute-start(bf16[2,16,1024]{2,1,0:T(8,128)(2,1)S(1)} %get-tuple-element.49), channel_id=1, source_target_pairs={{24,0},{28,4},{25,1},{29,5},{26,2},{30,6},{27,3},{31,7}} | collective-permute-start | bytes 196616 | tf_op jit(solution)/shard_map/ppermute | solution.py:303
  63.1 2.4 %collective-permute-done.14 = bf16[2,16,1024]{2,1,0:T(8,128)(2,1)S(1)} collective-permute-done((bf16[2,16,1024]{2,1,0:T(8,128)(2,1)S(1)}, bf16[2,16,1024]{2,1,0:T(8,128)(2,1)S(1)}, u32[]{:S(2)}, u32[]{:S(2)}) %collective-permute-start.14) | collective-permute-done | bytes 65568 | tf_op jit(solution)/shard_map/ppermute | solution.py:303
  65.5 2.7 %collective-permute-done.15 = bf16[2,16,1024]{2,1,0:T(8,128)(2,1)S(1)} collective-permute-done((bf16[2,16,1024]{2,1,0:T(8,128)(2,1)S(1)}, bf16[2,16,1024]{2,1,0:T(8,128)(2,1)S(1)}, u32[]{:S(2)}, u32[]{:S(2)}) %collective-permute-start.15) | collective-permute-done | bytes 65568 | tf_op jit(solution)/shard_map/ppermute | solution.py:303
  68.2 2.7 %collective-permute-done.16 = bf16[2,16,1024]{2,1,0:T(8,128)(2,1)S(1)} collective-permute-done((bf16[2,16,1024]{2,1,0:T(8,128)(2,1)S(1)}, bf16[2,16,1024]{2,1,0:T(8,128)(2,1)S(1)}, u32[]{:S(2)}, u32[]{:S(2)}) %collective-permute-start.16) | collective-permute-done | bytes 65568 | tf_op jit(solution)/shard_map/ppermute | solution.py:303
  70.9 1.0 %add_convert_fusion = (bf16[8,16,1024]{2,1,0:T(8,128)(2,1)}, bf16[8,16,1024]{2,1,0:T(8,128)(2,1)}) fusion(f32[8,16,1024]{2,1,0:T(8,128)S(1)} %bitcast.23, f32[16,1024]{1,0:T(8,128)S(1)} %get-tuple-element.51, pred[8]{0:T(512)(128)(4,1)S(1)} %iota_compare_fusion, f32[8,16,1024]{2,1,0:T(8,128)S(1)} %bitcast.22, f32[16,1024]{1,0:T(8,128)S(1)} %get-tuple-element.52), kind=kLoop, calls=%fused_computation | loop fusion | flops 786432 | bytes 1703944 | tf_op jit(solution)/shard_map/convert_element_type | solution.py:377
  (51 shorter events, 1.7 us)
Async XLA Ops:
  2.5 15.9 %collective-permute-start.4 = (bf16[2,128,1024]{2,1,0:T(8,128)(2,1)}, bf16[2,128,1024]{2,1,0:T(8,128)(2,1)S(1)}, u32[]{:S(2)}, u32[]{:S(2)}) collective-permute-start(bf16[2,128,1024]{2,1,0:T(8,128)(2,1)} %bitcast.25), channel_id=1, source_target_pairs={{0,2},{1,3},{2,0},{3,1},{4,6},{5,7},{6,4},{7,5},{8,10},{9,11},{10,... | collective-permute-start | bytes 1572872 | tf_op jit(solution)/shard_map/ppermute | solution.py:295
  5.5 12.8 %collective-permute-start = (bf16[2,16,1024]{2,1,0:T(8,128)(2,1)}, bf16[2,16,1024]{2,1,0:T(8,128)(2,1)S(1)}, u32[]{:S(2)}, u32[]{:S(2)}) collective-permute-start(bf16[2,16,1024]{2,1,0:T(8,128)(2,1)} %get-tuple-element.26.pair_ref), channel_id=1, source_target_pairs={{0,8},{4,12},{8,16},{12,20},{16,24},{20,28},{1,9},{5,13},{9,17},{1... | collective-permute-start | bytes 196616 | tf_op jit(solution)/shard_map/ppermute | solution.py:298
  9.0 9.4 %collective-permute-start.1 = (bf16[2,16,1024]{2,1,0:T(8,128)(2,1)}, bf16[2,16,1024]{2,1,0:T(8,128)(2,1)S(1)}, u32[]{:S(2)}, u32[]{:S(2)}) collective-permute-start(bf16[2,16,1024]{2,1,0:T(8,128)(2,1)} %get-tuple-element.26.pair_ref), channel_id=1, source_target_pairs={{0,16},{4,20},{8,24},{12,28},{1,17},{5,21},{9,25},{13,29},{2,18},{... | collective-permute-start | bytes 196616 | tf_op jit(solution)/shard_map/ppermute | solution.py:298
  13.5 4.9 %collective-permute-start.2 = (bf16[2,16,1024]{2,1,0:T(8,128)(2,1)}, bf16[2,16,1024]{2,1,0:T(8,128)(2,1)S(1)}, u32[]{:S(2)}, u32[]{:S(2)}) collective-permute-start(bf16[2,16,1024]{2,1,0:T(8,128)(2,1)} %get-tuple-element.26.pair_ref), channel_id=1, source_target_pairs={{0,24},{4,28},{1,25},{5,29},{2,26},{6,30},{3,27},{7,31}} | collective-permute-start | bytes 196616 | tf_op jit(solution)/shard_map/ppermute | solution.py:298
  14.8 7.7 %collective-permute-start.3 = (bf16[2,128,1024]{2,1,0:T(8,128)(2,1)}, bf16[2,128,1024]{2,1,0:T(8,128)(2,1)S(1)}, u32[]{:S(2)}, u32[]{:S(2)}) collective-permute-start(bf16[2,128,1024]{2,1,0:T(8,128)(2,1)} %bitcast.26), channel_id=1, source_target_pairs={{0,1},{1,0},{2,3},{3,2},{4,5},{5,4},{6,7},{7,6},{8,9},{9,8},{10,11... | collective-permute-start | bytes 1572872 | tf_op jit(solution)/shard_map/ppermute | solution.py:295
  18.1 4.4 %copy-start.1 = (bf16[512,1024]{1,0:T(8,128)(2,1)S(1)}, bf16[512,1024]{1,0:T(8,128)(2,1)}, u32[]{:S(2)}) copy-start(bf16[512,1024]{1,0:T(8,128)(2,1)} %q_ref.7) | copy-start | bytes 3145732
  18.1 4.4 %copy-start.5 = (bf16[2,8,16,1024]{3,2,1,0:T(8,128)(2,1)S(1)}, bf16[2,8,16,1024]{3,2,1,0:T(8,128)(2,1)}, u32[]{:S(2)}) copy-start(bf16[2,8,16,1024]{3,2,1,0:T(8,128)(2,1)} %get-tuple-element.28) | copy-start | bytes 1572868
  18.4 16.5 %copy-start.17 = (s32[64,15]{0,1:T(8,128)S(1)}, s32[64,15]{0,1:T(8,128)}, u32[]{:S(2)}) copy-start(s32[64,15]{0,1:T(8,128)} %param.8) | copy-start | bytes 11524
  18.4 18.5 %copy-start.3 = (bf16[512,1024]{1,0:T(8,128)(2,1)S(1)}, bf16[512,1024]{1,0:T(8,128)(2,1)}, u32[]{:S(2)}) copy-start(bf16[512,1024]{1,0:T(8,128)(2,1)} %g_ref.5) | copy-start | bytes 3145732
  18.4 7.7 %copy-start.7 = (bf16[2,128,1024]{2,1,0:T(8,128)(2,1)}, bf16[2,128,1024]{2,1,0:T(8,128)(2,1)S(1)}, u32[]{:S(2)}) copy-start(bf16[2,128,1024]{2,1,0:T(8,128)(2,1)S(1)} %collective-permute-done.4.refs_2_) | copy-start | bytes 1572868
  18.4 4.1 %collective-permute-start.5 = (bf16[2,128,1024]{2,1,0:T(8,128)(2,1)S(1)}, bf16[2,128,1024]{2,1,0:T(8,128)(2,1)S(1)}, u32[]{:S(2)}, u32[]{:S(2)}) collective-permute-start(bf16[2,128,1024]{2,1,0:T(8,128)(2,1)S(1)} %collective-permute-done.4.refs_2_), channel_id=1, source_target_pairs={{0,1},{1,0},{2,3},{3,2},{4,5},{5,4},{6,7},{7,6},{8,9},{9,8},{10,11... | collective-permute-start | bytes 1572872 | tf_op jit(solution)/shard_map/ppermute | solution.py:295
  19.0 10.2 %collective-permute-start.10 = (bf16[4,2,16,1024]{3,2,1,0:T(8,128)(2,1)S(1)}, bf16[4,2,16,1024]{3,2,1,0:T(8,128)(2,1)}, u32[]{:S(2)}, u32[]{:S(2)}) collective-permute-start(bf16[4,2,16,1024]{3,2,1,0:T(8,128)(2,1)S(1)} %pad_maximum_fusion.refs_0_), channel_id=1, source_target_pairs={{0,6},{1,7},{2,4},{3,5},{4,2},{5,3},{6,0},{7,1},{8,14},{9,15},{10,... | collective-permute-start | bytes 786440 | tf_op jit(solution)/shard_map/ppermute | solution.py:295
  20.4 13.5 %collective-permute-start.9 = (bf16[4,2,16,1024]{3,2,1,0:T(8,128)(2,1)S(1)}, bf16[4,2,16,1024]{3,2,1,0:T(8,128)(2,1)}, u32[]{:S(2)}, u32[]{:S(2)}) collective-permute-start(bf16[4,2,16,1024]{3,2,1,0:T(8,128)(2,1)S(1)} %pad_maximum_fusion.refs_0_), channel_id=1, source_target_pairs={{0,2},{1,3},{2,0},{3,1},{4,6},{5,7},{6,4},{7,5},{8,10},{9,11},{10,... | collective-permute-start | bytes 786440 | tf_op jit(solution)/shard_map/ppermute | solution.py:295
  22.0 12.5 %collective-permute-start.6 = (bf16[4,2,16,1024]{3,2,1,0:T(8,128)(2,1)S(1)}, bf16[4,2,16,1024]{3,2,1,0:T(8,128)(2,1)}, u32[]{:S(2)}, u32[]{:S(2)}) collective-permute-start(bf16[4,2,16,1024]{3,2,1,0:T(8,128)(2,1)S(1)} %pad_maximum_fusion.refs_0_), channel_id=1, source_target_pairs={{0,4},{1,5},{2,6},{3,7},{4,0},{5,1},{6,2},{7,3},{8,12},{9,13},{10,... | collective-permute-start | bytes 786440 | tf_op jit(solution)/shard_map/ppermute | solution.py:295
  22.5 3.6 %copy-start.9 = (bf16[2,128,1024]{2,1,0:T(8,128)(2,1)}, bf16[2,128,1024]{2,1,0:T(8,128)(2,1)S(1)}, u32[]{:S(2)}) copy-start(bf16[2,128,1024]{2,1,0:T(8,128)(2,1)S(1)} %collective-permute-done.3.refs_1_) | copy-start | bytes 1572868
  22.5 3.6 %copy-start.11 = (bf16[2,128,1024]{2,1,0:T(8,128)(2,1)}, bf16[2,128,1024]{2,1,0:T(8,128)(2,1)S(1)}, u32[]{:S(2)}) copy-start(bf16[2,128,1024]{2,1,0:T(8,128)(2,1)S(1)} %collective-permute-done.5.refs_3_) | copy-start | bytes 1572868
  26.1 1.4 %copy-start.13 = (f32[512,1024]{1,0:T(8,128)}, f32[512,1024]{1,0:T(8,128)S(1)}, u32[]{:S(2)}) copy-start(f32[512,1024]{1,0:T(8,128)S(1)} %get-tuple-element.31.sum_ref) | copy-start | bytes 6291460
  27.5 1.3 %copy-start.15 = (f32[512,1024]{1,0:T(8,128)}, f32[512,1024]{1,0:T(8,128)S(1)}, u32[]{:S(2)}) copy-start(f32[512,1024]{1,0:T(8,128)S(1)} %get-tuple-element.32.stat_ref) | copy-start | bytes 6291460
  33.9 2.3 %collective-permute-start.11 = (bf16[4,2,16,1024]{3,2,1,0:T(8,128)(2,1)}, bf16[4,2,16,1024]{3,2,1,0:T(8,128)(2,1)}, u32[]{:S(2)}, u32[]{:S(2)}) collective-permute-start(bf16[4,2,16,1024]{3,2,1,0:T(8,128)(2,1)} %collective-permute-done.9.refs_4_), channel_id=1, source_target_pairs={{0,1},{1,0},{2,3},{3,2},{4,5},{5,4},{6,7},{7,6},{8,9},{9,8},{10,11... | collective-permute-start | bytes 786440 | tf_op jit(solution)/shard_map/ppermute | solution.py:295
  33.9 2.3 %collective-permute-start.12 = (bf16[4,2,16,1024]{3,2,1,0:T(8,128)(2,1)}, bf16[4,2,16,1024]{3,2,1,0:T(8,128)(2,1)}, u32[]{:S(2)}, u32[]{:S(2)}) collective-permute-start(bf16[4,2,16,1024]{3,2,1,0:T(8,128)(2,1)} %collective-permute-done.10.refs_5_), channel_id=1, source_target_pairs={{0,1},{1,0},{2,3},{3,2},{4,5},{5,4},{6,7},{7,6},{8,9},{9,8},{10,11... | collective-permute-start | bytes 786440 | tf_op jit(solution)/shard_map/ppermute | solution.py:295
  34.4 2.3 %collective-permute-start.7 = (bf16[4,2,16,1024]{3,2,1,0:T(8,128)(2,1)S(1)}, bf16[4,2,16,1024]{3,2,1,0:T(8,128)(2,1)}, u32[]{:S(2)}, u32[]{:S(2)}) collective-permute-start(bf16[4,2,16,1024]{3,2,1,0:T(8,128)(2,1)S(1)} %pad_maximum_fusion.refs_0_), channel_id=1, source_target_pairs={{0,1},{1,0},{2,3},{3,2},{4,5},{5,4},{6,7},{7,6},{8,9},{9,8},{10,11... | collective-permute-start | bytes 786440 | tf_op jit(solution)/shard_map/ppermute | solution.py:295
  34.5 2.5 %collective-permute-start.8 = (bf16[4,2,16,1024]{3,2,1,0:T(8,128)(2,1)}, bf16[4,2,16,1024]{3,2,1,0:T(8,128)(2,1)}, u32[]{:S(2)}, u32[]{:S(2)}) collective-permute-start(bf16[4,2,16,1024]{3,2,1,0:T(8,128)(2,1)} %collective-permute-done.6.refs_1_), channel_id=1, source_target_pairs={{0,1},{1,0},{2,3},{3,2},{4,5},{5,4},{6,7},{7,6},{8,9},{9,8},{10,11... | collective-permute-start | bytes 786440 | tf_op jit(solution)/shard_map/ppermute | solution.py:295
  36.9 1.6 %copy-start.14 = (f32[512,1024]{1,0:T(8,128)S(1)}, f32[512,1024]{1,0:T(8,128)}, u32[]{:S(2)}) copy-start(f32[512,1024]{1,0:T(8,128)} %copy-done.13) | copy-start | bytes 6291460
  38.5 1.6 %copy-start.16 = (f32[512,1024]{1,0:T(8,128)S(1)}, f32[512,1024]{1,0:T(8,128)}, u32[]{:S(2)}) copy-start(f32[512,1024]{1,0:T(8,128)} %copy-done.15) | copy-start | bytes 6291460
  40.1 11.7 %copy-start.6 = (bf16[2,8,16,1024]{3,2,1,0:T(8,128)(2,1)S(1)}, bf16[2,8,16,1024]{3,2,1,0:T(8,128)(2,1)}, u32[]{:S(2)}) copy-start(bf16[2,8,16,1024]{3,2,1,0:T(8,128)(2,1)} %get-tuple-element.28) | copy-start | bytes 1572868
  40.1 11.7 %copy-start.8 = (bf16[2,128,1024]{2,1,0:T(8,128)(2,1)S(1)}, bf16[2,128,1024]{2,1,0:T(8,128)(2,1)}, u32[]{:S(2)}) copy-start(bf16[2,128,1024]{2,1,0:T(8,128)(2,1)} %copy-done.7) | copy-start | bytes 1572868
  40.1 11.7 %copy-start.10 = (bf16[2,128,1024]{2,1,0:T(8,128)(2,1)S(1)}, bf16[2,128,1024]{2,1,0:T(8,128)(2,1)}, u32[]{:S(2)}) copy-start(bf16[2,128,1024]{2,1,0:T(8,128)(2,1)} %copy-done.9) | copy-start | bytes 1572868
  40.1 11.7 %copy-start.12 = (bf16[2,128,1024]{2,1,0:T(8,128)(2,1)S(1)}, bf16[2,128,1024]{2,1,0:T(8,128)(2,1)}, u32[]{:S(2)}) copy-start(bf16[2,128,1024]{2,1,0:T(8,128)(2,1)} %copy-done.11) | copy-start | bytes 1572868
  50.8 8.3 %collective-permute-start.13 = (bf16[4,2,16,1024]{3,2,1,0:T(8,128)(2,1)S(1)}, bf16[4,2,16,1024]{3,2,1,0:T(8,128)(2,1)S(1)}, u32[]{:S(2)}, u32[]{:S(2)}) collective-permute-start(bf16[4,2,16,1024]{3,2,1,0:T(8,128)(2,1)S(1)} %get-tuple-element.42), channel_id=1, source_target_pairs={{0,4},{1,5},{2,6},{3,7},{4,0},{5,1},{6,2},{7,3},{8,12},{9,13},{10,... | collective-permute-start | bytes 786440 | tf_op jit(solution)/shard_map/ppermute | solution.py:295
  59.1 6.3 %collective-permute-start.14 = (bf16[2,16,1024]{2,1,0:T(8,128)(2,1)S(1)}, bf16[2,16,1024]{2,1,0:T(8,128)(2,1)S(1)}, u32[]{:S(2)}, u32[]{:S(2)}) collective-permute-start(bf16[2,16,1024]{2,1,0:T(8,128)(2,1)S(1)} %get-tuple-element.48), channel_id=1, source_target_pairs={{8,0},{12,4},{16,8},{20,12},{24,16},{28,20},{9,1},{13,5},{17,9},{2... | collective-permute-start | bytes 196616 | tf_op jit(solution)/shard_map/ppermute | solution.py:303
  60.5 7.8 %collective-permute-start.15 = (bf16[2,16,1024]{2,1,0:T(8,128)(2,1)S(1)}, bf16[2,16,1024]{2,1,0:T(8,128)(2,1)S(1)}, u32[]{:S(2)}, u32[]{:S(2)}) collective-permute-start(bf16[2,16,1024]{2,1,0:T(8,128)(2,1)S(1)} %get-tuple-element.50), channel_id=1, source_target_pairs={{16,0},{20,4},{24,8},{28,12},{17,1},{21,5},{25,9},{29,13},{18,2},{... | collective-permute-start | bytes 196616 | tf_op jit(solution)/shard_map/ppermute | solution.py:303
  61.8 9.1 %collective-permute-start.16 = (bf16[2,16,1024]{2,1,0:T(8,128)(2,1)S(1)}, bf16[2,16,1024]{2,1,0:T(8,128)(2,1)S(1)}, u32[]{:S(2)}, u32[]{:S(2)}) collective-permute-start(bf16[2,16,1024]{2,1,0:T(8,128)(2,1)S(1)} %get-tuple-element.49), channel_id=1, source_target_pairs={{24,0},{28,4},{25,1},{29,5},{26,2},{30,6},{27,3},{31,7}} | collective-permute-start | bytes 196616 | tf_op jit(solution)/shard_map/ppermute | solution.py:303
  (3 other events, 3.3 us)

commit v3 on v2

--- a/solution.py
+++ b/solution.py
@@ -32,11 +32,7 @@
 
 
 def pick_kernel(table_ref, keys_ref, values_ref, pair_ref, both_ref):
-    window = lax.axis_index("seq")
-    blocks = keys_ref.shape[0]
-    pick = jnp.minimum(window, lax.axis_size("seq") - 2)
-    block = table_ref[pick, table_ref.shape[1] - 1] - window * blocks
-    block = jnp.clip(block, 0, blocks - 1)
+    block = chosen_block(table_ref, keys_ref.shape[0])
     pair_ref[0] = keys_ref[block]
     pair_ref[1] = values_ref[block]
     both_ref[0] = keys_ref[...]
@@ -117,19 +113,20 @@
 
 
 def far_rows(parts, which, cols):
-    steps, _, part_tok, _ = parts[0].shape
-    return jnp.concatenate(
-        [ref[:, which, :, cols].reshape(steps * part_tok, cols.size) for ref in parts], axis=0
-    )
+    rows = []
+    for pair_ref, column_ref in zip(parts[0::2], parts[1::2]):
+        steps, _, part_tok, _ = column_ref.shape
+        rows.append(pair_ref[which, :, cols])
+        rows.append(column_ref[:, which, :, cols].reshape(steps * part_tok, cols.size))
+    return jnp.concatenate(rows, axis=0)
 
 
 def far_kernel(members, tile, heads, batch, q_ref, g_ref, sum_ref, stat_ref, *refs):
-    parts = refs[: COLUMNS * members]
-    att_ref, gq_ref, level_ref, drift_ref = refs[COLUMNS * members : COLUMNS * members + 4]
-    grad_refs = refs[COLUMNS * members + 4 :]
+    parts = refs[: 2 * COLUMNS * members]
+    att_ref, gq_ref, level_ref, drift_ref, *grad_refs = refs[2 * COLUMNS * members :]
     rows, feat_width = q_ref.shape
     head_dim = feat_width // HEADS
-    steps, _, part_tok, _ = parts[0].shape
+    steps, _, part_tok, _ = grad_refs[0].shape
     span = steps * part_tok
     width = COLUMNS * span
     score_scale = 1.0 / math.sqrt(head_dim)
@@ -258,6 +255,26 @@
                     ref[:used, cols] += grad
 
 
+def chosen_block(table_ref, blocks):
+    window = lax.axis_index("seq")
+    pick = jnp.minimum(window, lax.axis_size("seq") - 2)
+    block = table_ref[pick, table_ref.shape[1] - 1] - window * blocks
+    return jnp.clip(block, 0, blocks - 1)
+
+
+def finish_kernel(blocks, table_ref, gk_ref, gv_ref, crossed_ref, *refs):
+    arrived = refs[:-2]
+    part_tok = gk_ref.shape[0] // blocks
+    block = chosen_block(table_ref, blocks)
+    here = pl.ds(pl.multiple_of(block * part_tok, part_tok), part_tok)
+    for which, (near_ref, out_ref) in enumerate(zip((gk_ref, gv_ref), refs[-2:])):
+        out_ref[...] = near_ref[...].astype(out_ref.dtype)
+        extra = crossed_ref[0, which].astype(jnp.float32)
+        for ref in arrived:
+            extra += ref[which].astype(jnp.float32)
+        out_ref[here] = (near_ref[here] + extra).astype(out_ref.dtype)
+
+
 def call(kernel, operands, outs, pairs, products, head_dim):
     moved_bytes = sum(a.size * a.dtype.itemsize for a in operands)
     return pl.pallas_call(
@@ -274,7 +291,6 @@
 
 def shards(queries, keys, values, layout, grad_out):
     seq_count = lax.axis_size("seq")
-    seq_index = lax.axis_index("seq")
     members = lax.axis_size("kv")
     tok_rows, feat_width = queries.shape
     blocks, part_tok = (keys.shape[0], keys.shape[1])
@@ -282,10 +298,6 @@
     near = blocks * part_tok
     head_dim = feat_width // HEADS
     levels = seq_count // COLUMNS
-    pick_window = jnp.minimum(seq_index, seq_count - 2)
-    last_row = layout[layout.shape[0] - 1]
-    summary_local = jnp.clip(last_row[pick_window] - seq_index * blocks, 0, blocks - 1)
-
     def hop(part, column_step, member_step):
         pairs = [
             (s * members + m, (s ^ column_step) * members + (m ^ member_step))
@@ -306,7 +318,7 @@
 
     own_pair, both = pick_pair(layout.T, keys, values)
     both = both.reshape(2, near, feat_width)
-    column = jnp.stack([own_pair] + [climb(own_pair, d) for d in range(1, levels)])
+    column = jnp.stack([climb(own_pair, d) for d in range(1, levels)])
     bias = call(
         functools.partial(mask_kernel, members, near, blk_len, part_tok),
         [own_pair, queries, grad_out],
@@ -315,7 +327,11 @@
         0,
         1,
     )[0]
-    column, bias = lax.optimization_barrier((column, bias))
+    cross_pairs = []
+    for step in range(0, members, 2):
+        pair = hop(own_pair, 1, step)
+        cross_pairs += [pair, hop(pair, 0, 1)]
+    column, bias, cross_pairs = lax.optimization_barrier((column, bias, cross_pairs))
     crossing = [
         [column if (c, step) == (0, 0) else hop(column, c, step) for c in range(COLUMNS)]
         for step in range(0, members, 2)
@@ -329,7 +345,7 @@
         return jax.ShapeDtypeStruct((tok_rows, feat_width), dtype)
 
     near_out = jax.ShapeDtypeStruct((near, feat_width), jnp.float32)
-    far_out = jax.ShapeDtypeStruct(column.shape, jnp.bfloat16)
+    far_out = jax.ShapeDtypeStruct((levels,) + own_pair.shape, jnp.bfloat16)
     near_pairs = HEADS * tok_rows * members * near
     far_width = members * seq_count * part_tok
     far_pairs = HEADS * tok_rows * far_width
@@ -339,7 +355,7 @@
     near_sum, near_stat = call(
         functools.partial(near_forward_kernel, members),
         [bias, queries] + near_parts,
-        [rows_out(jnp.float32), rows_out(jnp.float32)],
+        [pltpu.VMEM((tok_rows, feat_width), jnp.float32)] * 2,
         near_pairs,
         2,
         head_dim,
@@ -347,7 +363,8 @@
     far_parts = []
     for group in crossing:
         group, _ = lax.optimization_barrier((group, near_stat))
-        far_parts += group + [hop(part, 0, 1) for part in group]
+        for same, other in (group, [hop(part, 0, 1) for part in group]):
+            far_parts += [own_pair, same, cross_pairs[len(far_parts) // 4], other]
     attended, far_gq, level, drift, own_grad, cross_grad = call(
         functools.partial(far_kernel, members, *far_plan),
         [queries, grad_out, near_sum, near_stat] + far_parts,
@@ -365,18 +382,17 @@
         head_dim,
     )
     crossed, near_k = lax.optimization_barrier((hop(cross_grad, 1, 0), near_k))
-    returned = [crossed[0].astype(jnp.float32)]
+    returned = []
     for d in range(1, levels):
         summed = own_grad[d].astype(jnp.float32) + crossed[d].astype(jnp.float32)
-        returned.append(sink(summed.astype(jnp.bfloat16), d).astype(jnp.float32))
-    extra = functools.reduce(lambda a, b: a + b, returned)
-    chosen = (jnp.arange(blocks) == summary_local)[:, None, None]
-
-    def finish(near_term, far_term):
-        near_term = near_term.reshape(blocks, part_tok, feat_width)
-        return (near_term + jnp.where(chosen, far_term[None], 0.0)).astype(jnp.bfloat16)
-
-    return (attended, grad_q, finish(near_k, extra[0]), finish(near_v, extra[1]))
+        returned.append(sink(summed.astype(jnp.bfloat16), d))
+    grad_k, grad_v = pl.pallas_call(
+        functools.partial(finish_kernel, blocks),
+        in_specs=[pl.BlockSpec(memory_space=pltpu.SMEM)] + [WHOLE] * (2 + levels),
+        out_specs=[WHOLE, WHOLE],
+        out_shape=[jax.ShapeDtypeStruct((near, feat_width), jnp.bfloat16)] * 2,
+    )(layout.T, near_k, near_v, crossed, *returned)
+    return (attended, grad_q, grad_k.reshape(keys.shape), grad_v.reshape(values.shape))
 
 
 def solution(mesh):

time: 72.4 us -> 70.1 us (0.968)
  local copies, waits for them, and re-layouts: 9.79 us -> 6.4 us
  starting transfers between devices: 22.3 us -> 24.8 us
  other arithmetic: 1.1 us -> 0.07 us
  between operations: 1.56 us -> 0.79 us
    unnamed x36 -> x26, local copies, waits for them, and re-layouts: 9.19 us -> 6.4 us
    pallas_call x0 -> x1, Pallas kernels: none -> 2.16 us  [shards(): pl.pallas_call(functools.partial(finish_kernel, blocks), in_specs=[pl.Blo...]
    ppermute x11 -> x15, starting transfers between devices: 9.19 us -> 11.2 us  [hop(): return lax.ppermute(part, ('seq', 'kv'), pairs)]
    pallas_call x4, Pallas kernels: 20.1 us -> 18.7 us  [call(): pl.pallas_call(kernel, in_specs=[WHOLE] * len(operands), out_specs=[WHOLE...]
    convert_element_type x2 -> x1, other arithmetic: 1.02 us -> 0.05 us  [shards(): returned.append(sink(summed.astype(jnp.bfloat16), d))]
    ppermute x3, waiting for transfers between devices: 7.82 us -> 6.86 us  [sink(): lax.ppermute(part, 'seq', [(s, s - COLUMNS * d) for s in range(COLUMNS *...]
    ppermute x11 -> x15, waiting for transfers between devices: 7.27 us -> 8.05 us  [hop(): return lax.ppermute(part, ('seq', 'kv'), pairs)]
  transfers between devices with their start and end apart: 17 -> 21, of which waited for: 8 -> 11; matrix products, arithmetic and copies ran while one was open for 1% -> 0% of each run, Pallas kernels for 13% -> 14%
where the time goes in v3:
time: 70.1 us; the launch traced here: 69.7 us
  starting transfers between devices  24.8 us (35%)
  Pallas kernels  22.7 us (32%)
  waiting for transfers between devices  14.9 us (21%)
  local copies, waits for them, and re-layouts  6.4 us (9%)
  between operations  0.79 us (1%)
    pallas_call x4, Pallas kernels, call(): pl.pallas_call(kernel, in_specs=[WHOLE] * len(operands), out_specs=[WHOLE...  18.7 us
    ppermute x15, starting transfers between devices, hop(): return lax.ppermute(part, ('seq', 'kv'), pairs)  11.2 us
    ppermute x3, starting transfers between devices, climb(): lax.ppermute(part, 'seq', [(s, s + COLUMNS * d) for s in range(seq_count...  9.73 us
    ppermute x15, waiting for transfers between devices, hop(): return lax.ppermute(part, ('seq', 'kv'), pairs)  8.05 us
    ppermute x3, waiting for transfers between devices, sink(): lax.ppermute(part, 'seq', [(s, s - COLUMNS * d) for s in range(COLUMNS *...  6.86 us
    unnamed x26, local copies, waits for them, and re-layouts  6.4 us
    ppermute x3, starting transfers between devices, sink(): lax.ppermute(part, 'seq', [(s, s - COLUMNS * d) for s in range(COLUMNS *...  3.88 us
    pallas_call x1, Pallas kernels, shards(): pl.pallas_call(functools.partial(finish_kernel, blocks), in_specs=[pl.Blo...  2.16 us
  transfers between devices with their start and end apart: 21, of which 11 were waited for; matrix products, arithmetic and copies ran while one was open for 0% of the time, Pallas kernels for 14%

profile of v3, /device:TPU:0, one launch (start us, length us, event | category | flops | bytes accessed | tf_op | source)
XLA Modules:
  0.0 69.7 jit_solution(6953038473345073447)
XLA Ops:
  0.6 1.9 %shard_map.84 = (bf16[2,16,1024]{2,1,0:T(8,128)(2,1)}, bf16[2,8,16,1024]{3,2,1,0:T(8,128)(2,1)}) custom-call(s32[15,64]{1,0:T(8,128)} %bitcast.20, bf16[8,16,1024]{2,1,0:T(8,128)(2,1)} %keys_ref.1, bf16[8,16,1024]{2,1,0:T(8,128)(2,1)} %values_ref.1), custom_call_target="tpu_custom_call" | custom-call | tf_op jit(solution)/shard_map/pallas_call | solution.py:44
  2.5 3.0 %collective-permute-start.8 = (bf16[2,128,1024]{2,1,0:T(8,128)(2,1)}, bf16[2,128,1024]{2,1,0:T(8,128)(2,1)S(1)}, u32[]{:S(2)}, u32[]{:S(2)}) collective-permute-start(bf16[2,128,1024]{2,1,0:T(8,128)(2,1)} %bitcast.13), channel_id=1, source_target_pairs={{0,2},{1,3},{2,0},{3,1},{4,6},{5,7},{6,4},{7,5},{8,10},{9,11},{10,... | collective-permute-start | bytes 1572872 | tf_op jit(solution)/shard_map/ppermute | solution.py:307
  5.5 1.4 %collective-permute-start.5 = (bf16[2,16,1024]{2,1,0:T(8,128)(2,1)}, bf16[2,16,1024]{2,1,0:T(8,128)(2,1)S(1)}, u32[]{:S(2)}, u32[]{:S(2)}) collective-permute-start(bf16[2,16,1024]{2,1,0:T(8,128)(2,1)} %get-tuple-element.32.pair_ref.refs_0_.refs_4_.refs_8_.refs_12_), channel_id=1, source_target_pairs={{0,6},{1,7},{2,4},{3,5},{4,2},{5,3},{6,0},{7,1},{8,14},{9,15},{10,... | collective-permute-start | bytes 196616 | tf_op jit(solution)/shard_map/ppermute | solution.py:307
  7.0 6.0 %collective-permute-start.2 = (bf16[2,16,1024]{2,1,0:T(8,128)(2,1)}, bf16[2,16,1024]{2,1,0:T(8,128)(2,1)S(1)}, u32[]{:S(2)}, u32[]{:S(2)}) collective-permute-start(bf16[2,16,1024]{2,1,0:T(8,128)(2,1)} %get-tuple-element.32.pair_ref.refs_0_.refs_4_.refs_8_.refs_12_), channel_id=1, source_target_pairs={{0,24},{4,28},{1,25},{5,29},{2,26},{6,30},{3,27},{7,31}} | collective-permute-start | bytes 196616 | tf_op jit(solution)/shard_map/ppermute | solution.py:310
  13.0 1.3 %collective-permute-start.1 = (bf16[2,16,1024]{2,1,0:T(8,128)(2,1)}, bf16[2,16,1024]{2,1,0:T(8,128)(2,1)S(1)}, u32[]{:S(2)}, u32[]{:S(2)}) collective-permute-start(bf16[2,16,1024]{2,1,0:T(8,128)(2,1)} %get-tuple-element.32.pair_ref.refs_0_.refs_4_.refs_8_.refs_12_), channel_id=1, source_target_pairs={{0,16},{4,20},{8,24},{12,28},{1,17},{5,21},{9,25},{13,29},{2,18},{... | collective-permute-start | bytes 196616 | tf_op jit(solution)/shard_map/ppermute | solution.py:310
  14.3 2.5 %collective-permute-start = (bf16[2,16,1024]{2,1,0:T(8,128)(2,1)}, bf16[2,16,1024]{2,1,0:T(8,128)(2,1)S(1)}, u32[]{:S(2)}, u32[]{:S(2)}) collective-permute-start(bf16[2,16,1024]{2,1,0:T(8,128)(2,1)} %get-tuple-element.32.pair_ref.refs_0_.refs_4_.refs_8_.refs_12_), channel_id=1, source_target_pairs={{0,8},{4,12},{8,16},{12,20},{16,24},{20,28},{1,9},{5,13},{9,17},{1... | collective-permute-start | bytes 196616 | tf_op jit(solution)/shard_map/ppermute | solution.py:310
  16.8 1.2 %copy-done = bf16[512,1024]{1,0:T(8,128)(2,1)S(1)} copy-done((bf16[512,1024]{1,0:T(8,128)(2,1)S(1)}, bf16[512,1024]{1,0:T(8,128)(2,1)}, u32[]{:S(2)}) %copy-start) | copy-done | bytes 1048600
  18.0 1.2 %copy-done.2 = bf16[512,1024]{1,0:T(8,128)(2,1)S(1)} copy-done((bf16[512,1024]{1,0:T(8,128)(2,1)S(1)}, bf16[512,1024]{1,0:T(8,128)(2,1)}, u32[]{:S(2)}) %copy-start.2) | copy-done | bytes 1048600
  19.2 0.8 %copy-done.6 = bf16[2,16,1024]{2,1,0:T(8,128)(2,1)S(1)} copy-done((bf16[2,16,1024]{2,1,0:T(8,128)(2,1)S(1)}, bf16[2,16,1024]{2,1,0:T(8,128)(2,1)}, u32[]{:S(2)}) %copy-start.6) | copy-done | bytes 65560
  20.2 0.9 %copy-done.8 = bf16[2,8,16,1024]{3,2,1,0:T(8,128)(2,1)S(1)} copy-done((bf16[2,8,16,1024]{3,2,1,0:T(8,128)(2,1)S(1)}, bf16[2,8,16,1024]{3,2,1,0:T(8,128)(2,1)}, u32[]{:S(2)}) %copy-start.8) | copy-done | bytes 524312
  21.1 0.5 collective-permute-start.6
  21.7 1.4 %collective-permute-done.6.refs_14_ = bf16[2,16,1024]{2,1,0:T(8,128)(2,1)S(1)} collective-permute-done((bf16[2,16,1024]{2,1,0:T(8,128)(2,1)S(1)}, bf16[2,16,1024]{2,1,0:T(8,128)(2,1)S(1)}, u32[]{:S(2)}, u32[]{:S(2)}) %collective-permute-start.6) | collective-permute-done | bytes 65568 | tf_op jit(solution)/shard_map/ppermute | solution.py:307
  23.3 2.5 %collective-permute-start.14 = (bf16[3,2,16,1024]{3,2,1,0:T(8,128)(2,1)S(1)}, bf16[3,2,16,1024]{3,2,1,0:T(8,128)(2,1)S(1)}, u32[]{:S(2)}, u32[]{:S(2)}) collective-permute-start(bf16[3,2,16,1024]{3,2,1,0:T(8,128)(2,1)S(1)} %pad_maximum_fusion.refs_1_), channel_id=1, source_target_pairs={{0,6},{1,7},{2,4},{3,5},{4,2},{5,3},{6,0},{7,1},{8,14},{9,15},{10,... | collective-permute-start | bytes 589832 | tf_op jit(solution)/shard_map/ppermute | solution.py:307
  25.8 0.5 collective-permute-start.13
  26.3 0.5 collective-permute-start.10
  26.8 3.6 %shard_map.86 = (f32[512,1024]{1,0:T(8,128)S(1)}, f32[512,1024]{1,0:T(8,128)S(1)}) custom-call(f32[512,512]{1,0:T(8,128)S(1)} %shard_map.85.bias_ref, bf16[512,1024]{1,0:T(8,128)(2,1)S(1)} %copy-done.1, bf16[2,128,1024]{2,1,0:T(8,128)(2,1)S(1)} %bitcast.15, bf16[2,128,1024]{2,1,0:T(8,128)(2,1)S(1)} %collective-permute-done.7.refs_1_, ...), custom_call_target="tpu_custom_call" | custom-call | flops 2147483648 | bytes 4194304 | tf_op jit(solution)/shard_map/pallas_call | solution.py:280
  30.4 1.6 %collective-permute-done.14.refs_11_ = bf16[3,2,16,1024]{3,2,1,0:T(8,128)(2,1)S(1)} collective-permute-done((bf16[3,2,16,1024]{3,2,1,0:T(8,128)(2,1)S(1)}, bf16[3,2,16,1024]{3,2,1,0:T(8,128)(2,1)S(1)}, u32[]{:S(2)}, u32[]{:S(2)}) %collective-permute-start.14) | collective-permute-done | bytes 196640 | tf_op jit(solution)/shard_map/ppermute | solution.py:307
  32.0 3.6 %collective-permute-done.13.refs_9_ = bf16[3,2,16,1024]{3,2,1,0:T(8,128)(2,1)S(1)} collective-permute-done((bf16[3,2,16,1024]{3,2,1,0:T(8,128)(2,1)S(1)}, bf16[3,2,16,1024]{3,2,1,0:T(8,128)(2,1)S(1)}, u32[]{:S(2)}, u32[]{:S(2)}) %collective-permute-start.13) | collective-permute-done | bytes 196640 | tf_op jit(solution)/shard_map/ppermute | solution.py:307
  35.7 0.5 collective-permute-start.12
  36.2 0.5 collective-permute-start.16
  38.0 9.2 %shard_map.87 = (bf16[512,1024]{1,0:T(8,128)(2,1)}, f32[512,1024]{1,0:T(8,128)S(1)}, f32[512,1024]{1,0:T(8,128)S(1)}, f32[512,1024]{1,0:T(8,128)S(1)}, bf16[4,2,...) custom-call(bf16[512,1024]{1,0:T(8,128)(2,1)S(1)} %copy-done.1, bf16[512,1024]{1,0:T(8,128)(2,1)S(1)} %copy-done.3, ...), custom_call_target="tpu_custom_call" | custom-call | flops 5368709120 | bytes 8388608 | tf_op jit(solution)/shard_map/pallas_call | solution.py:280
  47.2 1.5 %collective-permute-start.17 = (bf16[4,2,16,1024]{3,2,1,0:T(8,128)(2,1)S(1)}, bf16[4,2,16,1024]{3,2,1,0:T(8,128)(2,1)S(1)}, u32[]{:S(2)}, u32[]{:S(2)}) collective-permute-start(bf16[4,2,16,1024]{3,2,1,0:T(8,128)(2,1)S(1)} %get-tuple-element.52), channel_id=1, source_target_pairs={{0,4},{1,5},{2,6},{3,7},{4,0},{5,1},{6,2},{7,3},{8,12},{9,13},{10,... | collective-permute-start | bytes 786440 | tf_op jit(solution)/shard_map/ppermute | solution.py:307
  48.7 5.8 %shard_map.88 = (bf16[512,1024]{1,0:T(8,128)(2,1)}, f32[128,1024]{1,0:T(8,128)S(1)}, f32[128,1024]{1,0:T(8,128)S(1)}) custom-call(f32[512,512]{1,0:T(8,128)S(1)} %shard_map.85.bias_ref, bf16[512,1024]{1,0:T(8,128)(2,1)S(1)} %copy-done.1, bf16[512,1024]{1,0:T(8,128)(2,1)S(1)} %copy-done.3, f32[512,1024]{1,0:T(8,128)S(1)} %get-tuple-element.48.level_ref, ...), custom_call_target="tpu_custom_call" | custom-call | flops 4294967296 | bytes 11534336 | tf_op jit(solution)/shard_map/pallas_call | solution.py:280
  54.5 0.8 %copy-done.4 = f32[128,1024]{1,0:T(8,128)} copy-done((f32[128,1024]{1,0:T(8,128)}, f32[128,1024]{1,0:T(8,128)S(1)}, u32[]{:S(2)}) %copy-start.4) | copy-done | bytes 524312
  55.3 0.8 %copy-done.5 = f32[128,1024]{1,0:T(8,128)} copy-done((f32[128,1024]{1,0:T(8,128)}, f32[128,1024]{1,0:T(8,128)S(1)}, u32[]{:S(2)}) %copy-start.5) | copy-done | bytes 524312
  56.2 1.3 %collective-permute-start.20 = (bf16[2,16,1024]{2,1,0:T(8,128)(2,1)S(1)}, bf16[2,16,1024]{2,1,0:T(8,128)(2,1)S(1)}, u32[]{:S(2)}, u32[]{:S(2)}) collective-permute-start(bf16[2,16,1024]{2,1,0:T(8,128)(2,1)S(1)} %get-tuple-element.60), channel_id=1, source_target_pairs={{24,0},{28,4},{25,1},{29,5},{26,2},{30,6},{27,3},{31,7}} | collective-permute-start | bytes 196616 | tf_op jit(solution)/shard_map/ppermute | solution.py:315
  57.5 1.3 %collective-permute-start.19 = (bf16[2,16,1024]{2,1,0:T(8,128)(2,1)S(1)}, bf16[2,16,1024]{2,1,0:T(8,128)(2,1)S(1)}, u32[]{:S(2)}, u32[]{:S(2)}) collective-permute-start(bf16[2,16,1024]{2,1,0:T(8,128)(2,1)S(1)} %get-tuple-element.61), channel_id=1, source_target_pairs={{16,0},{20,4},{24,8},{28,12},{17,1},{21,5},{25,9},{29,13},{18,2},{... | collective-permute-start | bytes 196616 | tf_op jit(solution)/shard_map/ppermute | solution.py:315
  58.8 1.3 %collective-permute-start.18 = (bf16[2,16,1024]{2,1,0:T(8,128)(2,1)S(1)}, bf16[2,16,1024]{2,1,0:T(8,128)(2,1)S(1)}, u32[]{:S(2)}, u32[]{:S(2)}) collective-permute-start(bf16[2,16,1024]{2,1,0:T(8,128)(2,1)S(1)} %get-tuple-element.62), channel_id=1, source_target_pairs={{8,0},{12,4},{16,8},{20,12},{24,16},{28,20},{9,1},{13,5},{17,9},{2... | collective-permute-start | bytes 196616 | tf_op jit(solution)/shard_map/ppermute | solution.py:315
  60.1 4.5 %collective-permute-done.20.refs_2_ = bf16[2,16,1024]{2,1,0:T(8,128)(2,1)S(1)} collective-permute-done((bf16[2,16,1024]{2,1,0:T(8,128)(2,1)S(1)}, bf16[2,16,1024]{2,1,0:T(8,128)(2,1)S(1)}, u32[]{:S(2)}, u32[]{:S(2)}) %collective-permute-start.20) | collective-permute-done | bytes 65568 | tf_op jit(solution)/shard_map/ppermute | solution.py:315
  64.5 2.4 %collective-permute-done.19.refs_1_ = bf16[2,16,1024]{2,1,0:T(8,128)(2,1)S(1)} collective-permute-done((bf16[2,16,1024]{2,1,0:T(8,128)(2,1)S(1)}, bf16[2,16,1024]{2,1,0:T(8,128)(2,1)S(1)}, u32[]{:S(2)}, u32[]{:S(2)}) %collective-permute-start.19) | collective-permute-done | bytes 65568 | tf_op jit(solution)/shard_map/ppermute | solution.py:315
  66.9 0.6 copy-done.11
  67.6 2.2 %shard_map.89 = (bf16[128,1024]{1,0:T(8,128)(2,1)}, bf16[128,1024]{1,0:T(8,128)(2,1)}) custom-call(s32[15,64]{1,0:T(8,128)} %bitcast.21, f32[128,1024]{1,0:T(8,128)} %copy-done.4, f32[128,1024]{1,0:T(8,128)} %copy-done.5, bf16[4,2,16,1024]{3,2,1,0:T(8,128)(2,1)} %copy-done.9, bf16[2,16,1024]{2,1,0:T(8,128)(2,1)} %copy-done.12, ...), custom_call_target="tpu_custom_call" | custom-call | tf_op jit(solution)/shard_map/pallas_call | solution.py:389
  (44 shorter events, 2.1 us)
Async XLA Ops:
  2.5 20.7 %collective-permute-start.8 = (bf16[2,128,1024]{2,1,0:T(8,128)(2,1)}, bf16[2,128,1024]{2,1,0:T(8,128)(2,1)S(1)}, u32[]{:S(2)}, u32[]{:S(2)}) collective-permute-start(bf16[2,128,1024]{2,1,0:T(8,128)(2,1)} %bitcast.13), channel_id=1, source_target_pairs={{0,2},{1,3},{2,0},{3,1},{4,6},{5,7},{6,4},{7,5},{8,10},{9,11},{10,... | collective-permute-start | bytes 1572872 | tf_op jit(solution)/shard_map/ppermute | solution.py:307
  5.5 8.8 %collective-permute-start.5 = (bf16[2,16,1024]{2,1,0:T(8,128)(2,1)}, bf16[2,16,1024]{2,1,0:T(8,128)(2,1)S(1)}, u32[]{:S(2)}, u32[]{:S(2)}) collective-permute-start(bf16[2,16,1024]{2,1,0:T(8,128)(2,1)} %get-tuple-element.32.pair_ref.refs_0_.refs_4_.refs_8_.refs_12_), channel_id=1, source_target_pairs={{0,6},{1,7},{2,4},{3,5},{4,2},{5,3},{6,0},{7,1},{8,14},{9,15},{10,... | collective-permute-start | bytes 196616 | tf_op jit(solution)/shard_map/ppermute | solution.py:307
  6.9 13.3 %collective-permute-start.3 = (bf16[2,16,1024]{2,1,0:T(8,128)(2,1)}, bf16[2,16,1024]{2,1,0:T(8,128)(2,1)S(1)}, u32[]{:S(2)}, u32[]{:S(2)}) collective-permute-start(bf16[2,16,1024]{2,1,0:T(8,128)(2,1)} %get-tuple-element.32.pair_ref.refs_0_.refs_4_.refs_8_.refs_12_), channel_id=1, source_target_pairs={{0,4},{1,5},{2,6},{3,7},{4,0},{5,1},{6,2},{7,3},{8,12},{9,13},{10,... | collective-permute-start | bytes 196616 | tf_op jit(solution)/shard_map/ppermute | solution.py:307
  7.0 14.1 %collective-permute-start.2 = (bf16[2,16,1024]{2,1,0:T(8,128)(2,1)}, bf16[2,16,1024]{2,1,0:T(8,128)(2,1)S(1)}, u32[]{:S(2)}, u32[]{:S(2)}) collective-permute-start(bf16[2,16,1024]{2,1,0:T(8,128)(2,1)} %get-tuple-element.32.pair_ref.refs_0_.refs_4_.refs_8_.refs_12_), channel_id=1, source_target_pairs={{0,24},{4,28},{1,25},{5,29},{2,26},{6,30},{3,27},{7,31}} | collective-permute-start | bytes 196616 | tf_op jit(solution)/shard_map/ppermute | solution.py:310
  13.0 8.6 %collective-permute-start.1 = (bf16[2,16,1024]{2,1,0:T(8,128)(2,1)}, bf16[2,16,1024]{2,1,0:T(8,128)(2,1)S(1)}, u32[]{:S(2)}, u32[]{:S(2)}) collective-permute-start(bf16[2,16,1024]{2,1,0:T(8,128)(2,1)} %get-tuple-element.32.pair_ref.refs_0_.refs_4_.refs_8_.refs_12_), channel_id=1, source_target_pairs={{0,16},{4,20},{8,24},{12,28},{1,17},{5,21},{9,25},{13,29},{2,18},{... | collective-permute-start | bytes 196616 | tf_op jit(solution)/shard_map/ppermute | solution.py:310
  14.3 7.4 %collective-permute-start = (bf16[2,16,1024]{2,1,0:T(8,128)(2,1)}, bf16[2,16,1024]{2,1,0:T(8,128)(2,1)S(1)}, u32[]{:S(2)}, u32[]{:S(2)}) collective-permute-start(bf16[2,16,1024]{2,1,0:T(8,128)(2,1)} %get-tuple-element.32.pair_ref.refs_0_.refs_4_.refs_8_.refs_12_), channel_id=1, source_target_pairs={{0,8},{4,12},{8,16},{12,20},{16,24},{20,28},{1,9},{5,13},{9,17},{1... | collective-permute-start | bytes 196616 | tf_op jit(solution)/shard_map/ppermute | solution.py:310
  16.8 1.2 %copy-start = (bf16[512,1024]{1,0:T(8,128)(2,1)S(1)}, bf16[512,1024]{1,0:T(8,128)(2,1)}, u32[]{:S(2)}) copy-start(bf16[512,1024]{1,0:T(8,128)(2,1)} %q_ref.7) | copy-start | bytes 3145732
  18.0 1.2 %copy-start.2 = (bf16[512,1024]{1,0:T(8,128)(2,1)S(1)}, bf16[512,1024]{1,0:T(8,128)(2,1)}, u32[]{:S(2)}) copy-start(bf16[512,1024]{1,0:T(8,128)(2,1)} %g_ref.5) | copy-start | bytes 3145732
  19.2 0.8 %copy-start.6 = (bf16[2,16,1024]{2,1,0:T(8,128)(2,1)S(1)}, bf16[2,16,1024]{2,1,0:T(8,128)(2,1)}, u32[]{:S(2)}) copy-start(bf16[2,16,1024]{2,1,0:T(8,128)(2,1)} %get-tuple-element.32.pair_ref.refs_0_.refs_4_.refs_8_.refs_12_) | copy-start | bytes 196612
  20.0 1.0 %copy-start.8 = (bf16[2,8,16,1024]{3,2,1,0:T(8,128)(2,1)S(1)}, bf16[2,8,16,1024]{3,2,1,0:T(8,128)(2,1)}, u32[]{:S(2)}) copy-start(bf16[2,8,16,1024]{3,2,1,0:T(8,128)(2,1)} %get-tuple-element.34) | copy-start | bytes 1572868
  20.0 6.8 %copy-start.1 = (bf16[512,1024]{1,0:T(8,128)(2,1)S(1)}, bf16[512,1024]{1,0:T(8,128)(2,1)}, u32[]{:S(2)}) copy-start(bf16[512,1024]{1,0:T(8,128)(2,1)} %q_ref.7) | copy-start | bytes 3145732
  21.1 5.7 %collective-permute-start.7 = (bf16[2,128,1024]{2,1,0:T(8,128)(2,1)S(1)}, bf16[2,128,1024]{2,1,0:T(8,128)(2,1)S(1)}, u32[]{:S(2)}, u32[]{:S(2)}) collective-permute-start(bf16[2,128,1024]{2,1,0:T(8,128)(2,1)S(1)} %bitcast.14), channel_id=1, source_target_pairs={{0,1},{1,0},{2,3},{3,2},{4,5},{5,4},{6,7},{7,6},{8,9},{9,8},{10,11... | collective-permute-start | bytes 1572872 | tf_op jit(solution)/shard_map/ppermute | solution.py:307
  21.1 2.0 %collective-permute-start.6 = (bf16[2,16,1024]{2,1,0:T(8,128)(2,1)S(1)}, bf16[2,16,1024]{2,1,0:T(8,128)(2,1)S(1)}, u32[]{:S(2)}, u32[]{:S(2)}) collective-permute-start(bf16[2,16,1024]{2,1,0:T(8,128)(2,1)S(1)} %collective-permute-done.5.refs_10_), channel_id=1, source_target_pairs={{0,1},{1,0},{2,3},{3,2},{4,5},{5,4},{6,7},{7,6},{8,9},{9,8},{10,11... | collective-permute-start | bytes 196616 | tf_op jit(solution)/shard_map/ppermute | solution.py:307
  21.6 1.6 %collective-permute-start.4 = (bf16[2,16,1024]{2,1,0:T(8,128)(2,1)S(1)}, bf16[2,16,1024]{2,1,0:T(8,128)(2,1)S(1)}, u32[]{:S(2)}, u32[]{:S(2)}) collective-permute-start(bf16[2,16,1024]{2,1,0:T(8,128)(2,1)S(1)} %collective-permute-done.3.refs_2_), channel_id=1, source_target_pairs={{0,1},{1,0},{2,3},{3,2},{4,5},{5,4},{6,7},{7,6},{8,9},{9,8},{10,11... | collective-permute-start | bytes 196616 | tf_op jit(solution)/shard_map/ppermute | solution.py:307
  21.7 16.3 %copy-start.3 = (bf16[512,1024]{1,0:T(8,128)(2,1)S(1)}, bf16[512,1024]{1,0:T(8,128)(2,1)}, u32[]{:S(2)}) copy-start(bf16[512,1024]{1,0:T(8,128)(2,1)} %g_ref.5) | copy-start | bytes 3145732
  21.7 16.3 %copy-start.7 = (bf16[2,16,1024]{2,1,0:T(8,128)(2,1)S(1)}, bf16[2,16,1024]{2,1,0:T(8,128)(2,1)}, u32[]{:S(2)}) copy-start(bf16[2,16,1024]{2,1,0:T(8,128)(2,1)} %get-tuple-element.32.pair_ref.refs_0_.refs_4_.refs_8_.refs_12_) | copy-start | bytes 196612
  23.2 3.6 %collective-permute-start.9 = (bf16[2,128,1024]{2,1,0:T(8,128)(2,1)S(1)}, bf16[2,128,1024]{2,1,0:T(8,128)(2,1)S(1)}, u32[]{:S(2)}, u32[]{:S(2)}) collective-permute-start(bf16[2,128,1024]{2,1,0:T(8,128)(2,1)S(1)} %collective-permute-done.8.refs_2_), channel_id=1, source_target_pairs={{0,1},{1,0},{2,3},{3,2},{4,5},{5,4},{6,7},{7,6},{8,9},{9,8},{10,11... | collective-permute-start | bytes 1572872 | tf_op jit(solution)/shard_map/ppermute | solution.py:307
  23.3 8.7 %collective-permute-start.14 = (bf16[3,2,16,1024]{3,2,1,0:T(8,128)(2,1)S(1)}, bf16[3,2,16,1024]{3,2,1,0:T(8,128)(2,1)S(1)}, u32[]{:S(2)}, u32[]{:S(2)}) collective-permute-start(bf16[3,2,16,1024]{3,2,1,0:T(8,128)(2,1)S(1)} %pad_maximum_fusion.refs_1_), channel_id=1, source_target_pairs={{0,6},{1,7},{2,4},{3,5},{4,2},{5,3},{6,0},{7,1},{8,14},{9,15},{10,... | collective-permute-start | bytes 589832 | tf_op jit(solution)/shard_map/ppermute | solution.py:307
  25.8 9.8 %collective-permute-start.13 = (bf16[3,2,16,1024]{3,2,1,0:T(8,128)(2,1)S(1)}, bf16[3,2,16,1024]{3,2,1,0:T(8,128)(2,1)S(1)}, u32[]{:S(2)}, u32[]{:S(2)}) collective-permute-start(bf16[3,2,16,1024]{3,2,1,0:T(8,128)(2,1)S(1)} %pad_maximum_fusion.refs_1_), channel_id=1, source_target_pairs={{0,2},{1,3},{2,0},{3,1},{4,6},{5,7},{6,4},{7,5},{8,10},{9,11},{10,... | collective-permute-start | bytes 589832 | tf_op jit(solution)/shard_map/ppermute | solution.py:307
  26.3 9.4 %collective-permute-start.10 = (bf16[3,2,16,1024]{3,2,1,0:T(8,128)(2,1)S(1)}, bf16[3,2,16,1024]{3,2,1,0:T(8,128)(2,1)S(1)}, u32[]{:S(2)}, u32[]{:S(2)}) collective-permute-start(bf16[3,2,16,1024]{3,2,1,0:T(8,128)(2,1)S(1)} %pad_maximum_fusion.refs_1_), channel_id=1, source_target_pairs={{0,4},{1,5},{2,6},{3,7},{4,0},{5,1},{6,2},{7,3},{8,12},{9,13},{10,... | collective-permute-start | bytes 589832 | tf_op jit(solution)/shard_map/ppermute | solution.py:307
  35.7 1.4 %collective-permute-start.11 = (bf16[3,2,16,1024]{3,2,1,0:T(8,128)(2,1)S(1)}, bf16[3,2,16,1024]{3,2,1,0:T(8,128)(2,1)S(1)}, u32[]{:S(2)}, u32[]{:S(2)}) collective-permute-start(bf16[3,2,16,1024]{3,2,1,0:T(8,128)(2,1)S(1)} %pad_maximum_fusion.refs_1_), channel_id=1, source_target_pairs={{0,1},{1,0},{2,3},{3,2},{4,5},{5,4},{6,7},{7,6},{8,9},{9,8},{10,11... | collective-permute-start | bytes 589832 | tf_op jit(solution)/shard_map/ppermute | solution.py:307
  35.7 1.7 %collective-permute-start.12 = (bf16[3,2,16,1024]{3,2,1,0:T(8,128)(2,1)S(1)}, bf16[3,2,16,1024]{3,2,1,0:T(8,128)(2,1)S(1)}, u32[]{:S(2)}, u32[]{:S(2)}) collective-permute-start(bf16[3,2,16,1024]{3,2,1,0:T(8,128)(2,1)S(1)} %collective-permute-done.10.refs_3_), channel_id=1, source_target_pairs={{0,1},{1,0},{2,3},{3,2},{4,5},{5,4},{6,7},{7,6},{8,9},{9,8},{10,11... | collective-permute-start | bytes 589832 | tf_op jit(solution)/shard_map/ppermute | solution.py:307
  36.2 1.5 %collective-permute-start.15 = (bf16[3,2,16,1024]{3,2,1,0:T(8,128)(2,1)S(1)}, bf16[3,2,16,1024]{3,2,1,0:T(8,128)(2,1)S(1)}, u32[]{:S(2)}, u32[]{:S(2)}) collective-permute-start(bf16[3,2,16,1024]{3,2,1,0:T(8,128)(2,1)S(1)} %collective-permute-done.13.refs_9_), channel_id=1, source_target_pairs={{0,1},{1,0},{2,3},{3,2},{4,5},{5,4},{6,7},{7,6},{8,9},{9,8},{10,11... | collective-permute-start | bytes 589832 | tf_op jit(solution)/shard_map/ppermute | solution.py:307
  36.2 1.8 %collective-permute-start.16 = (bf16[3,2,16,1024]{3,2,1,0:T(8,128)(2,1)S(1)}, bf16[3,2,16,1024]{3,2,1,0:T(8,128)(2,1)S(1)}, u32[]{:S(2)}, u32[]{:S(2)}) collective-permute-start(bf16[3,2,16,1024]{3,2,1,0:T(8,128)(2,1)S(1)} %collective-permute-done.14.refs_11_), channel_id=1, source_target_pairs={{0,1},{1,0},{2,3},{3,2},{4,5},{5,4},{6,7},{7,6},{8,9},{9,8},{10,11... | collective-permute-start | bytes 589832 | tf_op jit(solution)/shard_map/ppermute | solution.py:307
  47.2 8.9 %collective-permute-start.17 = (bf16[4,2,16,1024]{3,2,1,0:T(8,128)(2,1)S(1)}, bf16[4,2,16,1024]{3,2,1,0:T(8,128)(2,1)S(1)}, u32[]{:S(2)}, u32[]{:S(2)}) collective-permute-start(bf16[4,2,16,1024]{3,2,1,0:T(8,128)(2,1)S(1)} %get-tuple-element.52), channel_id=1, source_target_pairs={{0,4},{1,5},{2,6},{3,7},{4,0},{5,1},{6,2},{7,3},{8,12},{9,13},{10,... | collective-permute-start | bytes 786440 | tf_op jit(solution)/shard_map/ppermute | solution.py:307
  54.5 0.8 %copy-start.4 = (f32[128,1024]{1,0:T(8,128)}, f32[128,1024]{1,0:T(8,128)S(1)}, u32[]{:S(2)}) copy-start(f32[128,1024]{1,0:T(8,128)S(1)} %get-tuple-element.54.gk_ref) | copy-start | bytes 1572868
  55.3 0.8 %copy-start.5 = (f32[128,1024]{1,0:T(8,128)}, f32[128,1024]{1,0:T(8,128)S(1)}, u32[]{:S(2)}) copy-start(f32[128,1024]{1,0:T(8,128)S(1)} %get-tuple-element.55.gv_ref) | copy-start | bytes 1572868
  56.1 10.8 %copy-start.9 = (bf16[4,2,16,1024]{3,2,1,0:T(8,128)(2,1)}, bf16[4,2,16,1024]{3,2,1,0:T(8,128)(2,1)S(1)}, u32[]{:S(2)}) copy-start(bf16[4,2,16,1024]{3,2,1,0:T(8,128)(2,1)S(1)} %collective-permute-done.17.crossed_ref) | copy-start | bytes 786436
  56.2 8.4 %collective-permute-start.20 = (bf16[2,16,1024]{2,1,0:T(8,128)(2,1)S(1)}, bf16[2,16,1024]{2,1,0:T(8,128)(2,1)S(1)}, u32[]{:S(2)}, u32[]{:S(2)}) collective-permute-start(bf16[2,16,1024]{2,1,0:T(8,128)(2,1)S(1)} %get-tuple-element.60), channel_id=1, source_target_pairs={{24,0},{28,4},{25,1},{29,5},{26,2},{30,6},{27,3},{31,7}} | collective-permute-start | bytes 196616 | tf_op jit(solution)/shard_map/ppermute | solution.py:315
  57.5 9.5 %collective-permute-start.19 = (bf16[2,16,1024]{2,1,0:T(8,128)(2,1)S(1)}, bf16[2,16,1024]{2,1,0:T(8,128)(2,1)S(1)}, u32[]{:S(2)}, u32[]{:S(2)}) collective-permute-start(bf16[2,16,1024]{2,1,0:T(8,128)(2,1)S(1)} %get-tuple-element.61), channel_id=1, source_target_pairs={{16,0},{20,4},{24,8},{28,12},{17,1},{21,5},{25,9},{29,13},{18,2},{... | collective-permute-start | bytes 196616 | tf_op jit(solution)/shard_map/ppermute | solution.py:315
  58.8 8.2 %collective-permute-start.18 = (bf16[2,16,1024]{2,1,0:T(8,128)(2,1)S(1)}, bf16[2,16,1024]{2,1,0:T(8,128)(2,1)S(1)}, u32[]{:S(2)}, u32[]{:S(2)}) collective-permute-start(bf16[2,16,1024]{2,1,0:T(8,128)(2,1)S(1)} %get-tuple-element.62), channel_id=1, source_target_pairs={{8,0},{12,4},{16,8},{20,12},{24,16},{28,20},{9,1},{13,5},{17,9},{2... | collective-permute-start | bytes 196616 | tf_op jit(solution)/shard_map/ppermute | solution.py:315
  64.5 2.4 %copy-start.10 = (bf16[2,16,1024]{2,1,0:T(8,128)(2,1)}, bf16[2,16,1024]{2,1,0:T(8,128)(2,1)S(1)}, u32[]{:S(2)}) copy-start(bf16[2,16,1024]{2,1,0:T(8,128)(2,1)S(1)} %collective-permute-done.20.refs_2_) | copy-start | bytes 196612
  (2 other events, 1.3 us)

commit v4 on v3

--- a/solution.py
+++ b/solution.py
@@ -31,23 +31,35 @@
     return math.log2(math.e) / math.sqrt(head_dim)
 
 
-def pick_kernel(table_ref, keys_ref, values_ref, pair_ref, both_ref):
-    block = chosen_block(table_ref, keys_ref.shape[0])
-    pair_ref[0] = keys_ref[block]
-    pair_ref[1] = values_ref[block]
-    both_ref[0] = keys_ref[...]
-    both_ref[1] = values_ref[...]
+def pick_kernel(table_ref, keys_ref, values_ref, pair_ref, both_ref, block_ref):
+    window = lax.axis_index("seq")
+    blocks = keys_ref.shape[0]
+    pick = jnp.minimum(window, lax.axis_size("seq") - 2)
+    entry = lax.broadcasted_iota(jnp.int32, table_ref.shape, 0)
+    row = lax.broadcasted_iota(jnp.int32, table_ref.shape, 1)
+    here = (entry == pick) & (row == table_ref.shape[1] - 1)
+    named = jnp.where(here, table_ref[...].astype(jnp.float32), -1.0)
+    named = jnp.max(jnp.max(named, axis=1, keepdims=True), axis=0, keepdims=True)
+    block = jnp.clip(named - (window * blocks).astype(jnp.float32), 0.0, blocks - 1.0)
+    block_ref[...] = jnp.broadcast_to(block, block_ref.shape).astype(jnp.int32)
+    for which, ref in enumerate((keys_ref, values_ref)):
+        chosen = ref[0].astype(jnp.float32)
+        for b in range(1, blocks):
+            chosen = jnp.where(block == b, ref[b].astype(jnp.float32), chosen)
+        pair_ref[which] = chosen.astype(pair_ref.dtype)
+        both_ref[which] = ref[...]
 
 
 def pick_pair(table, keys, values):
     _, part_tok, feat_width = keys.shape
     return pl.pallas_call(
         pick_kernel,
-        in_specs=[pl.BlockSpec(memory_space=pltpu.SMEM), WHOLE, WHOLE],
-        out_specs=[WHOLE, WHOLE],
+        in_specs=[WHOLE] * 3,
+        out_specs=[WHOLE] * 3,
         out_shape=[
             jax.ShapeDtypeStruct((2, part_tok, feat_width), keys.dtype),
             jax.ShapeDtypeStruct((2,) + keys.shape, keys.dtype),
+            jax.ShapeDtypeStruct((8, 128), jnp.int32),
         ],
     )(table, keys, values)
 
@@ -57,7 +69,7 @@
     return [(0, half, near // 2), (half, half, near)]
 
 
-def mask_kernel(members, near, blk_len, part_tok, pair_ref, q_ref, g_ref, bias_ref):
+def fill_mask(members, near, blk_len, part_tok, bias_ref):
     member = lax.axis_index("kv")
     shift = part_tok.bit_length() - 1
     for start, count, used in near_tiles(bias_ref.shape[0], near):
@@ -80,15 +92,30 @@
     return jnp.concatenate([ref[which, :used, cols] for ref in parts], axis=0)
 
 
-def near_forward_kernel(members, bias_ref, q_ref, *refs):
+def near_forward_kernel(members, blk_len, part_tok, q_hbm, g_hbm, *refs):
     parts = refs[:members]
-    out_ref, stat_ref = refs[members:]
+    out_ref, stat_ref, bias_ref, q_ref, g_ref, sems = refs[members:]
     rows, feat_width = q_ref.shape
     head_dim = feat_width // HEADS
     near = parts[0].shape[1]
+    slab = feat_width * GROUP // HEADS
+    copies = [
+        pltpu.make_async_copy(q_hbm.at[:, pl.ds(c, slab)], q_ref.at[:, pl.ds(c, slab)], sems.at[i])
+        for i, c in enumerate(range(0, feat_width, slab))
+    ]
+    copies.append(pltpu.make_async_copy(g_hbm, g_ref, sems.at[HEADS // GROUP]))
+    for copy in copies:
+        copy.start()
+    fill_mask(members, near, blk_len, part_tok, bias_ref)
+    copies[0].wait()
 
     @pl.loop(0, HEADS // GROUP)
     def _(group):
+        @pl.when(group > 0)
+        def _():
+            cols = pl.ds(pl.multiple_of(group * slab, slab), slab)
+            pltpu.make_async_copy(q_hbm.at[:, cols], q_ref.at[:, cols], sems.at[group]).wait()
+
         units = [
             (head_columns(group * GROUP + i, feat_width), pl.ds(start, count), used)
             for i in range(GROUP)
@@ -110,6 +137,8 @@
             level = peak + jnp.log2(total)
             stat_ref[here, cols] = jnp.broadcast_to(level, summed.shape)
             out_ref[here, cols] = summed * (1.0 / total)
+
+    copies[-1].wait()
 
 
 def far_rows(parts, which, cols):
@@ -255,33 +284,14 @@
                     ref[:used, cols] += grad
 
 
-def chosen_block(table_ref, blocks):
-    window = lax.axis_index("seq")
-    pick = jnp.minimum(window, lax.axis_size("seq") - 2)
-    block = table_ref[pick, table_ref.shape[1] - 1] - window * blocks
-    return jnp.clip(block, 0, blocks - 1)
-
-
-def finish_kernel(blocks, table_ref, gk_ref, gv_ref, crossed_ref, *refs):
-    arrived = refs[:-2]
-    part_tok = gk_ref.shape[0] // blocks
-    block = chosen_block(table_ref, blocks)
-    here = pl.ds(pl.multiple_of(block * part_tok, part_tok), part_tok)
-    for which, (near_ref, out_ref) in enumerate(zip((gk_ref, gv_ref), refs[-2:])):
-        out_ref[...] = near_ref[...].astype(out_ref.dtype)
-        extra = crossed_ref[0, which].astype(jnp.float32)
-        for ref in arrived:
-            extra += ref[which].astype(jnp.float32)
-        out_ref[here] = (near_ref[here] + extra).astype(out_ref.dtype)
-
-
-def call(kernel, operands, outs, pairs, products, head_dim):
+def call(kernel, operands, outs, pairs, products, head_dim, in_specs=None, scratch=()):
     moved_bytes = sum(a.size * a.dtype.itemsize for a in operands)
     return pl.pallas_call(
         kernel,
-        in_specs=[WHOLE] * len(operands),
+        in_specs=in_specs or [WHOLE] * len(operands),
         out_specs=[WHOLE] * len(outs),
         out_shape=outs,
+        scratch_shapes=scratch,
         compiler_params=LIMIT,
         cost_estimate=pl.CostEstimate(
             flops=4 * products * pairs * head_dim, bytes_accessed=moved_bytes, transcendentals=pairs
@@ -316,22 +326,16 @@
             part, "seq", [(s, s - COLUMNS * d) for s in range(COLUMNS * d, seq_count)]
         )
 
-    own_pair, both = pick_pair(layout.T, keys, values)
+    own_pair, both, block = pick_pair(layout.T, keys, values)
     both = both.reshape(2, near, feat_width)
-    column = jnp.stack([climb(own_pair, d) for d in range(1, levels)])
-    bias = call(
-        functools.partial(mask_kernel, members, near, blk_len, part_tok),
-        [own_pair, queries, grad_out],
-        [jax.ShapeDtypeStruct((tok_rows, members * near), jnp.float32)],
-        tok_rows * members * near,
-        0,
-        1,
-    )[0]
+    climbed = [climb(own_pair, d) for d in range(1, levels)]
+    column = jnp.stack(climbed)
+    sent_pair, _ = lax.optimization_barrier((own_pair, climbed[0]))
     cross_pairs = []
     for step in range(0, members, 2):
-        pair = hop(own_pair, 1, step)
+        pair = hop(sent_pair, 1, step)
         cross_pairs += [pair, hop(pair, 0, 1)]
-    column, bias, cross_pairs = lax.optimization_barrier((column, bias, cross_pairs))
+    column, cross_pairs = lax.optimization_barrier((column, cross_pairs))
     crossing = [
         [column if (c, step) == (0, 0) else hop(column, c, step) for c in range(COLUMNS)]
         for step in range(0, members, 2)
@@ -352,13 +356,18 @@
     roomy = far_width <= 512
     far_plan = (tok_rows // 2, GROUP, 2 * GROUP) if roomy else (tok_rows // 8, 1, 1)
 
-    near_sum, near_stat = call(
-        functools.partial(near_forward_kernel, members),
-        [bias, queries] + near_parts,
-        [pltpu.VMEM((tok_rows, feat_width), jnp.float32)] * 2,
+    in_hbm = pl.BlockSpec(memory_space=pltpu.HBM)
+    near_sum, near_stat, bias, queries, grad_out = call(
+        functools.partial(near_forward_kernel, members, blk_len, part_tok),
+        [pltpu.with_memory_space_constraint(a, pltpu.HBM) for a in (queries, grad_out)] + near_parts,
+        [pltpu.VMEM((tok_rows, feat_width), jnp.float32)] * 2
+        + [pltpu.VMEM((tok_rows, members * near), jnp.float32)]
+        + [pltpu.VMEM((tok_rows, feat_width), jnp.bfloat16)] * 2,
         near_pairs,
         2,
         head_dim,
+        [in_hbm, in_hbm] + [WHOLE] * members,
+        [pltpu.SemaphoreType.DMA((HEADS // GROUP + 1,))],
     )
     far_parts = []
     for group in crossing:
@@ -386,13 +395,14 @@
     for d in range(1, levels):
         summed = own_grad[d].astype(jnp.float32) + crossed[d].astype(jnp.float32)
         returned.append(sink(summed.astype(jnp.bfloat16), d))
-    grad_k, grad_v = pl.pallas_call(
-        functools.partial(finish_kernel, blocks),
-        in_specs=[pl.BlockSpec(memory_space=pltpu.SMEM)] + [WHOLE] * (2 + levels),
-        out_specs=[WHOLE, WHOLE],
-        out_shape=[jax.ShapeDtypeStruct((near, feat_width), jnp.bfloat16)] * 2,
-    )(layout.T, near_k, near_v, crossed, *returned)
-    return (attended, grad_q, grad_k.reshape(keys.shape), grad_v.reshape(values.shape))
+    extra = sum(part.astype(jnp.float32) for part in [crossed[0]] + returned)
+    chosen = (jnp.arange(blocks) == block[0, 0])[:, None, None]
+
+    def finish(near_term, far_term):
+        near_term = near_term.reshape(blocks, part_tok, feat_width)
+        return (near_term + jnp.where(chosen, far_term[None], 0.0)).astype(jnp.bfloat16)
+
+    return (attended, grad_q, finish(near_k, extra[0]), finish(near_v, extra[1]))
 
 
 def solution(mesh):

time: 70.1 us -> 66.4 us (0.947)
  local copies, waits for them, and re-layouts: 6.4 us -> 2.29 us
  other arithmetic: 0.07 us -> 1.69 us
  waiting for transfers between devices: 14.9 us -> 13.3 us
  starting transfers between devices: 24.8 us -> 26.4 us
  Pallas kernels: 22.7 us -> 21.5 us
    unnamed x26 -> x6, local copies, waits for them, and re-layouts: 6.4 us -> 1.05 us
    ppermute x15, waiting for transfers between devices: 8.05 us -> 4.48 us  [hop(): return lax.ppermute(part, ('seq', 'kv'), pairs)]
    ppermute x3, waiting for transfers between devices: 0.01 us -> 1.53 us  [climb(): lax.ppermute(part, 'seq', [(s, s + COLUMNS * d) for s in range(seq_count...]
    pallas_call x6 -> x4, Pallas kernels: 22.7 us -> 21.5 us  [the longest x3 19.6 us: call(): pl.pallas_call(kernel, in_specs=in_specs or [WHOLE] * len(operands), out_...]
    slice x0 -> x1, local copies, waits for them, and re-layouts: none -> 1.23 us  [shards(): chosen = (jnp.arange(blocks) == block[0, 0])[:, None, None]]
    ppermute x3, starting transfers between devices: 9.73 us -> 10.8 us  [climb(): lax.ppermute(part, 'seq', [(s, s + COLUMNS * d) for s in range(seq_count...]
    convert_element_type x0 -> x1, other arithmetic: none -> 0.97 us  [finish(): (near_term + jnp.where(chosen, far_term[None], 0.0)).astype(jnp.bfloat16)]
  transfers between devices with their start and end apart: 21 -> 21, of which waited for: 11 -> 7; matrix products, arithmetic and copies ran while one was open for 0% -> 3% of each run, Pallas kernels for 14% -> 16%
where the time goes in v4:
time: 66.4 us; the launch traced here: 66.1 us
  starting transfers between devices  26.4 us (40%)
  Pallas kernels  21.5 us (32%)
  waiting for transfers between devices  13.3 us (20%)
  local copies, waits for them, and re-layouts  2.29 us (3%)
  other arithmetic  1.69 us (3%)
  between operations  0.81 us (1%)
    pallas_call x3, Pallas kernels, call(): pl.pallas_call(kernel, in_specs=in_specs or [WHOLE] * len(operands), out_...  19.6 us
    ppermute x15, starting transfers between devices, hop(): return lax.ppermute(part, ('seq', 'kv'), pairs)  11.8 us
    ppermute x3, starting transfers between devices, climb(): lax.ppermute(part, 'seq', [(s, s + COLUMNS * d) for s in range(seq_count...  10.8 us
    ppermute x3, waiting for transfers between devices, sink(): lax.ppermute(part, 'seq', [(s, s - COLUMNS * d) for s in range(COLUMNS *...  7.33 us
    ppermute x15, waiting for transfers between devices, hop(): return lax.ppermute(part, ('seq', 'kv'), pairs)  4.48 us
    ppermute x3, starting transfers between devices, sink(): lax.ppermute(part, 'seq', [(s, s - COLUMNS * d) for s in range(COLUMNS *...  3.88 us
    pallas_call x1, Pallas kernels, pick_pair(): pl.pallas_call(pick_kernel, in_specs=[WHOLE] * 3, out_specs=[WHOLE] * 3,...  1.9 us
    ppermute x3, waiting for transfers between devices, climb(): lax.ppermute(part, 'seq', [(s, s + COLUMNS * d) for s in range(seq_count...  1.53 us
  transfers between devices with their start and end apart: 21, of which 7 were waited for; matrix products, arithmetic and copies ran while one was open for 3% of the time, Pallas kernels for 16%

profile of v4, /device:TPU:0, one launch (start us, length us, event | category | flops | bytes accessed | tf_op | source)
XLA Modules:
  0.0 66.1 jit_solution(8676956249435868537)
XLA Ops:
  0.6 1.9 %shard_map.84 = (bf16[2,16,1024]{2,1,0:T(8,128)(2,1)}, bf16[2,8,16,1024]{3,2,1,0:T(8,128)(2,1)}, s32[8,128]{1,0:T(8,128)}) custom-call(s32[15,64]{1,0:T(8,128)} %bitcast.30, bf16[8,16,1024]{2,1,0:T(8,128)(2,1)} %keys_ref.1, bf16[8,16,1024]{2,1,0:T(8,128)(2,1)} %values_ref.1), custom_call_target="tpu_custom_call" | custom-call | tf_op jit(solution)/shard_map/pallas_call | solution.py:55
  2.5 3.0 %collective-permute-start.1 = (bf16[2,128,1024]{2,1,0:T(8,128)(2,1)}, bf16[2,128,1024]{2,1,0:T(8,128)(2,1)S(1)}, u32[]{:S(2)}, u32[]{:S(2)}) collective-permute-start(bf16[2,128,1024]{2,1,0:T(8,128)(2,1)} %bitcast.23), channel_id=1, source_target_pairs={{0,2},{1,3},{2,0},{3,1},{4,6},{5,7},{6,4},{7,5},{8,10},{9,11},{10,... | collective-permute-start | bytes 1572872 | tf_op jit(solution)/shard_map/ppermute | solution.py:317
  5.5 3.5 %collective-permute-start.2 = (bf16[2,16,1024]{2,1,0:T(8,128)(2,1)}, bf16[2,16,1024]{2,1,0:T(8,128)(2,1)S(1)}, u32[]{:S(2)}, u32[]{:S(2)}) collective-permute-start(bf16[2,16,1024]{2,1,0:T(8,128)(2,1)} %get-tuple-element.36.refs_0_.refs_4_.refs_8_.refs_12_), channel_id=1, source_target_pairs={{0,8},{4,12},{8,16},{12,20},{16,24},{20,28},{1,9},{5,13},{9,17},{1... | collective-permute-start | bytes 196616 | tf_op jit(solution)/shard_map/ppermute | solution.py:320
  9.0 3.3 %collective-permute-start.4 = (bf16[2,16,1024]{2,1,0:T(8,128)(2,1)}, bf16[2,16,1024]{2,1,0:T(8,128)(2,1)S(1)}, u32[]{:S(2)}, u32[]{:S(2)}) collective-permute-start(bf16[2,16,1024]{2,1,0:T(8,128)(2,1)} %get-tuple-element.36.refs_0_.refs_4_.refs_8_.refs_12_), channel_id=1, source_target_pairs={{0,24},{4,28},{1,25},{5,29},{2,26},{6,30},{3,27},{7,31}} | collective-permute-start | bytes 196616 | tf_op jit(solution)/shard_map/ppermute | solution.py:320
  12.3 1.5 %collective-permute-start.7 = (bf16[2,16,1024]{2,1,0:T(8,128)(2,1)}, bf16[2,16,1024]{2,1,0:T(8,128)(2,1)S(1)}, u32[]{:S(2)}, u32[]{:S(2)}) collective-permute-start(bf16[2,16,1024]{2,1,0:T(8,128)(2,1)} %get-tuple-element.36.refs_0_.refs_4_.refs_8_.refs_12_), channel_id=1, source_target_pairs={{0,6},{1,7},{2,4},{3,5},{4,2},{5,3},{6,0},{7,1},{8,14},{9,15},{10,... | collective-permute-start | bytes 196616 | tf_op jit(solution)/shard_map/ppermute | solution.py:317
  13.8 0.5 collective-permute-start.5
  14.3 4.0 %collective-permute-start.3 = (bf16[2,16,1024]{2,1,0:T(8,128)(2,1)}, bf16[2,16,1024]{2,1,0:T(8,128)(2,1)S(1)}, u32[]{:S(2)}, u32[]{:S(2)}) collective-permute-start(bf16[2,16,1024]{2,1,0:T(8,128)(2,1)} %get-tuple-element.36.refs_0_.refs_4_.refs_8_.refs_12_), channel_id=1, source_target_pairs={{0,16},{4,20},{8,24},{12,28},{1,17},{5,21},{9,25},{13,29},{2,18},{... | collective-permute-start | bytes 196616 | tf_op jit(solution)/shard_map/ppermute | solution.py:320
  18.4 0.5 collective-permute-start.8
  18.9 0.1 collective-permute-start.6
  19.0 1.5 %collective-permute-done.3 = bf16[2,16,1024]{2,1,0:T(8,128)(2,1)S(1)} collective-permute-done((bf16[2,16,1024]{2,1,0:T(8,128)(2,1)}, bf16[2,16,1024]{2,1,0:T(8,128)(2,1)S(1)}, u32[]{:S(2)}, u32[]{:S(2)}) %collective-permute-start.3) | collective-permute-done | bytes 65568 | tf_op jit(solution)/shard_map/ppermute | solution.py:320
  20.7 2.5 %collective-permute-start.14 = (bf16[3,2,16,1024]{3,2,1,0:T(8,128)(2,1)S(1)}, bf16[3,2,16,1024]{3,2,1,0:T(8,128)(2,1)S(1)}, u32[]{:S(2)}, u32[]{:S(2)}) collective-permute-start(bf16[3,2,16,1024]{3,2,1,0:T(8,128)(2,1)S(1)} %pad_maximum_fusion.refs_1_), channel_id=1, source_target_pairs={{0,6},{1,7},{2,4},{3,5},{4,2},{5,3},{6,0},{7,1},{8,14},{9,15},{10,... | collective-permute-start | bytes 589832 | tf_op jit(solution)/shard_map/ppermute | solution.py:317
  23.2 0.5 collective-permute-start.13
  23.7 0.5 collective-permute-start.10
  24.2 1.0 %copy-done = bf16[2,8,16,1024]{3,2,1,0:T(8,128)(2,1)S(1)} copy-done((bf16[2,8,16,1024]{3,2,1,0:T(8,128)(2,1)S(1)}, bf16[2,8,16,1024]{3,2,1,0:T(8,128)(2,1)}, u32[]{:S(2)}) %copy-start) | copy-done | bytes 524312
  25.3 4.6 %shard_map.85 = (f32[512,1024]{1,0:T(8,128)S(1)}, f32[512,1024]{1,0:T(8,128)S(1)}, f32[512,512]{1,0:T(8,128)S(1)}, bf16[512,1024]{1,0:T(8,128)(2,1)S(1)}, bf16[512,1024]{1,0:T(8,128)(2,1)S(1)}) custom-call(bf16[512,1024]{1,0:T(8,128)(2,1)} %q_hbm.1, bf16[512,1024]{1,0:T(8,128)(2,1)} %g_hbm.1, bf16[2,128,1024]{2,1,0:T(8,128)(2,1)S(1)} %bitcast.25, ...), custom_call_target="tpu_custom_call" | custom-call | flops 2147483648 | bytes 4194304 | tf_op jit(solution)/shard_map/pallas_call | solution.py:289
  29.9 3.2 %collective-permute-done.13.refs_9_ = bf16[3,2,16,1024]{3,2,1,0:T(8,128)(2,1)S(1)} collective-permute-done((bf16[3,2,16,1024]{3,2,1,0:T(8,128)(2,1)S(1)}, bf16[3,2,16,1024]{3,2,1,0:T(8,128)(2,1)S(1)}, u32[]{:S(2)}, u32[]{:S(2)}) %collective-permute-start.13) | collective-permute-done | bytes 196640 | tf_op jit(solution)/shard_map/ppermute | solution.py:317
  33.1 0.1 collective-permute-done.10.refs_3_
  33.2 0.5 collective-permute-start.12
  33.7 0.5 collective-permute-start.16
  34.2 1.2 %slice.30 = s32[1,1]{1,0:T(1,128)} slice(s32[8,128]{1,0:T(8,128)} %get-tuple-element.60), slice={[0:1], [0:1]} | slice | bytes 8 | tf_op jit(solution)/shard_map/slice | solution.py:399
  35.5 9.2 %shard_map.86 = (bf16[512,1024]{1,0:T(8,128)(2,1)}, f32[512,1024]{1,0:T(8,128)S(1)}, f32[512,1024]{1,0:T(8,128)S(1)}, f32[512,1024]{1,0:T(8,128)S(1)}, bf16[4,2,...) custom-call(bf16[512,1024]{1,0:T(8,128)(2,1)S(1)} %get-tuple-element.39.q_ref, ...), custom_call_target="tpu_custom_call" | custom-call | flops 5368709120 | bytes 8388608 | tf_op jit(solution)/shard_map/pallas_call | solution.py:289
  44.7 1.5 %collective-permute-start.17 = (bf16[4,2,16,1024]{3,2,1,0:T(8,128)(2,1)S(1)}, bf16[4,2,16,1024]{3,2,1,0:T(8,128)(2,1)S(1)}, u32[]{:S(2)}, u32[]{:S(2)}) collective-permute-start(bf16[4,2,16,1024]{3,2,1,0:T(8,128)(2,1)S(1)} %get-tuple-element.57), channel_id=1, source_target_pairs={{0,4},{1,5},{2,6},{3,7},{4,0},{5,1},{6,2},{7,3},{8,12},{9,13},{10,... | collective-permute-start | bytes 786440 | tf_op jit(solution)/shard_map/ppermute | solution.py:317
  46.2 5.8 %shard_map.87 = (bf16[512,1024]{1,0:T(8,128)(2,1)}, f32[128,1024]{1,0:T(8,128)S(1)}, f32[128,1024]{1,0:T(8,128)S(1)}) custom-call(f32[512,512]{1,0:T(8,128)S(1)} %get-tuple-element.52.bias_ref, bf16[512,1024]{1,0:T(8,128)(2,1)S(1)} %get-tuple-element.39.q_ref, bf16[512,1024]{1,0:T(8,128)(2,1)S(1)} %get-tuple-element.40.g_ref, ...), custom_call_target="tpu_custom_call" | custom-call | flops 4294967296 | bytes 11534336 | tf_op jit(solution)/shard_map/pallas_call | solution.py:289
  52.0 1.1 %collective-permute-done.17 = bf16[4,2,16,1024]{3,2,1,0:T(8,128)(2,1)S(1)} collective-permute-done((bf16[4,2,16,1024]{3,2,1,0:T(8,128)(2,1)S(1)}, bf16[4,2,16,1024]{3,2,1,0:T(8,128)(2,1)S(1)}, u32[]{:S(2)}, u32[]{:S(2)}) %collective-permute-start.17) | collective-permute-done | bytes 262176 | tf_op jit(solution)/shard_map/ppermute | solution.py:317
  53.2 1.3 %collective-permute-start.18 = (bf16[2,16,1024]{2,1,0:T(8,128)(2,1)S(1)}, bf16[2,16,1024]{2,1,0:T(8,128)(2,1)S(1)}, u32[]{:S(2)}, u32[]{:S(2)}) collective-permute-start(bf16[2,16,1024]{2,1,0:T(8,128)(2,1)S(1)} %get-tuple-element.64), channel_id=1, source_target_pairs={{8,0},{12,4},{16,8},{20,12},{24,16},{28,20},{9,1},{13,5},{17,9},{2... | collective-permute-start | bytes 196616 | tf_op jit(solution)/shard_map/ppermute | solution.py:325
  54.5 1.3 %collective-permute-start.20 = (bf16[2,16,1024]{2,1,0:T(8,128)(2,1)S(1)}, bf16[2,16,1024]{2,1,0:T(8,128)(2,1)S(1)}, u32[]{:S(2)}, u32[]{:S(2)}) collective-permute-start(bf16[2,16,1024]{2,1,0:T(8,128)(2,1)S(1)} %get-tuple-element.65), channel_id=1, source_target_pairs={{24,0},{28,4},{25,1},{29,5},{26,2},{30,6},{27,3},{31,7}} | collective-permute-start | bytes 196616 | tf_op jit(solution)/shard_map/ppermute | solution.py:325
  55.8 1.3 %collective-permute-start.19 = (bf16[2,16,1024]{2,1,0:T(8,128)(2,1)S(1)}, bf16[2,16,1024]{2,1,0:T(8,128)(2,1)S(1)}, u32[]{:S(2)}, u32[]{:S(2)}) collective-permute-start(bf16[2,16,1024]{2,1,0:T(8,128)(2,1)S(1)} %get-tuple-element.66), channel_id=1, source_target_pairs={{16,0},{20,4},{24,8},{28,12},{17,1},{21,5},{25,9},{29,13},{18,2},{... | collective-permute-start | bytes 196616 | tf_op jit(solution)/shard_map/ppermute | solution.py:325
  57.1 0.6 iota_compare_fusion
  57.7 1.7 %collective-permute-done.18 = bf16[2,16,1024]{2,1,0:T(8,128)(2,1)S(1)} collective-permute-done((bf16[2,16,1024]{2,1,0:T(8,128)(2,1)S(1)}, bf16[2,16,1024]{2,1,0:T(8,128)(2,1)S(1)}, u32[]{:S(2)}, u32[]{:S(2)}) %collective-permute-start.18) | collective-permute-done | bytes 65568 | tf_op jit(solution)/shard_map/ppermute | solution.py:325
  59.4 4.4 %collective-permute-done.20 = bf16[2,16,1024]{2,1,0:T(8,128)(2,1)S(1)} collective-permute-done((bf16[2,16,1024]{2,1,0:T(8,128)(2,1)S(1)}, bf16[2,16,1024]{2,1,0:T(8,128)(2,1)S(1)}, u32[]{:S(2)}, u32[]{:S(2)}) %collective-permute-start.20) | collective-permute-done | bytes 65568 | tf_op jit(solution)/shard_map/ppermute | solution.py:325
  63.8 1.2 %collective-permute-done.19 = bf16[2,16,1024]{2,1,0:T(8,128)(2,1)S(1)} collective-permute-done((bf16[2,16,1024]{2,1,0:T(8,128)(2,1)S(1)}, bf16[2,16,1024]{2,1,0:T(8,128)(2,1)S(1)}, u32[]{:S(2)}, u32[]{:S(2)}) %collective-permute-start.19) | collective-permute-done | bytes 65568 | tf_op jit(solution)/shard_map/ppermute | solution.py:325
  65.1 1.0 %add_convert_fusion = (bf16[8,16,1024]{2,1,0:T(8,128)(2,1)}, bf16[8,16,1024]{2,1,0:T(8,128)(2,1)}) fusion(f32[8,16,1024]{2,1,0:T(8,128)S(1)} %bitcast.22, f32[16,1024]{1,0:T(8,128)S(1)} %get-tuple-element.67, pred[8]{0:T(512)(128)(4,1)S(1)} %iota_compare_fusion, f32[8,16,1024]{2,1,0:T(8,128)S(1)} %bitcast.21, f32[16,1024]{1,0:T(8,128)S(1)} %get-tuple-element.68), kind=kLoop, calls=%fused_computation | loop fusion | flops 786432 | bytes 1703944 | tf_op jit(solution)/shard_map/convert_element_type | solution.py:403
  (27 shorter events, 0.3 us)
Async XLA Ops:
  2.5 18.0 %collective-permute-start.1 = (bf16[2,128,1024]{2,1,0:T(8,128)(2,1)}, bf16[2,128,1024]{2,1,0:T(8,128)(2,1)S(1)}, u32[]{:S(2)}, u32[]{:S(2)}) collective-permute-start(bf16[2,128,1024]{2,1,0:T(8,128)(2,1)} %bitcast.23), channel_id=1, source_target_pairs={{0,2},{1,3},{2,0},{3,1},{4,6},{5,7},{6,4},{7,5},{8,10},{9,11},{10,... | collective-permute-start | bytes 1572872 | tf_op jit(solution)/shard_map/ppermute | solution.py:317
  5.5 6.8 %collective-permute-start.2 = (bf16[2,16,1024]{2,1,0:T(8,128)(2,1)}, bf16[2,16,1024]{2,1,0:T(8,128)(2,1)S(1)}, u32[]{:S(2)}, u32[]{:S(2)}) collective-permute-start(bf16[2,16,1024]{2,1,0:T(8,128)(2,1)} %get-tuple-element.36.refs_0_.refs_4_.refs_8_.refs_12_), channel_id=1, source_target_pairs={{0,8},{4,12},{8,16},{12,20},{16,24},{20,28},{1,9},{5,13},{9,17},{1... | collective-permute-start | bytes 196616 | tf_op jit(solution)/shard_map/ppermute | solution.py:320
  9.0 9.3 %collective-permute-start.4 = (bf16[2,16,1024]{2,1,0:T(8,128)(2,1)}, bf16[2,16,1024]{2,1,0:T(8,128)(2,1)S(1)}, u32[]{:S(2)}, u32[]{:S(2)}) collective-permute-start(bf16[2,16,1024]{2,1,0:T(8,128)(2,1)} %get-tuple-element.36.refs_0_.refs_4_.refs_8_.refs_12_), channel_id=1, source_target_pairs={{0,24},{4,28},{1,25},{5,29},{2,26},{6,30},{3,27},{7,31}} | collective-permute-start | bytes 196616 | tf_op jit(solution)/shard_map/ppermute | solution.py:320
  12.3 6.1 %collective-permute-start.7 = (bf16[2,16,1024]{2,1,0:T(8,128)(2,1)}, bf16[2,16,1024]{2,1,0:T(8,128)(2,1)S(1)}, u32[]{:S(2)}, u32[]{:S(2)}) collective-permute-start(bf16[2,16,1024]{2,1,0:T(8,128)(2,1)} %get-tuple-element.36.refs_0_.refs_4_.refs_8_.refs_12_), channel_id=1, source_target_pairs={{0,6},{1,7},{2,4},{3,5},{4,2},{5,3},{6,0},{7,1},{8,14},{9,15},{10,... | collective-permute-start | bytes 196616 | tf_op jit(solution)/shard_map/ppermute | solution.py:317
  13.8 5.1 %collective-permute-start.5 = (bf16[2,16,1024]{2,1,0:T(8,128)(2,1)}, bf16[2,16,1024]{2,1,0:T(8,128)(2,1)S(1)}, u32[]{:S(2)}, u32[]{:S(2)}) collective-permute-start(bf16[2,16,1024]{2,1,0:T(8,128)(2,1)} %get-tuple-element.36.refs_0_.refs_4_.refs_8_.refs_12_), channel_id=1, source_target_pairs={{0,4},{1,5},{2,6},{3,7},{4,0},{5,1},{6,2},{7,3},{8,12},{9,13},{10,... | collective-permute-start | bytes 196616 | tf_op jit(solution)/shard_map/ppermute | solution.py:317
  14.3 6.2 %collective-permute-start.3 = (bf16[2,16,1024]{2,1,0:T(8,128)(2,1)}, bf16[2,16,1024]{2,1,0:T(8,128)(2,1)S(1)}, u32[]{:S(2)}, u32[]{:S(2)}) collective-permute-start(bf16[2,16,1024]{2,1,0:T(8,128)(2,1)} %get-tuple-element.36.refs_0_.refs_4_.refs_8_.refs_12_), channel_id=1, source_target_pairs={{0,16},{4,20},{8,24},{12,28},{1,17},{5,21},{9,25},{13,29},{2,18},{... | collective-permute-start | bytes 196616 | tf_op jit(solution)/shard_map/ppermute | solution.py:320
  18.3 5.9 %collective-permute-start = (bf16[2,128,1024]{2,1,0:T(8,128)(2,1)}, bf16[2,128,1024]{2,1,0:T(8,128)(2,1)S(1)}, u32[]{:S(2)}, u32[]{:S(2)}) collective-permute-start(bf16[2,128,1024]{2,1,0:T(8,128)(2,1)} %bitcast.24), channel_id=1, source_target_pairs={{0,1},{1,0},{2,3},{3,2},{4,5},{5,4},{6,7},{7,6},{8,9},{9,8},{10,11... | collective-permute-start | bytes 1572872 | tf_op jit(solution)/shard_map/ppermute | solution.py:317
  18.4 2.1 %collective-permute-start.8 = (bf16[2,16,1024]{2,1,0:T(8,128)(2,1)S(1)}, bf16[2,16,1024]{2,1,0:T(8,128)(2,1)S(1)}, u32[]{:S(2)}, u32[]{:S(2)}) collective-permute-start(bf16[2,16,1024]{2,1,0:T(8,128)(2,1)S(1)} %collective-permute-done.7.refs_10_), channel_id=1, source_target_pairs={{0,1},{1,0},{2,3},{3,2},{4,5},{5,4},{6,7},{7,6},{8,9},{9,8},{10,11... | collective-permute-start | bytes 196616 | tf_op jit(solution)/shard_map/ppermute | solution.py:317
  18.9 1.6 %collective-permute-start.6 = (bf16[2,16,1024]{2,1,0:T(8,128)(2,1)S(1)}, bf16[2,16,1024]{2,1,0:T(8,128)(2,1)S(1)}, u32[]{:S(2)}, u32[]{:S(2)}) collective-permute-start(bf16[2,16,1024]{2,1,0:T(8,128)(2,1)S(1)} %collective-permute-done.5.refs_2_), channel_id=1, source_target_pairs={{0,1},{1,0},{2,3},{3,2},{4,5},{5,4},{6,7},{7,6},{8,9},{9,8},{10,11... | collective-permute-start | bytes 196616 | tf_op jit(solution)/shard_map/ppermute | solution.py:317
  20.5 15.0 %copy-start.2 = (bf16[2,16,1024]{2,1,0:T(8,128)(2,1)S(1)}, bf16[2,16,1024]{2,1,0:T(8,128)(2,1)}, u32[]{:S(2)}) copy-start(bf16[2,16,1024]{2,1,0:T(8,128)(2,1)} %get-tuple-element.36.refs_0_.refs_4_.refs_8_.refs_12_) | copy-start | bytes 196612
  20.6 3.6 %collective-permute-start.9 = (bf16[2,128,1024]{2,1,0:T(8,128)(2,1)S(1)}, bf16[2,128,1024]{2,1,0:T(8,128)(2,1)S(1)}, u32[]{:S(2)}, u32[]{:S(2)}) collective-permute-start(bf16[2,128,1024]{2,1,0:T(8,128)(2,1)S(1)} %collective-permute-done.1.refs_2_), channel_id=1, source_target_pairs={{0,1},{1,0},{2,3},{3,2},{4,5},{5,4},{6,7},{7,6},{8,9},{9,8},{10,11... | collective-permute-start | bytes 1572872 | tf_op jit(solution)/shard_map/ppermute | solution.py:317
  20.7 9.2 %collective-permute-start.14 = (bf16[3,2,16,1024]{3,2,1,0:T(8,128)(2,1)S(1)}, bf16[3,2,16,1024]{3,2,1,0:T(8,128)(2,1)S(1)}, u32[]{:S(2)}, u32[]{:S(2)}) collective-permute-start(bf16[3,2,16,1024]{3,2,1,0:T(8,128)(2,1)S(1)} %pad_maximum_fusion.refs_1_), channel_id=1, source_target_pairs={{0,6},{1,7},{2,4},{3,5},{4,2},{5,3},{6,0},{7,1},{8,14},{9,15},{10,... | collective-permute-start | bytes 589832 | tf_op jit(solution)/shard_map/ppermute | solution.py:317
  23.2 9.9 %collective-permute-start.13 = (bf16[3,2,16,1024]{3,2,1,0:T(8,128)(2,1)S(1)}, bf16[3,2,16,1024]{3,2,1,0:T(8,128)(2,1)S(1)}, u32[]{:S(2)}, u32[]{:S(2)}) collective-permute-start(bf16[3,2,16,1024]{3,2,1,0:T(8,128)(2,1)S(1)} %pad_maximum_fusion.refs_1_), channel_id=1, source_target_pairs={{0,2},{1,3},{2,0},{3,1},{4,6},{5,7},{6,4},{7,5},{8,10},{9,11},{10,... | collective-permute-start | bytes 589832 | tf_op jit(solution)/shard_map/ppermute | solution.py:317
  23.7 9.5 %collective-permute-start.10 = (bf16[3,2,16,1024]{3,2,1,0:T(8,128)(2,1)S(1)}, bf16[3,2,16,1024]{3,2,1,0:T(8,128)(2,1)S(1)}, u32[]{:S(2)}, u32[]{:S(2)}) collective-permute-start(bf16[3,2,16,1024]{3,2,1,0:T(8,128)(2,1)S(1)} %pad_maximum_fusion.refs_1_), channel_id=1, source_target_pairs={{0,4},{1,5},{2,6},{3,7},{4,0},{5,1},{6,2},{7,3},{8,12},{9,13},{10,... | collective-permute-start | bytes 589832 | tf_op jit(solution)/shard_map/ppermute | solution.py:317
  24.2 1.0 %copy-start = (bf16[2,8,16,1024]{3,2,1,0:T(8,128)(2,1)S(1)}, bf16[2,8,16,1024]{3,2,1,0:T(8,128)(2,1)}, u32[]{:S(2)}) copy-start(bf16[2,8,16,1024]{3,2,1,0:T(8,128)(2,1)} %get-tuple-element.34) | copy-start | bytes 1572868
  33.2 2.3 %collective-permute-start.11 = (bf16[3,2,16,1024]{3,2,1,0:T(8,128)(2,1)S(1)}, bf16[3,2,16,1024]{3,2,1,0:T(8,128)(2,1)S(1)}, u32[]{:S(2)}, u32[]{:S(2)}) collective-permute-start(bf16[3,2,16,1024]{3,2,1,0:T(8,128)(2,1)S(1)} %pad_maximum_fusion.refs_1_), channel_id=1, source_target_pairs={{0,1},{1,0},{2,3},{3,2},{4,5},{5,4},{6,7},{7,6},{8,9},{9,8},{10,11... | collective-permute-start | bytes 589832 | tf_op jit(solution)/shard_map/ppermute | solution.py:317
  33.2 2.3 %collective-permute-start.12 = (bf16[3,2,16,1024]{3,2,1,0:T(8,128)(2,1)S(1)}, bf16[3,2,16,1024]{3,2,1,0:T(8,128)(2,1)S(1)}, u32[]{:S(2)}, u32[]{:S(2)}) collective-permute-start(bf16[3,2,16,1024]{3,2,1,0:T(8,128)(2,1)S(1)} %collective-permute-done.10.refs_3_), channel_id=1, source_target_pairs={{0,1},{1,0},{2,3},{3,2},{4,5},{5,4},{6,7},{7,6},{8,9},{9,8},{10,11... | collective-permute-start | bytes 589832 | tf_op jit(solution)/shard_map/ppermute | solution.py:317
  33.7 1.8 %collective-permute-start.15 = (bf16[3,2,16,1024]{3,2,1,0:T(8,128)(2,1)S(1)}, bf16[3,2,16,1024]{3,2,1,0:T(8,128)(2,1)S(1)}, u32[]{:S(2)}, u32[]{:S(2)}) collective-permute-start(bf16[3,2,16,1024]{3,2,1,0:T(8,128)(2,1)S(1)} %collective-permute-done.13.refs_9_), channel_id=1, source_target_pairs={{0,1},{1,0},{2,3},{3,2},{4,5},{5,4},{6,7},{7,6},{8,9},{9,8},{10,11... | collective-permute-start | bytes 589832 | tf_op jit(solution)/shard_map/ppermute | solution.py:317
  33.7 1.8 %collective-permute-start.16 = (bf16[3,2,16,1024]{3,2,1,0:T(8,128)(2,1)S(1)}, bf16[3,2,16,1024]{3,2,1,0:T(8,128)(2,1)S(1)}, u32[]{:S(2)}, u32[]{:S(2)}) collective-permute-start(bf16[3,2,16,1024]{3,2,1,0:T(8,128)(2,1)S(1)} %collective-permute-done.14.refs_11_), channel_id=1, source_target_pairs={{0,1},{1,0},{2,3},{3,2},{4,5},{5,4},{6,7},{7,6},{8,9},{9,8},{10,11... | collective-permute-start | bytes 589832 | tf_op jit(solution)/shard_map/ppermute | solution.py:317
  35.5 10.7 %copy-start.1 = (bf16[2,8,16,1024]{3,2,1,0:T(8,128)(2,1)S(1)}, bf16[2,8,16,1024]{3,2,1,0:T(8,128)(2,1)}, u32[]{:S(2)}) copy-start(bf16[2,8,16,1024]{3,2,1,0:T(8,128)(2,1)} %get-tuple-element.34) | copy-start | bytes 1572868
  44.7 8.4 %collective-permute-start.17 = (bf16[4,2,16,1024]{3,2,1,0:T(8,128)(2,1)S(1)}, bf16[4,2,16,1024]{3,2,1,0:T(8,128)(2,1)S(1)}, u32[]{:S(2)}, u32[]{:S(2)}) collective-permute-start(bf16[4,2,16,1024]{3,2,1,0:T(8,128)(2,1)S(1)} %get-tuple-element.57), channel_id=1, source_target_pairs={{0,4},{1,5},{2,6},{3,7},{4,0},{5,1},{6,2},{7,3},{8,12},{9,13},{10,... | collective-permute-start | bytes 786440 | tf_op jit(solution)/shard_map/ppermute | solution.py:317
  53.2 6.2 %collective-permute-start.18 = (bf16[2,16,1024]{2,1,0:T(8,128)(2,1)S(1)}, bf16[2,16,1024]{2,1,0:T(8,128)(2,1)S(1)}, u32[]{:S(2)}, u32[]{:S(2)}) collective-permute-start(bf16[2,16,1024]{2,1,0:T(8,128)(2,1)S(1)} %get-tuple-element.64), channel_id=1, source_target_pairs={{8,0},{12,4},{16,8},{20,12},{24,16},{28,20},{9,1},{13,5},{17,9},{2... | collective-permute-start | bytes 196616 | tf_op jit(solution)/shard_map/ppermute | solution.py:325
  54.5 9.3 %collective-permute-start.20 = (bf16[2,16,1024]{2,1,0:T(8,128)(2,1)S(1)}, bf16[2,16,1024]{2,1,0:T(8,128)(2,1)S(1)}, u32[]{:S(2)}, u32[]{:S(2)}) collective-permute-start(bf16[2,16,1024]{2,1,0:T(8,128)(2,1)S(1)} %get-tuple-element.65), channel_id=1, source_target_pairs={{24,0},{28,4},{25,1},{29,5},{26,2},{30,6},{27,3},{31,7}} | collective-permute-start | bytes 196616 | tf_op jit(solution)/shard_map/ppermute | solution.py:325
  55.8 9.3 %collective-permute-start.19 = (bf16[2,16,1024]{2,1,0:T(8,128)(2,1)S(1)}, bf16[2,16,1024]{2,1,0:T(8,128)(2,1)S(1)}, u32[]{:S(2)}, u32[]{:S(2)}) collective-permute-start(bf16[2,16,1024]{2,1,0:T(8,128)(2,1)S(1)} %get-tuple-element.66), channel_id=1, source_target_pairs={{16,0},{20,4},{24,8},{28,12},{17,1},{21,5},{25,9},{29,13},{18,2},{... | collective-permute-start | bytes 196616 | tf_op jit(solution)/shard_map/ppermute | solution.py:325

commit v5 on v4

--- a/solution.py
+++ b/solution.py
@@ -10,11 +10,13 @@
 
 HEADS = 8
 COLUMNS = 2
+CORES = 2
 GROUP = 2
 HIDDEN = -1e30
 NT = (((1,), (1,)), ((), ()))
 NN = (((1,), (0,)), ((), ()))
 TN = (((0,), (0,)), ((), ()))
+IN_HBM = pl.BlockSpec(memory_space=pltpu.HBM)
 WHOLE = pl.BlockSpec(memory_space=pltpu.VMEM)
 LIMIT = pltpu.CompilerParams(vmem_limit_bytes=20 * 1024 * 1024)
 
@@ -31,9 +33,20 @@
     return math.log2(math.e) / math.sqrt(head_dim)
 
 
-def pick_kernel(table_ref, keys_ref, values_ref, pair_ref, both_ref, block_ref):
+def pick_kernel(table_hbm, keys_hbm, values_hbm, mine_ref, theirs_ref, pair_ref, sent_ref, mask_ref, table_ref, sems):
     window = lax.axis_index("seq")
-    blocks = keys_ref.shape[0]
+    core = lax.axis_index("kv") % CORES
+    blocks, _, half = mask_ref.shape
+    copies = [pltpu.make_async_copy(table_hbm, table_ref, sems.at[0])]
+    for which, ref in enumerate((keys_hbm, values_hbm)):
+        for side, out_ref in enumerate((mine_ref, theirs_ref)):
+            cols = pl.ds(pl.multiple_of((core ^ side) * half, half), half)
+            copies.append(
+                pltpu.make_async_copy(ref.at[:, :, cols], out_ref.at[which], sems.at[len(copies)])
+            )
+    for copy in copies:
+        copy.start()
+    copies[0].wait()
     pick = jnp.minimum(window, lax.axis_size("seq") - 2)
     entry = lax.broadcasted_iota(jnp.int32, table_ref.shape, 0)
     row = lax.broadcasted_iota(jnp.int32, table_ref.shape, 1)
@@ -41,27 +54,78 @@
     named = jnp.where(here, table_ref[...].astype(jnp.float32), -1.0)
     named = jnp.max(jnp.max(named, axis=1, keepdims=True), axis=0, keepdims=True)
     block = jnp.clip(named - (window * blocks).astype(jnp.float32), 0.0, blocks - 1.0)
-    block_ref[...] = jnp.broadcast_to(block, block_ref.shape).astype(jnp.int32)
-    for which, ref in enumerate((keys_ref, values_ref)):
-        chosen = ref[0].astype(jnp.float32)
-        for b in range(1, blocks):
-            chosen = jnp.where(block == b, ref[b].astype(jnp.float32), chosen)
-        pair_ref[which] = chosen.astype(pair_ref.dtype)
-        both_ref[which] = ref[...]
+    block = jnp.broadcast_to(block, mask_ref.shape[1:])
+    for b in range(blocks):
+        mask_ref[b] = jnp.where(block == b, 1.0, 0.0)
+    for copy in copies[1:]:
+        copy.wait()
+    for ref, out_ref in ((mine_ref, pair_ref), (theirs_ref, sent_ref)):
+        for which in range(2):
+            chosen = ref[which, 0].astype(jnp.float32)
+            for b in range(1, blocks):
+                chosen = jnp.where(block == b, ref[which, b].astype(jnp.float32), chosen)
+            out_ref[which] = chosen.astype(out_ref.dtype)
 
 
 def pick_pair(table, keys, values):
-    _, part_tok, feat_width = keys.shape
+    blocks, part_tok, feat_width = keys.shape
+    half = feat_width // CORES
+    operands = [pltpu.with_memory_space_constraint(a, pltpu.HBM) for a in (table, keys, values)]
     return pl.pallas_call(
         pick_kernel,
-        in_specs=[WHOLE] * 3,
-        out_specs=[WHOLE] * 3,
-        out_shape=[
-            jax.ShapeDtypeStruct((2, part_tok, feat_width), keys.dtype),
-            jax.ShapeDtypeStruct((2,) + keys.shape, keys.dtype),
-            jax.ShapeDtypeStruct((8, 128), jnp.int32),
-        ],
-    )(table, keys, values)
+        in_specs=[IN_HBM] * 3,
+        out_specs=[WHOLE] * 5,
+        out_shape=[pltpu.VMEM((2, blocks, part_tok, half), keys.dtype)] * 2
+        + [pltpu.VMEM((2, part_tok, half), keys.dtype)] * 2
+        + [pltpu.VMEM((blocks, part_tok, half), jnp.float32)],
+        scratch_shapes=[pltpu.VMEM(table.shape, table.dtype), pltpu.SemaphoreType.DMA((5,))],
+    )(*operands)
+
+
+def join_kernel(*refs):
+    sems = refs[-1]
+    count = (len(refs) - 1) // 3
+    core = lax.axis_index("kv") % CORES
+    copies = []
+    for i in range(count):
+        out_ref = refs[2 * count + i]
+        half = refs[2 * i].shape[1]
+        for side in range(CORES):
+            cols = pl.ds(pl.multiple_of((core ^ side) * half, half), half)
+            copies.append(
+                pltpu.make_async_copy(refs[2 * i + side], out_ref.at[:, cols], sems.at[len(copies)])
+            )
+    for copy in copies:
+        copy.start()
+    for copy in copies:
+        copy.wait()
+
+
+def join(pairs):
+    rows, half = pairs[0][0].shape
+    operands = [pltpu.with_memory_space_constraint(a, pltpu.VMEM) for pair in pairs for a in pair]
+    return pl.pallas_call(
+        join_kernel,
+        in_specs=[WHOLE] * len(operands),
+        out_specs=[IN_HBM] * len(pairs),
+        out_shape=[pltpu.HBM((rows, half * CORES), pairs[0][0].dtype)] * len(pairs),
+        scratch_shapes=[pltpu.SemaphoreType.DMA((len(operands),))],
+    )(*operands)
+
+
+def finish_kernel(mask_ref, gk_ref, gv_ref, near_ref, far_ref, *refs):
+    arrived = refs[:-2]
+    core = lax.axis_index("kv") % CORES
+    half = mask_ref.shape[-1]
+    mine = pl.ds(pl.multiple_of(core * half, half), half)
+    theirs = pl.ds(pl.multiple_of((core ^ 1) * half, half), half)
+    mask = mask_ref[...]
+    for which, (own_ref, out_ref) in enumerate(zip((gk_ref, gv_ref), refs[-2:])):
+        extra = sum(ref[0, which].astype(jnp.float32) for ref in arrived)
+        out_ref[:, :, mine] = (own_ref[...] + mask * extra[None]).astype(out_ref.dtype)
+        near = near_ref[which].astype(jnp.float32)
+        extra = far_ref[which].astype(jnp.float32)
+        out_ref[:, :, theirs] = (near + mask * extra[None]).astype(out_ref.dtype)
 
 
 def near_tiles(rows, near):
@@ -83,8 +147,7 @@
             )
 
 
-def head_columns(head, feat_width):
-    head_dim = feat_width // HEADS
+def head_columns(head, head_dim):
     return pl.ds(pl.multiple_of(head * head_dim, head_dim), head_dim)
 
 
@@ -92,32 +155,31 @@
     return jnp.concatenate([ref[which, :used, cols] for ref in parts], axis=0)
 
 
-def near_forward_kernel(members, blk_len, part_tok, q_hbm, g_hbm, *refs):
+def near_forward_kernel(members, blk_len, part_tok, head_dim, q_hbm, g_hbm, *refs):
     parts = refs[:members]
     out_ref, stat_ref, bias_ref, q_ref, g_ref, sems = refs[members:]
-    rows, feat_width = q_ref.shape
-    head_dim = feat_width // HEADS
+    rows, half = q_ref.shape
     near = parts[0].shape[1]
-    slab = feat_width * GROUP // HEADS
-    copies = [
-        pltpu.make_async_copy(q_hbm.at[:, pl.ds(c, slab)], q_ref.at[:, pl.ds(c, slab)], sems.at[i])
-        for i, c in enumerate(range(0, feat_width, slab))
-    ]
-    copies.append(pltpu.make_async_copy(g_hbm, g_ref, sems.at[HEADS // GROUP]))
-    for copy in copies:
-        copy.start()
+    slab = GROUP * head_dim
+    core = lax.axis_index("kv") % CORES
+
+    def fetch(group):
+        there = pl.ds(pl.multiple_of(core * half + group * slab, slab), slab)
+        here = pl.ds(pl.multiple_of(group * slab, slab), slab)
+        return pltpu.make_async_copy(q_hbm.at[:, there], q_ref.at[:, here], sems.at[group])
+
+    there = pl.ds(pl.multiple_of(core * half, half), half)
+    last = pltpu.make_async_copy(g_hbm.at[:, there], g_ref, sems.at[half // slab])
+    for group in range(half // slab):
+        fetch(group).start()
+    last.start()
     fill_mask(members, near, blk_len, part_tok, bias_ref)
-    copies[0].wait()
-
-    @pl.loop(0, HEADS // GROUP)
+
+    @pl.loop(0, half // slab)
     def _(group):
-        @pl.when(group > 0)
-        def _():
-            cols = pl.ds(pl.multiple_of(group * slab, slab), slab)
-            pltpu.make_async_copy(q_hbm.at[:, cols], q_ref.at[:, cols], sems.at[group]).wait()
-
+        fetch(group).wait()
         units = [
-            (head_columns(group * GROUP + i, feat_width), pl.ds(start, count), used)
+            (head_columns(group * GROUP + i, head_dim), pl.ds(start, count), used)
             for i in range(GROUP)
             for start, count, used in near_tiles(rows, near)
         ]
@@ -138,33 +200,32 @@
             stat_ref[here, cols] = jnp.broadcast_to(level, summed.shape)
             out_ref[here, cols] = summed * (1.0 / total)
 
-    copies[-1].wait()
+    last.wait()
 
 
 def far_rows(parts, which, cols):
     rows = []
     for pair_ref, column_ref in zip(parts[0::2], parts[1::2]):
-        steps, _, part_tok, _ = column_ref.shape
-        rows.append(pair_ref[which, :, cols])
-        rows.append(column_ref[:, which, :, cols].reshape(steps * part_tok, cols.size))
+        steps, cores, _, part_tok, _ = column_ref.shape
+        rows.append(pair_ref[:, which, :, cols].reshape(cores * part_tok, cols.size))
+        rows.append(column_ref[:, :, which, :, cols].reshape(steps * cores * part_tok, cols.size))
     return jnp.concatenate(rows, axis=0)
 
 
-def far_kernel(members, tile, heads, batch, q_ref, g_ref, sum_ref, stat_ref, *refs):
-    parts = refs[: 2 * COLUMNS * members]
-    att_ref, gq_ref, level_ref, drift_ref, *grad_refs = refs[2 * COLUMNS * members :]
-    rows, feat_width = q_ref.shape
-    head_dim = feat_width // HEADS
-    steps, _, part_tok, _ = grad_refs[0].shape
-    span = steps * part_tok
+def far_kernel(groups, head_dim, tile, heads, batch, q_ref, g_ref, sum_ref, stat_ref, *refs):
+    parts = refs[: 2 * COLUMNS * groups]
+    att_ref, gq_ref, level_ref, drift_ref, *grad_refs = refs[2 * COLUMNS * groups :]
+    rows, half = q_ref.shape
+    steps, cores, _, part_tok, _ = grad_refs[0].shape
+    span = steps * cores * part_tok
     width = COLUMNS * span
     score_scale = 1.0 / math.sqrt(head_dim)
     window = lax.axis_index("seq")
     level, side = window // COLUMNS, window % COLUMNS
-    step = lax.broadcasted_iota(jnp.int32, (1, span), 1) >> (part_tok.bit_length() - 1)
+    step = lax.broadcasted_iota(jnp.int32, (1, span), 1) >> ((cores * part_tok).bit_length() - 1)
     valid = [(step >= 1) & (step <= level), (step >= 1 - side) & (step <= level)]
-    bias = jnp.concatenate([jnp.where(ok, 0.0, HIDDEN) for ok in valid] * members, axis=1)
-    total_width = members * width
+    bias = jnp.concatenate([jnp.where(ok, 0.0, HIDDEN) for ok in valid] * groups, axis=1)
+    total_width = groups * width
 
     def work(units, keys, values, key_grads, value_grads):
         raws = [
@@ -217,9 +278,9 @@
             key_grads[i].append(dot(own_scores[u], q_ref[here, cols], TN))
             value_grads[i].append(dot(own_probs[u], g_ref[here, cols], TN))
 
-    @pl.loop(0, HEADS // heads)
+    @pl.loop(0, half // (heads * head_dim))
     def _(group):
-        columns = [head_columns(group * heads + i, feat_width) for i in range(heads)]
+        columns = [head_columns(group * heads + i, head_dim) for i in range(heads)]
         units = [
             (i, cols, pl.ds(r, tile)) for i, cols in enumerate(columns) for r in range(0, rows, tile)
         ]
@@ -233,23 +294,22 @@
                 total = functools.reduce(lambda a, b: a + b, terms).astype(jnp.bfloat16)
                 for c, ref in enumerate(grad_refs):
                     piece = total[c * span : (c + 1) * span]
-                    ref[:, which, :, cols] = piece.reshape(steps, part_tok, head_dim)
-
-
-def near_backward_kernel(members, bias_ref, q_ref, g_ref, level_ref, drift_ref, far_gq_ref, *refs):
+                    ref[:, :, which, :, cols] = piece.reshape(steps, cores, part_tok, head_dim)
+
+
+def near_backward_kernel(members, head_dim, bias_ref, q_ref, g_ref, level_ref, drift_ref, far_gq_ref, *refs):
     parts = refs[:members]
-    gq_ref, gk_ref, gv_ref = refs[members:]
-    rows, feat_width = q_ref.shape
-    head_dim = feat_width // HEADS
+    gq_ref, gk_ref, gv_ref, sent_ref = refs[members:]
+    rows, half = q_ref.shape
     near = parts[0].shape[1]
     score_scale = 1.0 / math.sqrt(head_dim)
 
-    @pl.loop(0, HEADS // GROUP)
+    @pl.loop(0, half // (GROUP * head_dim))
     def _(group):
         units = [
-            (head_columns(group * GROUP + i, feat_width), pl.ds(start, count), used)
+            (head_columns(group * GROUP + i, head_dim), pl.ds(start, count), used)
             for i in range(GROUP)
-            for start, count, used in reversed(near_tiles(rows, near))
+            for start, count, used in near_tiles(rows, near)
         ]
         keys = [near_rows(parts, 0, used, cols) for cols, here, used in units]
         values = [near_rows(parts, 1, used, cols) for cols, here, used in units]
@@ -273,15 +333,24 @@
             gq_ref[here, cols] = (
                 dot(part.astype(jnp.bfloat16), key, NN) * score_scale + far_gq_ref[here, cols]
             ).astype(jnp.bfloat16)
+        grads = []
         for (cols, here, used), part, prob in zip(units, moved, probs):
-            own_score = (part[:, :used] * score_scale).astype(jnp.bfloat16)
-            own_prob = prob[:, :used].astype(jnp.bfloat16)
-            for left, right_ref, ref in ((own_score, q_ref, gk_ref), (own_prob, g_ref, gv_ref)):
-                grad = dot(left, right_ref[here, cols], TN)
-                if used == near:
-                    ref[:, cols] = grad
-                else:
-                    ref[:used, cols] += grad
+            own_score = (part[:, : CORES * used] * score_scale).astype(jnp.bfloat16)
+            own_prob = prob[:, : CORES * used].astype(jnp.bfloat16)
+            grads.append((dot(own_score, q_ref[here, cols], TN), dot(own_prob, g_ref[here, cols], TN)))
+        low = near // 2
+        for (cols, _, _), early, late in zip(units[0::2], grads[0::2], grads[1::2]):
+            for which, own_ref in enumerate((gk_ref, gv_ref)):
+                for core in range(CORES):
+                    top = late[which][core * near : core * near + low]
+                    top += early[which][core * low : (core + 1) * low]
+                    bottom = late[which][core * near + low : (core + 1) * near]
+                    if core == 0:
+                        own_ref[:low, cols] = top
+                        own_ref[low:, cols] = bottom
+                    else:
+                        sent_ref[which, :low, cols] = top.astype(sent_ref.dtype)
+                        sent_ref[which, low:, cols] = bottom.astype(sent_ref.dtype)
 
 
 def call(kernel, operands, outs, pairs, products, head_dim, in_specs=None, scratch=()):
@@ -307,7 +376,10 @@
     blk_len = part_tok * members
     near = blocks * part_tok
     head_dim = feat_width // HEADS
+    half = feat_width // CORES
     levels = seq_count // COLUMNS
+    groups = members // CORES
+
     def hop(part, column_step, member_step):
         pairs = [
             (s * members + m, (s ^ column_step) * members + (m ^ member_step))
@@ -326,83 +398,90 @@
             part, "seq", [(s, s - COLUMNS * d) for s in range(COLUMNS * d, seq_count)]
         )
 
-    own_pair, both, block = pick_pair(layout.T, keys, values)
-    both = both.reshape(2, near, feat_width)
+    mine, theirs, pair_mine, pair_theirs, mask = pick_pair(layout.T, keys, values)
+    own_pair = jnp.stack([pair_mine, hop(pair_theirs, 0, 1)])
     climbed = [climb(own_pair, d) for d in range(1, levels)]
     column = jnp.stack(climbed)
+    chip_parts = [mine, hop(theirs, 0, 1)]
+    near_parts = list(chip_parts)
+    for group in range(1, groups):
+        near_parts += [hop(part, 0, CORES * group) for part in chip_parts]
     sent_pair, _ = lax.optimization_barrier((own_pair, climbed[0]))
-    cross_pairs = []
-    for step in range(0, members, 2):
-        pair = hop(sent_pair, 1, step)
-        cross_pairs += [pair, hop(pair, 0, 1)]
-    column, cross_pairs = lax.optimization_barrier((column, cross_pairs))
+    cross_pairs = [hop(sent_pair, 1, CORES * group) for group in range(groups)]
+    column, cross_pairs, near_parts = lax.optimization_barrier((column, cross_pairs, near_parts))
+    near_parts = [part.reshape(2, near, half) for part in near_parts]
     crossing = [
-        [column if (c, step) == (0, 0) else hop(column, c, step) for c in range(COLUMNS)]
-        for step in range(0, members, 2)
+        [column if (c, group) == (0, 0) else hop(column, c, CORES * group) for c in range(COLUMNS)]
+        for group in range(groups)
     ]
-    near_parts = [both, hop(both, 0, 1)]
-    for step in range(2, members, 2):
-        landed, _ = lax.optimization_barrier((hop(both, 0, step), column))
-        near_parts += [landed, hop(landed, 0, 1)]
 
     def rows_out(dtype):
-        return jax.ShapeDtypeStruct((tok_rows, feat_width), dtype)
-
-    near_out = jax.ShapeDtypeStruct((near, feat_width), jnp.float32)
+        return pltpu.VMEM((tok_rows, half), dtype)
+
+    near_out = pltpu.VMEM((near, half), jnp.float32)
     far_out = jax.ShapeDtypeStruct((levels,) + own_pair.shape, jnp.bfloat16)
-    near_pairs = HEADS * tok_rows * members * near
+    near_pairs = HEADS // CORES * tok_rows * members * near
     far_width = members * seq_count * part_tok
-    far_pairs = HEADS * tok_rows * far_width
+    far_pairs = HEADS // CORES * tok_rows * far_width
     roomy = far_width <= 512
     far_plan = (tok_rows // 2, GROUP, 2 * GROUP) if roomy else (tok_rows // 8, 1, 1)
 
-    in_hbm = pl.BlockSpec(memory_space=pltpu.HBM)
     near_sum, near_stat, bias, queries, grad_out = call(
-        functools.partial(near_forward_kernel, members, blk_len, part_tok),
+        functools.partial(near_forward_kernel, members, blk_len, part_tok, head_dim),
         [pltpu.with_memory_space_constraint(a, pltpu.HBM) for a in (queries, grad_out)] + near_parts,
-        [pltpu.VMEM((tok_rows, feat_width), jnp.float32)] * 2
+        [rows_out(jnp.float32)] * 2
         + [pltpu.VMEM((tok_rows, members * near), jnp.float32)]
-        + [pltpu.VMEM((tok_rows, feat_width), jnp.bfloat16)] * 2,
+        + [rows_out(jnp.bfloat16)] * 2,
         near_pairs,
         2,
         head_dim,
-        [in_hbm, in_hbm] + [WHOLE] * members,
-        [pltpu.SemaphoreType.DMA((HEADS // GROUP + 1,))],
+        [IN_HBM, IN_HBM] + [WHOLE] * members,
+        [pltpu.SemaphoreType.DMA((half // (GROUP * head_dim) + 1,))],
     )
     far_parts = []
-    for group in crossing:
-        group, _ = lax.optimization_barrier((group, near_stat))
-        for same, other in (group, [hop(part, 0, 1) for part in group]):
-            far_parts += [own_pair, same, cross_pairs[len(far_parts) // 4], other]
+    for group, cross_pair in zip(crossing, cross_pairs):
+        (same, other), _ = lax.optimization_barrier((group, near_stat))
+        far_parts += [own_pair, same, cross_pair, other]
     attended, far_gq, level, drift, own_grad, cross_grad = call(
-        functools.partial(far_kernel, members, *far_plan),
+        functools.partial(far_kernel, groups, head_dim, *far_plan),
         [queries, grad_out, near_sum, near_stat] + far_parts,
         [rows_out(jnp.bfloat16)] + [rows_out(jnp.float32)] * 3 + [far_out, far_out],
         far_pairs,
         5,
         head_dim,
     )
-    grad_q, near_k, near_v = call(
-        functools.partial(near_backward_kernel, members),
+    grad_q, near_k, near_v, near_sent = call(
+        functools.partial(near_backward_kernel, members, head_dim),
         [bias, queries, grad_out, level, drift, far_gq] + near_parts,
-        [rows_out(jnp.bfloat16), near_out, near_out],
+        [rows_out(jnp.bfloat16), near_out, near_out, pltpu.VMEM((2, near, half), jnp.bfloat16)],
         near_pairs,
         4,
         head_dim,
     )
     crossed, near_k = lax.optimization_barrier((hop(cross_grad, 1, 0), near_k))
-    returned = []
+    returned = [crossed[0]]
     for d in range(1, levels):
         summed = own_grad[d].astype(jnp.float32) + crossed[d].astype(jnp.float32)
         returned.append(sink(summed.astype(jnp.bfloat16), d))
-    extra = sum(part.astype(jnp.float32) for part in [crossed[0]] + returned)
-    chosen = (jnp.arange(blocks) == block[0, 0])[:, None, None]
-
-    def finish(near_term, far_term):
-        near_term = near_term.reshape(blocks, part_tok, feat_width)
-        return (near_term + jnp.where(chosen, far_term[None], 0.0)).astype(jnp.bfloat16)
-
-    return (attended, grad_q, finish(near_k, extra[0]), finish(near_v, extra[1]))
+    near_theirs = hop(near_sent, 0, 1)
+    attended, grad_q = join([(attended, hop(attended, 0, 1)), (grad_q, hop(grad_q, 0, 1))])
+    returned, attended, grad_q = lax.optimization_barrier((returned, attended, grad_q))
+    far_sent = sum(part[1].astype(jnp.float32) for part in returned).astype(jnp.bfloat16)
+    shape = (blocks, part_tok, half)
+    grad_k, grad_v = pl.pallas_call(
+        finish_kernel,
+        in_specs=[WHOLE] * (5 + levels),
+        out_specs=[WHOLE] * 2,
+        out_shape=[jax.ShapeDtypeStruct(keys.shape, keys.dtype)] * 2,
+    )(
+        mask,
+        near_k.reshape(shape),
+        near_v.reshape(shape),
+        near_theirs.reshape((2,) + shape),
+        hop(far_sent, 0, 1),
+        *returned,
+    )
+    return (attended, grad_q, grad_k, grad_v)
 
 
 def solution(mesh):

time: 66.4 us -> 63.1 us (0.950)
  waiting for transfers between devices: 13.3 us -> 21.7 us
  Pallas kernels: 21.5 us -> 14.5 us
  starting transfers between devices: 26.4 us -> 24.4 us
  other arithmetic: 1.69 us -> 0.11 us
  local copies, waits for them, and re-layouts: 2.29 us -> 1.2 us
    ppermute x15 -> x14, waiting for transfers between devices: 4.48 us -> 16.2 us  [hop(): return lax.ppermute(part, ('seq', 'kv'), pairs)]
    pallas_call x3, Pallas kernels: 19.6 us -> 9.71 us  [call(): pl.pallas_call(kernel, in_specs=in_specs or [WHOLE] * len(operands), out_...]
    pallas_call x1 -> x3, Pallas kernels: 1.9 us -> 4.79 us  [the longest x1 2.14 us: shards(): pl.pallas_call(finish_kernel, in_specs=[WHOLE] * (5 + levels), out_specs=...]
    ppermute x3, starting transfers between devices: 10.8 us -> 8.65 us  [climb(): lax.ppermute(part, 'seq', [(s, s + COLUMNS * d) for s in range(seq_count...]
    ppermute x3, waiting for transfers between devices: 7.33 us -> 5.48 us  [sink(): lax.ppermute(part, 'seq', [(s, s - COLUMNS * d) for s in range(COLUMNS *...]
    ppermute x3, waiting for transfers between devices: 1.53 us -> 0.01 us  [climb(): lax.ppermute(part, 'seq', [(s, s + COLUMNS * d) for s in range(seq_count...]
    slice x1 -> x0, local copies, waits for them, and re-layouts: 1.23 us -> none  [shards(): chosen = (jnp.arange(blocks) == block[0, 0])[:, None, None]]
    convert_element_type x1 -> x0, other arithmetic: 0.97 us -> none  [finish(): (near_term + jnp.where(chosen, far_term[None], 0.0)).astype(jnp.bfloat16)]
  transfers between devices with their start and end apart: 21 -> 20, of which waited for: 7 -> 9; matrix products, arithmetic and copies ran while one was open for 3% -> 0% of each run, Pallas kernels for 16% -> 7%
where the time goes in v5:
time: 63.1 us; the launch traced here: 62.7 us
  starting transfers between devices  24.4 us (39%)
  waiting for transfers between devices  21.7 us (34%)
  Pallas kernels  14.5 us (23%)
  local copies, waits for them, and re-layouts  1.2 us (2%)
  between operations  0.87 us (1%)
    ppermute x14, waiting for transfers between devices, hop(): return lax.ppermute(part, ('seq', 'kv'), pairs)  16.2 us
    ppermute x14, starting transfers between devices, hop(): return lax.ppermute(part, ('seq', 'kv'), pairs)  11.9 us
    pallas_call x3, Pallas kernels, call(): pl.pallas_call(kernel, in_specs=in_specs or [WHOLE] * len(operands), out_...  9.71 us
    ppermute x3, starting transfers between devices, climb(): lax.ppermute(part, 'seq', [(s, s + COLUMNS * d) for s in range(seq_count...  8.65 us
    ppermute x3, waiting for transfers between devices, sink(): lax.ppermute(part, 'seq', [(s, s - COLUMNS * d) for s in range(COLUMNS *...  5.48 us
    ppermute x3, starting transfers between devices, sink(): lax.ppermute(part, 'seq', [(s, s - COLUMNS * d) for s in range(COLUMNS *...  3.88 us
    pallas_call x1, Pallas kernels, shards(): pl.pallas_call(finish_kernel, in_specs=[WHOLE] * (5 + levels), out_specs=...  2.14 us
    pallas_call x1, Pallas kernels, join(): pl.pallas_call(join_kernel, in_specs=[WHOLE] * len(operands), out_specs=[...  1.42 us
  transfers between devices with their start and end apart: 20, of which 9 were waited for; matrix products, arithmetic and copies ran while one was open for 0% of the time, Pallas kernels for 7%

profile of v5, /device:TPU:0, one launch (start us, length us, event | category | flops | bytes accessed | tf_op | source)
XLA Modules:
  0.0 62.7 jit_solution(5850175215204645802)
XLA Ops:
  0.6 1.2 %shard_map.84 = (bf16[2,8,16,512]{3,2,1,0:T(8,128)(2,1)S(1)}, bf16[2,8,16,512]{3,2,1,0:T(8,128)(2,1)S(1)}, bf16[2,16,512]{2,1,0:T(8,128)(2,1)S(1)}, bf16[2,16,512]{2,1,0:T(8,128)(2,1)S(1)}, f32[8,16,512]{2,1,0:T(8,128)S(1)}) custom-call(s32[15,64]{1,0:T(8,128)} %bitcast.39, bf16[8,16,1024]{2,1,0:T(8,128)(2,1)} %keys_hbm.1, bf16[8,16,1024]{2,1,0:T(8,128)(2,1)} %values_hbm.1), custom_call_target="tpu_custom_call" | custom-call | tf_op jit(solution)/shard_map/pallas_call | solution.py:74
  1.9 0.5 collective-permute-start.6
  2.5 2.9 %collective-permute-start.7 = (bf16[2,8,16,512]{3,2,1,0:T(8,128)(2,1)S(1)}, bf16[2,8,16,512]{3,2,1,0:T(8,128)(2,1)S(1)}, u32[]{:S(2)}, u32[]{:S(2)}) collective-permute-start(bf16[2,8,16,512]{3,2,1,0:T(8,128)(2,1)S(1)} %get-tuple-element.53), channel_id=1, source_target_pairs={{0,2},{1,3},{2,0},{3,1},{4,6},{5,7},{6,4},{7,5},{8,10},{9,11},{10,... | collective-permute-start | bytes 786440 | tf_op jit(solution)/shard_map/ppermute | solution.py:389
  5.4 1.0 %collective-permute-start.8 = (bf16[2,8,16,512]{3,2,1,0:T(8,128)(2,1)S(1)}, bf16[2,8,16,512]{3,2,1,0:T(8,128)(2,1)S(1)}, u32[]{:S(2)}, u32[]{:S(2)}) collective-permute-start(bf16[2,8,16,512]{3,2,1,0:T(8,128)(2,1)S(1)} %collective-permute-done.6), channel_id=1, source_target_pairs={{0,2},{1,3},{2,0},{3,1},{4,6},{5,7},{6,4},{7,5},{8,10},{9,11},{10,... | collective-permute-start | bytes 786440 | tf_op jit(solution)/shard_map/ppermute | solution.py:389
  6.5 3.5 %collective-permute-start.1 = (bf16[2,2,16,512]{3,2,1,0:T(8,128)(2,1)S(1)}, bf16[2,2,16,512]{3,2,1,0:T(8,128)(2,1)S(1)}, u32[]{:S(2)}, u32[]{:S(2)}) collective-permute-start(bf16[2,2,16,512]{3,2,1,0:T(8,128)(2,1)S(1)} %pad_maximum_fusion.1.refs_0_.refs_4_), channel_id=1, source_target_pairs={{0,8},{4,12},{8,16},{12,20},{16,24},{20,28},{1,9},{5,13},{9,17},{1... | collective-permute-start | bytes 196616 | tf_op jit(solution)/shard_map/ppermute | solution.py:392
  9.9 3.3 %collective-permute-start.3 = (bf16[2,2,16,512]{3,2,1,0:T(8,128)(2,1)S(1)}, bf16[2,2,16,512]{3,2,1,0:T(8,128)(2,1)S(1)}, u32[]{:S(2)}, u32[]{:S(2)}) collective-permute-start(bf16[2,2,16,512]{3,2,1,0:T(8,128)(2,1)S(1)} %pad_maximum_fusion.1.refs_0_.refs_4_), channel_id=1, source_target_pairs={{0,24},{4,28},{1,25},{5,29},{2,26},{6,30},{3,27},{7,31}} | collective-permute-start | bytes 196616 | tf_op jit(solution)/shard_map/ppermute | solution.py:392
  13.3 1.8 %collective-permute-start.2 = (bf16[2,2,16,512]{3,2,1,0:T(8,128)(2,1)S(1)}, bf16[2,2,16,512]{3,2,1,0:T(8,128)(2,1)S(1)}, u32[]{:S(2)}, u32[]{:S(2)}) collective-permute-start(bf16[2,2,16,512]{3,2,1,0:T(8,128)(2,1)S(1)} %pad_maximum_fusion.1.refs_0_.refs_4_), channel_id=1, source_target_pairs={{0,16},{4,20},{8,24},{12,28},{1,17},{5,21},{9,25},{13,29},{2,18},{... | collective-permute-start | bytes 196616 | tf_op jit(solution)/shard_map/ppermute | solution.py:392
  15.1 2.0 %collective-permute-start.5 = (bf16[2,2,16,512]{3,2,1,0:T(8,128)(2,1)S(1)}, bf16[2,2,16,512]{3,2,1,0:T(8,128)(2,1)S(1)}, u32[]{:S(2)}, u32[]{:S(2)}) collective-permute-start(bf16[2,2,16,512]{3,2,1,0:T(8,128)(2,1)S(1)} %pad_maximum_fusion.1.refs_0_.refs_4_), channel_id=1, source_target_pairs={{0,6},{1,7},{2,4},{3,5},{4,2},{5,3},{6,0},{7,1},{8,14},{9,15},{10,... | collective-permute-start | bytes 196616 | tf_op jit(solution)/shard_map/ppermute | solution.py:389
  17.1 0.5 collective-permute-start.4
  17.7 2.9 %collective-permute-done.5.refs_6_ = bf16[2,2,16,512]{3,2,1,0:T(8,128)(2,1)S(1)} collective-permute-done((bf16[2,2,16,512]{3,2,1,0:T(8,128)(2,1)S(1)}, bf16[2,2,16,512]{3,2,1,0:T(8,128)(2,1)S(1)}, u32[]{:S(2)}, u32[]{:S(2)}) %collective-permute-start.5) | collective-permute-done | bytes 65568 | tf_op jit(solution)/shard_map/ppermute | solution.py:389
  20.6 0.8 %collective-permute-done.4.refs_2_ = bf16[2,2,16,512]{3,2,1,0:T(8,128)(2,1)S(1)} collective-permute-done((bf16[2,2,16,512]{3,2,1,0:T(8,128)(2,1)S(1)}, bf16[2,2,16,512]{3,2,1,0:T(8,128)(2,1)S(1)}, u32[]{:S(2)}, u32[]{:S(2)}) %collective-permute-start.4) | collective-permute-done | bytes 65568 | tf_op jit(solution)/shard_map/ppermute | solution.py:389
  21.4 1.2 %collective-permute-start.11 = (bf16[3,2,2,16,512]{4,3,2,1,0:T(8,128)(2,1)S(1)}, bf16[3,2,2,16,512]{4,3,2,1,0:T(8,128)(2,1)S(1)}, u32[]{:S(2)}, u32[]{:S(2)}) collective-permute-start(bf16[3,2,2,16,512]{4,3,2,1,0:T(8,128)(2,1)S(1)} %pad_maximum_fusion.refs_1_), channel_id=1, source_target_pairs={{0,6},{1,7},{2,4},{3,5},{4,2},{5,3},{6,0},{7,1},{8,14},{9,15},{10,... | collective-permute-start | bytes 589832 | tf_op jit(solution)/shard_map/ppermute | solution.py:389
  22.6 1.0 %collective-permute-start.10 = (bf16[3,2,2,16,512]{4,3,2,1,0:T(8,128)(2,1)S(1)}, bf16[3,2,2,16,512]{4,3,2,1,0:T(8,128)(2,1)S(1)}, u32[]{:S(2)}, u32[]{:S(2)}) collective-permute-start(bf16[3,2,2,16,512]{4,3,2,1,0:T(8,128)(2,1)S(1)} %pad_maximum_fusion.refs_1_), channel_id=1, source_target_pairs={{0,2},{1,3},{2,0},{3,1},{4,6},{5,7},{6,4},{7,5},{8,10},{9,11},{10,... | collective-permute-start | bytes 589832 | tf_op jit(solution)/shard_map/ppermute | solution.py:389
  23.6 1.3 %collective-permute-start.9 = (bf16[3,2,2,16,512]{4,3,2,1,0:T(8,128)(2,1)S(1)}, bf16[3,2,2,16,512]{4,3,2,1,0:T(8,128)(2,1)S(1)}, u32[]{:S(2)}, u32[]{:S(2)}) collective-permute-start(bf16[3,2,2,16,512]{4,3,2,1,0:T(8,128)(2,1)S(1)} %pad_maximum_fusion.refs_1_), channel_id=1, source_target_pairs={{0,4},{1,5},{2,6},{3,7},{4,0},{5,1},{6,2},{7,3},{8,12},{9,13},{10,... | collective-permute-start | bytes 589832 | tf_op jit(solution)/shard_map/ppermute | solution.py:389
  24.9 2.7 %shard_map.85 = (f32[512,512]{1,0:T(8,128)S(1)}, f32[512,512]{1,0:T(8,128)S(1)}, f32[512,512]{1,0:T(8,128)S(1)}, bf16[512,512]{1,0:T(8,128)(2,1)S(1)}, bf16[512,512]{1,0:T(8,128)(2,1)S(1)}) custom-call(bf16[512,1024]{1,0:T(8,128)(2,1)} %q_hbm.1, bf16[512,1024]{1,0:T(8,128)(2,1)} %g_hbm.1, bf16[2,128,512]{2,1,0:T(8,128)(2,1)S(1)} %bitcast.26, ...), custom_call_target="tpu_custom_call" | custom-call | flops 1073741824 | bytes 3145728 | tf_op jit(solution)/shard_map/pallas_call | solution.py:358
  27.6 1.2 %collective-permute-done.11.refs_7_ = bf16[3,2,2,16,512]{4,3,2,1,0:T(8,128)(2,1)S(1)} collective-permute-done((bf16[3,2,2,16,512]{4,3,2,1,0:T(8,128)(2,1)S(1)}, bf16[3,2,2,16,512]{4,3,2,1,0:T(8,128)(2,1)S(1)}, u32[]{:S(2)}, u32[]{:S(2)}) %collective-permute-start.11) | collective-permute-done | bytes 196640 | tf_op jit(solution)/shard_map/ppermute | solution.py:389
  28.9 2.0 %collective-permute-done.10.refs_5_ = bf16[3,2,2,16,512]{4,3,2,1,0:T(8,128)(2,1)S(1)} collective-permute-done((bf16[3,2,2,16,512]{4,3,2,1,0:T(8,128)(2,1)S(1)}, bf16[3,2,2,16,512]{4,3,2,1,0:T(8,128)(2,1)S(1)}, u32[]{:S(2)}, u32[]{:S(2)}) %collective-permute-start.10) | collective-permute-done | bytes 196640 | tf_op jit(solution)/shard_map/ppermute | solution.py:389
  30.9 0.6 collective-permute-done.9.refs_3_
  31.4 4.5 %shard_map.86 = (bf16[512,512]{1,0:T(8,128)(2,1)S(1)}, f32[512,512]{1,0:T(8,128)S(1)}, f32[512,512]{1,0:T(8,128)S(1)}, f32[512,512]{1,0:T(8,128)S(1)}, bf16[4,2,...) custom-call(bf16[512,512]{1,0:T(8,128)(2,1)S(1)} %get-tuple-element.57.q_ref, ...), custom_call_target="tpu_custom_call" | custom-call | flops 2684354560 | bytes 4194304 | tf_op jit(solution)/shard_map/pallas_call | solution.py:358
  36.0 2.4 %shard_map.87 = (bf16[512,512]{1,0:T(8,128)(2,1)S(1)}, f32[128,512]{1,0:T(8,128)S(1)}, f32[128,512]{1,0:T(8,128)S(1)}, bf16[2,128,512]{2,1,0:T(8,128)(2,1)S(1)}) custom-call(f32[512,512]{1,0:T(8,128)S(1)} %get-tuple-element.69.bias_ref, bf16[512,512]{1,0:T(8,128)(2,1)S(1)} %get-tuple-element.57.q_ref, bf16[512,512]{1,0:T(8,128)(2,1)S(1)} %get-tuple-element.58.g_ref, ...), custom_call_target="tpu_custom_call" | custom-call | flops 2147483648 | bytes 6291456 | tf_op jit(solution)/shard_map/pallas_call | solution.py:358
  38.5 0.7 %collective-permute-start.12 = (bf16[4,2,2,16,512]{4,3,2,1,0:T(8,128)(2,1)S(1)}, bf16[4,2,2,16,512]{4,3,2,1,0:T(8,128)(2,1)S(1)}, u32[]{:S(2)}, u32[]{:S(2)}) collective-permute-start(bf16[4,2,2,16,512]{4,3,2,1,0:T(8,128)(2,1)S(1)} %get-tuple-element.68), channel_id=1, source_target_pairs={{0,4},{1,5},{2,6},{3,7},{4,0},{5,1},{6,2},{7,3},{8,12},{9,13},{10,... | collective-permute-start | bytes 786440 | tf_op jit(solution)/shard_map/ppermute | solution.py:389
  39.8 7.5 %collective-permute-done.12 = bf16[4,2,2,16,512]{4,3,2,1,0:T(8,128)(2,1)S(1)} collective-permute-done((bf16[4,2,2,16,512]{4,3,2,1,0:T(8,128)(2,1)S(1)}, bf16[4,2,2,16,512]{4,3,2,1,0:T(8,128)(2,1)S(1)}, u32[]{:S(2)}, u32[]{:S(2)}) %collective-permute-start.12) | collective-permute-done | bytes 262176 | tf_op jit(solution)/shard_map/ppermute | solution.py:389
  47.3 1.3 %collective-permute-start.15 = (bf16[2,2,16,512]{3,2,1,0:T(8,128)(2,1)S(1)}, bf16[2,2,16,512]{3,2,1,0:T(8,128)(2,1)S(1)}, u32[]{:S(2)}, u32[]{:S(2)}) collective-permute-start(bf16[2,2,16,512]{3,2,1,0:T(8,128)(2,1)S(1)} %get-tuple-element.92), channel_id=1, source_target_pairs={{24,0},{28,4},{25,1},{29,5},{26,2},{30,6},{27,3},{31,7}} | collective-permute-start | bytes 196616 | tf_op jit(solution)/shard_map/ppermute | solution.py:397
  48.6 1.3 %collective-permute-start.14 = (bf16[2,2,16,512]{3,2,1,0:T(8,128)(2,1)S(1)}, bf16[2,2,16,512]{3,2,1,0:T(8,128)(2,1)S(1)}, u32[]{:S(2)}, u32[]{:S(2)}) collective-permute-start(bf16[2,2,16,512]{3,2,1,0:T(8,128)(2,1)S(1)} %get-tuple-element.93), channel_id=1, source_target_pairs={{16,0},{20,4},{24,8},{28,12},{17,1},{21,5},{25,9},{29,13},{18,2},{... | collective-permute-start | bytes 196616 | tf_op jit(solution)/shard_map/ppermute | solution.py:397
  49.9 1.3 %collective-permute-start.13 = (bf16[2,2,16,512]{3,2,1,0:T(8,128)(2,1)S(1)}, bf16[2,2,16,512]{3,2,1,0:T(8,128)(2,1)S(1)}, u32[]{:S(2)}, u32[]{:S(2)}) collective-permute-start(bf16[2,2,16,512]{3,2,1,0:T(8,128)(2,1)S(1)} %get-tuple-element.94), channel_id=1, source_target_pairs={{8,0},{12,4},{16,8},{20,12},{24,16},{28,20},{9,1},{13,5},{17,9},{2... | collective-permute-start | bytes 196616 | tf_op jit(solution)/shard_map/ppermute | solution.py:397
  51.3 1.4 %shard_map.88 = (bf16[512,1024]{1,0:T(8,128)(2,1)}, bf16[512,1024]{1,0:T(8,128)(2,1)}) custom-call(bf16[512,512]{1,0:T(8,128)(2,1)S(1)} %get-tuple-element.76.refs_0_, bf16[512,512]{1,0:T(8,128)(2,1)S(1)} %collective-permute-done.16.refs_1_, bf16[512,512]{1,0:T(8,128)(2,1)S(1)} %get-tuple-element.77.refs_2_, bf16[512,512]{1,0:T(8,128)(2,1)S(1)} %collective-permute-done.17.refs_3_), custom_call_target="tpu_custom_call" | custom-call | tf_op jit(solution)/shard_map/pallas_call | solution.py:107
  52.7 3.4 %collective-permute-done.15.refs_3_ = bf16[2,2,16,512]{3,2,1,0:T(8,128)(2,1)S(1)} collective-permute-done((bf16[2,2,16,512]{3,2,1,0:T(8,128)(2,1)S(1)}, bf16[2,2,16,512]{3,2,1,0:T(8,128)(2,1)S(1)}, u32[]{:S(2)}, u32[]{:S(2)}) %collective-permute-start.15) | collective-permute-done | bytes 65568 | tf_op jit(solution)/shard_map/ppermute | solution.py:397
  56.1 2.1 %collective-permute-done.14.refs_2_ = bf16[2,2,16,512]{3,2,1,0:T(8,128)(2,1)S(1)} collective-permute-done((bf16[2,2,16,512]{3,2,1,0:T(8,128)(2,1)S(1)}, bf16[2,2,16,512]{3,2,1,0:T(8,128)(2,1)S(1)}, u32[]{:S(2)}, u32[]{:S(2)}) %collective-permute-start.14) | collective-permute-done | bytes 65568 | tf_op jit(solution)/shard_map/ppermute | solution.py:397
  58.2 0.6 copy-done.6
  58.8 1.2 %collective-permute-done.19.far_ref = bf16[2,16,512]{2,1,0:T(8,128)(2,1)S(1)} collective-permute-done((bf16[2,16,512]{2,1,0:T(8,128)(2,1)S(1)}, bf16[2,16,512]{2,1,0:T(8,128)(2,1)S(1)}, u32[]{:S(2)}, u32[]{:S(2)}) %collective-permute-start.19) | collective-permute-done | bytes 32800 | tf_op jit(solution)/shard_map/ppermute | solution.py:389
  60.0 0.6 copy-done.8
  60.6 2.1 %shard_map.89 = (bf16[8,16,1024]{2,1,0:T(8,128)(2,1)}, bf16[8,16,1024]{2,1,0:T(8,128)(2,1)}) custom-call(f32[8,16,512]{2,1,0:T(8,128)} %copy-done, f32[8,16,512]{2,1,0:T(8,128)} %bitcast.23, f32[8,16,512]{2,1,0:T(8,128)} %bitcast.24, bf16[2,8,16,512]{3,2,1,0:T(8,128)(2,1)} %bitcast.34, bf16[2,16,512]{2,1,0:T(8,128)(2,1)} %copy-done.8, ...), custom_call_target="tpu_custom_call" | custom-call | tf_op jit(solution)/shard_map/pallas_call | solution.py:471
  (37 shorter events, 0.8 us)
Async XLA Ops:
  1.9 15.8 %copy-start = (f32[8,16,512]{2,1,0:T(8,128)}, f32[8,16,512]{2,1,0:T(8,128)S(1)}, u32[]{:S(2)}) copy-start(f32[8,16,512]{2,1,0:T(8,128)S(1)} %get-tuple-element.82.mask_ref) | copy-start | bytes 786436
  1.9 3.5 %collective-permute-start.6 = (bf16[2,8,16,512]{3,2,1,0:T(8,128)(2,1)S(1)}, bf16[2,8,16,512]{3,2,1,0:T(8,128)(2,1)S(1)}, u32[]{:S(2)}, u32[]{:S(2)}) collective-permute-start(bf16[2,8,16,512]{3,2,1,0:T(8,128)(2,1)S(1)} %get-tuple-element.52), channel_id=1, source_target_pairs={{0,1},{1,0},{2,3},{3,2},{4,5},{5,4},{6,7},{7,6},{8,9},{9,8},{10,11... | collective-permute-start | bytes 786440 | tf_op jit(solution)/shard_map/ppermute | solution.py:389
  2.4 4.1 %collective-permute-start = (bf16[2,16,512]{2,1,0:T(8,128)(2,1)S(1)}, bf16[2,16,512]{2,1,0:T(8,128)(2,1)S(1)}, u32[]{:S(2)}, u32[]{:S(2)}) collective-permute-start(bf16[2,16,512]{2,1,0:T(8,128)(2,1)S(1)} %get-tuple-element.49), channel_id=1, source_target_pairs={{0,1},{1,0},{2,3},{3,2},{4,5},{5,4},{6,7},{7,6},{8,9},{9,8},{10,11... | collective-permute-start | bytes 98312 | tf_op jit(solution)/shard_map/ppermute | solution.py:389
  2.5 18.9 %collective-permute-start.7 = (bf16[2,8,16,512]{3,2,1,0:T(8,128)(2,1)S(1)}, bf16[2,8,16,512]{3,2,1,0:T(8,128)(2,1)S(1)}, u32[]{:S(2)}, u32[]{:S(2)}) collective-permute-start(bf16[2,8,16,512]{3,2,1,0:T(8,128)(2,1)S(1)} %get-tuple-element.53), channel_id=1, source_target_pairs={{0,2},{1,3},{2,0},{3,1},{4,6},{5,7},{6,4},{7,5},{8,10},{9,11},{10,... | collective-permute-start | bytes 786440 | tf_op jit(solution)/shard_map/ppermute | solution.py:389
  5.4 16.0 %collective-permute-start.8 = (bf16[2,8,16,512]{3,2,1,0:T(8,128)(2,1)S(1)}, bf16[2,8,16,512]{3,2,1,0:T(8,128)(2,1)S(1)}, u32[]{:S(2)}, u32[]{:S(2)}) collective-permute-start(bf16[2,8,16,512]{3,2,1,0:T(8,128)(2,1)S(1)} %collective-permute-done.6), channel_id=1, source_target_pairs={{0,2},{1,3},{2,0},{3,1},{4,6},{5,7},{6,4},{7,5},{8,10},{9,11},{10,... | collective-permute-start | bytes 786440 | tf_op jit(solution)/shard_map/ppermute | solution.py:389
  6.5 8.7 %collective-permute-start.1 = (bf16[2,2,16,512]{3,2,1,0:T(8,128)(2,1)S(1)}, bf16[2,2,16,512]{3,2,1,0:T(8,128)(2,1)S(1)}, u32[]{:S(2)}, u32[]{:S(2)}) collective-permute-start(bf16[2,2,16,512]{3,2,1,0:T(8,128)(2,1)S(1)} %pad_maximum_fusion.1.refs_0_.refs_4_), channel_id=1, source_target_pairs={{0,8},{4,12},{8,16},{12,20},{16,24},{20,28},{1,9},{5,13},{9,17},{1... | collective-permute-start | bytes 196616 | tf_op jit(solution)/shard_map/ppermute | solution.py:392
  9.9 7.2 %collective-permute-start.3 = (bf16[2,2,16,512]{3,2,1,0:T(8,128)(2,1)S(1)}, bf16[2,2,16,512]{3,2,1,0:T(8,128)(2,1)S(1)}, u32[]{:S(2)}, u32[]{:S(2)}) collective-permute-start(bf16[2,2,16,512]{3,2,1,0:T(8,128)(2,1)S(1)} %pad_maximum_fusion.1.refs_0_.refs_4_), channel_id=1, source_target_pairs={{0,24},{4,28},{1,25},{5,29},{2,26},{6,30},{3,27},{7,31}} | collective-permute-start | bytes 196616 | tf_op jit(solution)/shard_map/ppermute | solution.py:392
  13.3 4.4 %collective-permute-start.2 = (bf16[2,2,16,512]{3,2,1,0:T(8,128)(2,1)S(1)}, bf16[2,2,16,512]{3,2,1,0:T(8,128)(2,1)S(1)}, u32[]{:S(2)}, u32[]{:S(2)}) collective-permute-start(bf16[2,2,16,512]{3,2,1,0:T(8,128)(2,1)S(1)} %pad_maximum_fusion.1.refs_0_.refs_4_), channel_id=1, source_target_pairs={{0,16},{4,20},{8,24},{12,28},{1,17},{5,21},{9,25},{13,29},{2,18},{... | collective-permute-start | bytes 196616 | tf_op jit(solution)/shard_map/ppermute | solution.py:392
  15.1 5.5 %collective-permute-start.5 = (bf16[2,2,16,512]{3,2,1,0:T(8,128)(2,1)S(1)}, bf16[2,2,16,512]{3,2,1,0:T(8,128)(2,1)S(1)}, u32[]{:S(2)}, u32[]{:S(2)}) collective-permute-start(bf16[2,2,16,512]{3,2,1,0:T(8,128)(2,1)S(1)} %pad_maximum_fusion.1.refs_0_.refs_4_), channel_id=1, source_target_pairs={{0,6},{1,7},{2,4},{3,5},{4,2},{5,3},{6,0},{7,1},{8,14},{9,15},{10,... | collective-permute-start | bytes 196616 | tf_op jit(solution)/shard_map/ppermute | solution.py:389
  17.1 4.3 %collective-permute-start.4 = (bf16[2,2,16,512]{3,2,1,0:T(8,128)(2,1)S(1)}, bf16[2,2,16,512]{3,2,1,0:T(8,128)(2,1)S(1)}, u32[]{:S(2)}, u32[]{:S(2)}) collective-permute-start(bf16[2,2,16,512]{3,2,1,0:T(8,128)(2,1)S(1)} %pad_maximum_fusion.1.refs_0_.refs_4_), channel_id=1, source_target_pairs={{0,4},{1,5},{2,6},{3,7},{4,0},{5,1},{6,2},{7,3},{8,12},{9,13},{10,... | collective-permute-start | bytes 196616 | tf_op jit(solution)/shard_map/ppermute | solution.py:389
  21.4 7.4 %collective-permute-start.11 = (bf16[3,2,2,16,512]{4,3,2,1,0:T(8,128)(2,1)S(1)}, bf16[3,2,2,16,512]{4,3,2,1,0:T(8,128)(2,1)S(1)}, u32[]{:S(2)}, u32[]{:S(2)}) collective-permute-start(bf16[3,2,2,16,512]{4,3,2,1,0:T(8,128)(2,1)S(1)} %pad_maximum_fusion.refs_1_), channel_id=1, source_target_pairs={{0,6},{1,7},{2,4},{3,5},{4,2},{5,3},{6,0},{7,1},{8,14},{9,15},{10,... | collective-permute-start | bytes 589832 | tf_op jit(solution)/shard_map/ppermute | solution.py:389
  22.6 8.3 %collective-permute-start.10 = (bf16[3,2,2,16,512]{4,3,2,1,0:T(8,128)(2,1)S(1)}, bf16[3,2,2,16,512]{4,3,2,1,0:T(8,128)(2,1)S(1)}, u32[]{:S(2)}, u32[]{:S(2)}) collective-permute-start(bf16[3,2,2,16,512]{4,3,2,1,0:T(8,128)(2,1)S(1)} %pad_maximum_fusion.refs_1_), channel_id=1, source_target_pairs={{0,2},{1,3},{2,0},{3,1},{4,6},{5,7},{6,4},{7,5},{8,10},{9,11},{10,... | collective-permute-start | bytes 589832 | tf_op jit(solution)/shard_map/ppermute | solution.py:389
  23.6 7.8 %collective-permute-start.9 = (bf16[3,2,2,16,512]{4,3,2,1,0:T(8,128)(2,1)S(1)}, bf16[3,2,2,16,512]{4,3,2,1,0:T(8,128)(2,1)S(1)}, u32[]{:S(2)}, u32[]{:S(2)}) collective-permute-start(bf16[3,2,2,16,512]{4,3,2,1,0:T(8,128)(2,1)S(1)} %pad_maximum_fusion.refs_1_), channel_id=1, source_target_pairs={{0,4},{1,5},{2,6},{3,7},{4,0},{5,1},{6,2},{7,3},{8,12},{9,13},{10,... | collective-permute-start | bytes 589832 | tf_op jit(solution)/shard_map/ppermute | solution.py:389
  38.4 8.9 %copy-start.1 = (f32[128,512]{1,0:T(8,128)}, f32[128,512]{1,0:T(8,128)S(1)}, u32[]{:S(2)}) copy-start(f32[128,512]{1,0:T(8,128)S(1)} %get-tuple-element.83) | copy-start | bytes 786436
  38.4 8.9 %copy-start.2 = (f32[128,512]{1,0:T(8,128)}, f32[128,512]{1,0:T(8,128)S(1)}, u32[]{:S(2)}) copy-start(f32[128,512]{1,0:T(8,128)S(1)} %get-tuple-element.84) | copy-start | bytes 786436
  38.4 11.5 %collective-permute-start.17 = (bf16[512,512]{1,0:T(8,128)(2,1)S(1)}, bf16[512,512]{1,0:T(8,128)(2,1)S(1)}, u32[]{:S(2)}, u32[]{:S(2)}) collective-permute-start(bf16[512,512]{1,0:T(8,128)(2,1)S(1)} %get-tuple-element.77.refs_2_), channel_id=1, source_target_pairs={{0,1},{1,0},{2,3},{3,2},{4,5},{5,4},{6,7},{7,6},{8,9},{9,8},{10,11... | collective-permute-start | bytes 1572872 | tf_op jit(solution)/shard_map/ppermute | solution.py:389
  38.5 8.7 %collective-permute-start.12 = (bf16[4,2,2,16,512]{4,3,2,1,0:T(8,128)(2,1)S(1)}, bf16[4,2,2,16,512]{4,3,2,1,0:T(8,128)(2,1)S(1)}, u32[]{:S(2)}, u32[]{:S(2)}) collective-permute-start(bf16[4,2,2,16,512]{4,3,2,1,0:T(8,128)(2,1)S(1)} %get-tuple-element.68), channel_id=1, source_target_pairs={{0,4},{1,5},{2,6},{3,7},{4,0},{5,1},{6,2},{7,3},{8,12},{9,13},{10,... | collective-permute-start | bytes 786440 | tf_op jit(solution)/shard_map/ppermute | solution.py:389
  39.2 12.0 %collective-permute-start.16 = (bf16[512,512]{1,0:T(8,128)(2,1)S(1)}, bf16[512,512]{1,0:T(8,128)(2,1)S(1)}, u32[]{:S(2)}, u32[]{:S(2)}) collective-permute-start(bf16[512,512]{1,0:T(8,128)(2,1)S(1)} %get-tuple-element.76.refs_0_), channel_id=1, source_target_pairs={{0,1},{1,0},{2,3},{3,2},{4,5},{5,4},{6,7},{7,6},{8,9},{9,8},{10,11... | collective-permute-start | bytes 1572872 | tf_op jit(solution)/shard_map/ppermute | solution.py:389
  39.4 19.4 %collective-permute-start.18 = (bf16[2,128,512]{2,1,0:T(8,128)(2,1)S(1)}, bf16[2,128,512]{2,1,0:T(8,128)(2,1)S(1)}, u32[]{:S(2)}, u32[]{:S(2)}) collective-permute-start(bf16[2,128,512]{2,1,0:T(8,128)(2,1)S(1)} %get-tuple-element.85), channel_id=1, source_target_pairs={{0,1},{1,0},{2,3},{3,2},{4,5},{5,4},{6,7},{7,6},{8,9},{9,8},{10,11... | collective-permute-start | bytes 786440 | tf_op jit(solution)/shard_map/ppermute | solution.py:389
  47.3 8.8 %collective-permute-start.15 = (bf16[2,2,16,512]{3,2,1,0:T(8,128)(2,1)S(1)}, bf16[2,2,16,512]{3,2,1,0:T(8,128)(2,1)S(1)}, u32[]{:S(2)}, u32[]{:S(2)}) collective-permute-start(bf16[2,2,16,512]{3,2,1,0:T(8,128)(2,1)S(1)} %get-tuple-element.92), channel_id=1, source_target_pairs={{24,0},{28,4},{25,1},{29,5},{26,2},{30,6},{27,3},{31,7}} | collective-permute-start | bytes 196616 | tf_op jit(solution)/shard_map/ppermute | solution.py:397
  48.6 9.6 %collective-permute-start.14 = (bf16[2,2,16,512]{3,2,1,0:T(8,128)(2,1)S(1)}, bf16[2,2,16,512]{3,2,1,0:T(8,128)(2,1)S(1)}, u32[]{:S(2)}, u32[]{:S(2)}) collective-permute-start(bf16[2,2,16,512]{3,2,1,0:T(8,128)(2,1)S(1)} %get-tuple-element.93), channel_id=1, source_target_pairs={{16,0},{20,4},{24,8},{28,12},{17,1},{21,5},{25,9},{29,13},{18,2},{... | collective-permute-start | bytes 196616 | tf_op jit(solution)/shard_map/ppermute | solution.py:397
  49.9 8.2 %collective-permute-start.13 = (bf16[2,2,16,512]{3,2,1,0:T(8,128)(2,1)S(1)}, bf16[2,2,16,512]{3,2,1,0:T(8,128)(2,1)S(1)}, u32[]{:S(2)}, u32[]{:S(2)}) collective-permute-start(bf16[2,2,16,512]{3,2,1,0:T(8,128)(2,1)S(1)} %get-tuple-element.94), channel_id=1, source_target_pairs={{8,0},{12,4},{16,8},{20,12},{24,16},{28,20},{9,1},{13,5},{17,9},{2... | collective-permute-start | bytes 196616 | tf_op jit(solution)/shard_map/ppermute | solution.py:397
  51.2 6.9 %copy-start.3 = (bf16[2,2,16,512]{3,2,1,0:T(8,128)(2,1)}, bf16[2,2,16,512]{3,2,1,0:T(8,128)(2,1)S(1)}, u32[]{:S(2)}) copy-start(bf16[2,2,16,512]{3,2,1,0:T(8,128)(2,1)S(1)} %slice_bitcast_fusion.refs_0_) | copy-start | bytes 196612
  56.1 2.1 %copy-start.5 = (bf16[2,2,16,512]{3,2,1,0:T(8,128)(2,1)}, bf16[2,2,16,512]{3,2,1,0:T(8,128)(2,1)S(1)}, u32[]{:S(2)}) copy-start(bf16[2,2,16,512]{3,2,1,0:T(8,128)(2,1)S(1)} %collective-permute-done.15.refs_3_) | copy-start | bytes 196612
  58.2 0.6 copy-start.6
  58.2 1.8 %copy-start.7 = (bf16[2,2,16,512]{3,2,1,0:T(8,128)(2,1)}, bf16[2,2,16,512]{3,2,1,0:T(8,128)(2,1)S(1)}, u32[]{:S(2)}) copy-start(bf16[2,2,16,512]{3,2,1,0:T(8,128)(2,1)S(1)} %collective-permute-done.13.refs_1_) | copy-start | bytes 196612
  58.8 1.2 %collective-permute-start.19 = (bf16[2,16,512]{2,1,0:T(8,128)(2,1)S(1)}, bf16[2,16,512]{2,1,0:T(8,128)(2,1)S(1)}, u32[]{:S(2)}, u32[]{:S(2)}) collective-permute-start(bf16[2,16,512]{2,1,0:T(8,128)(2,1)S(1)} %fusion.3), channel_id=1, source_target_pairs={{0,1},{1,0},{2,3},{3,2},{4,5},{5,4},{6,7},{7,6},{8,9},{9,8},{10,11... | collective-permute-start | bytes 98312 | tf_op jit(solution)/shard_map/ppermute | solution.py:389
  58.8 1.2 %copy-start.4 = (bf16[2,128,512]{2,1,0:T(8,128)(2,1)}, bf16[2,128,512]{2,1,0:T(8,128)(2,1)S(1)}, u32[]{:S(2)}) copy-start(bf16[2,128,512]{2,1,0:T(8,128)(2,1)S(1)} %collective-permute-done.18) | copy-start | bytes 786436
  60.0 0.6 copy-start.8

commit v6 on v5

--- a/solution.py
+++ b/solution.py
@@ -33,10 +33,10 @@
     return math.log2(math.e) / math.sqrt(head_dim)
 
 
-def pick_kernel(table_hbm, keys_hbm, values_hbm, mine_ref, theirs_ref, pair_ref, sent_ref, mask_ref, table_ref, sems):
+def pick_kernel(table_hbm, keys_hbm, values_hbm, mine_ref, theirs_ref, pair_ref, sent_ref, block_ref, table_ref, sems):
     window = lax.axis_index("seq")
     core = lax.axis_index("kv") % CORES
-    blocks, _, half = mask_ref.shape
+    _, blocks, part_tok, half = mine_ref.shape
     copies = [pltpu.make_async_copy(table_hbm, table_ref, sems.at[0])]
     for which, ref in enumerate((keys_hbm, values_hbm)):
         for side, out_ref in enumerate((mine_ref, theirs_ref)):
@@ -54,9 +54,8 @@
     named = jnp.where(here, table_ref[...].astype(jnp.float32), -1.0)
     named = jnp.max(jnp.max(named, axis=1, keepdims=True), axis=0, keepdims=True)
     block = jnp.clip(named - (window * blocks).astype(jnp.float32), 0.0, blocks - 1.0)
-    block = jnp.broadcast_to(block, mask_ref.shape[1:])
-    for b in range(blocks):
-        mask_ref[b] = jnp.where(block == b, 1.0, 0.0)
+    block_ref[...] = jnp.broadcast_to(block, block_ref.shape)
+    block = jnp.broadcast_to(block, (part_tok, half))
     for copy in copies[1:]:
         copy.wait()
     for ref, out_ref in ((mine_ref, pair_ref), (theirs_ref, sent_ref)):
@@ -77,55 +76,78 @@
         out_specs=[WHOLE] * 5,
         out_shape=[pltpu.VMEM((2, blocks, part_tok, half), keys.dtype)] * 2
         + [pltpu.VMEM((2, part_tok, half), keys.dtype)] * 2
-        + [pltpu.VMEM((blocks, part_tok, half), jnp.float32)],
+        + [pltpu.VMEM((8, 128), jnp.float32)],
         scratch_shapes=[pltpu.VMEM(table.shape, table.dtype), pltpu.SemaphoreType.DMA((5,))],
     )(*operands)
 
 
-def join_kernel(*refs):
-    sems = refs[-1]
-    count = (len(refs) - 1) // 3
+def join_kernel(att_ref, att_far, gq_ref, gq_far, near_ref, near_far, att_out, gq_out, gk_out, gv_out, sems):
     core = lax.axis_index("kv") % CORES
     copies = []
-    for i in range(count):
-        out_ref = refs[2 * count + i]
-        half = refs[2 * i].shape[1]
-        for side in range(CORES):
+    for out_ref, sides in (
+        (att_out, (att_ref, att_far)),
+        (gq_out, (gq_ref, gq_far)),
+        (gk_out, (near_ref.at[0], near_far.at[0])),
+        (gv_out, (near_ref.at[1], near_far.at[1])),
+    ):
+        half = out_ref.shape[1] // CORES
+        for side, ref in enumerate(sides):
             cols = pl.ds(pl.multiple_of((core ^ side) * half, half), half)
-            copies.append(
-                pltpu.make_async_copy(refs[2 * i + side], out_ref.at[:, cols], sems.at[len(copies)])
-            )
+            copies.append(pltpu.make_async_copy(ref, out_ref.at[:, cols], sems.at[len(copies)]))
     for copy in copies:
         copy.start()
     for copy in copies:
         copy.wait()
 
 
-def join(pairs):
-    rows, half = pairs[0][0].shape
-    operands = [pltpu.with_memory_space_constraint(a, pltpu.VMEM) for pair in pairs for a in pair]
+def join(operands, shapes):
+    operands = [pltpu.with_memory_space_constraint(a, pltpu.VMEM) for a in operands]
     return pl.pallas_call(
         join_kernel,
         in_specs=[WHOLE] * len(operands),
-        out_specs=[IN_HBM] * len(pairs),
-        out_shape=[pltpu.HBM((rows, half * CORES), pairs[0][0].dtype)] * len(pairs),
-        scratch_shapes=[pltpu.SemaphoreType.DMA((len(operands),))],
+        out_specs=[IN_HBM] * len(shapes),
+        out_shape=[pltpu.HBM(shape, jnp.bfloat16) for shape in shapes],
+        scratch_shapes=[pltpu.SemaphoreType.DMA((2 * len(shapes),))],
     )(*operands)
 
 
-def finish_kernel(mask_ref, gk_ref, gv_ref, near_ref, far_ref, *refs):
-    arrived = refs[:-2]
+def finish_kernel(block_ref, near_ref, near_far_ref, far_ref, *refs):
+    arrived, outs, rows_ref, sems = refs[:-6], refs[-4:-2], refs[-2], refs[-1]
     core = lax.axis_index("kv") % CORES
-    half = mask_ref.shape[-1]
+    part_tok, half = far_ref.shape[1:]
+    block = jnp.max(block_ref[...]).astype(jnp.int32)
+    here = pl.ds(pl.multiple_of(block * part_tok, part_tok), part_tok)
     mine = pl.ds(pl.multiple_of(core * half, half), half)
     theirs = pl.ds(pl.multiple_of((core ^ 1) * half, half), half)
-    mask = mask_ref[...]
-    for which, (own_ref, out_ref) in enumerate(zip((gk_ref, gv_ref), refs[-2:])):
-        extra = sum(ref[0, which].astype(jnp.float32) for ref in arrived)
-        out_ref[:, :, mine] = (own_ref[...] + mask * extra[None]).astype(out_ref.dtype)
-        near = near_ref[which].astype(jnp.float32)
-        extra = far_ref[which].astype(jnp.float32)
-        out_ref[:, :, theirs] = (near + mask * extra[None]).astype(out_ref.dtype)
+    copies = []
+    for which, out_ref in enumerate(outs):
+        total = near_ref[which, here]
+        for ref in arrived:
+            total += ref[0, which].astype(jnp.float32)
+        rows_ref[which, :, mine] = total.astype(rows_ref.dtype)
+        total = near_far_ref[which, here].astype(jnp.float32) + far_ref[which].astype(jnp.float32)
+        rows_ref[which, :, theirs] = total.astype(rows_ref.dtype)
+        copies.append(pltpu.make_async_copy(rows_ref.at[which], out_ref.at[here], sems.at[which]))
+        copies[-1].start()
+    for copy in copies:
+        copy.wait()
+
+
+def finish(operands, outs):
+    part_tok, half = operands[3].shape[1:]
+    operands = [pltpu.with_memory_space_constraint(a, pltpu.VMEM) for a in operands]
+    outs = [pltpu.with_memory_space_constraint(a, pltpu.HBM) for a in outs]
+    return pl.pallas_call(
+        finish_kernel,
+        in_specs=[WHOLE] * len(operands) + [IN_HBM] * 2,
+        out_specs=[IN_HBM] * 2,
+        out_shape=[pltpu.HBM(a.shape, a.dtype) for a in outs],
+        input_output_aliases={len(operands): 0, len(operands) + 1: 1},
+        scratch_shapes=[
+            pltpu.VMEM((2, part_tok, half * CORES), jnp.bfloat16),
+            pltpu.SemaphoreType.DMA((2,)),
+        ],
+    )(*operands, *outs)
 
 
 def near_tiles(rows, near):
@@ -212,11 +234,11 @@
     return jnp.concatenate(rows, axis=0)
 
 
-def far_kernel(groups, head_dim, tile, heads, batch, q_ref, g_ref, sum_ref, stat_ref, *refs):
+def far_kernel(groups, steps, head_dim, tile, heads, batch, q_ref, g_ref, sum_ref, stat_ref, *refs):
     parts = refs[: 2 * COLUMNS * groups]
     att_ref, gq_ref, level_ref, drift_ref, *grad_refs = refs[2 * COLUMNS * groups :]
+    _, cores, _, part_tok, _ = grad_refs[0].shape
     rows, half = q_ref.shape
-    steps, cores, _, part_tok, _ = grad_refs[0].shape
     span = steps * cores * part_tok
     width = COLUMNS * span
     score_scale = 1.0 / math.sqrt(head_dim)
@@ -292,14 +314,17 @@
         for which, per_head in enumerate(grads):
             for cols, terms in zip(columns, per_head):
                 total = functools.reduce(lambda a, b: a + b, terms).astype(jnp.bfloat16)
-                for c, ref in enumerate(grad_refs):
-                    piece = total[c * span : (c + 1) * span]
-                    ref[:, :, which, :, cols] = piece.reshape(steps, cores, part_tok, head_dim)
+                start = 0
+                for ref in grad_refs:
+                    shape = ref.shape[:2] + (part_tok, head_dim)
+                    count = math.prod(shape[:3])
+                    ref[:, :, which, :, cols] = total[start : start + count].reshape(shape)
+                    start += count
 
 
 def near_backward_kernel(members, head_dim, bias_ref, q_ref, g_ref, level_ref, drift_ref, far_gq_ref, *refs):
     parts = refs[:members]
-    gq_ref, gk_ref, gv_ref, sent_ref = refs[members:]
+    gq_ref, own_ref, kept_ref, sent_ref = refs[members:]
     rows, half = q_ref.shape
     near = parts[0].shape[1]
     score_scale = 1.0 / math.sqrt(head_dim)
@@ -340,17 +365,17 @@
             grads.append((dot(own_score, q_ref[here, cols], TN), dot(own_prob, g_ref[here, cols], TN)))
         low = near // 2
         for (cols, _, _), early, late in zip(units[0::2], grads[0::2], grads[1::2]):
-            for which, own_ref in enumerate((gk_ref, gv_ref)):
+            for which in range(2):
                 for core in range(CORES):
                     top = late[which][core * near : core * near + low]
                     top += early[which][core * low : (core + 1) * low]
                     bottom = late[which][core * near + low : (core + 1) * near]
                     if core == 0:
-                        own_ref[:low, cols] = top
-                        own_ref[low:, cols] = bottom
-                    else:
-                        sent_ref[which, :low, cols] = top.astype(sent_ref.dtype)
-                        sent_ref[which, low:, cols] = bottom.astype(sent_ref.dtype)
+                        own_ref[which, :low, cols] = top
+                        own_ref[which, low:, cols] = bottom
+                    ref = (kept_ref, sent_ref)[core]
+                    ref[which, :low, cols] = top.astype(ref.dtype)
+                    ref[which, low:, cols] = bottom.astype(ref.dtype)
 
 
 def call(kernel, operands, outs, pairs, products, head_dim, in_specs=None, scratch=()):
@@ -398,7 +423,7 @@
             part, "seq", [(s, s - COLUMNS * d) for s in range(COLUMNS * d, seq_count)]
         )
 
-    mine, theirs, pair_mine, pair_theirs, mask = pick_pair(layout.T, keys, values)
+    mine, theirs, pair_mine, pair_theirs, block = pick_pair(layout.T, keys, values)
     own_pair = jnp.stack([pair_mine, hop(pair_theirs, 0, 1)])
     climbed = [climb(own_pair, d) for d in range(1, levels)]
     column = jnp.stack(climbed)
@@ -406,7 +431,7 @@
     near_parts = list(chip_parts)
     for group in range(1, groups):
         near_parts += [hop(part, 0, CORES * group) for part in chip_parts]
-    sent_pair, _ = lax.optimization_barrier((own_pair, climbed[0]))
+    sent_pair, _ = lax.optimization_barrier((own_pair, chip_parts[1]))
     cross_pairs = [hop(sent_pair, 1, CORES * group) for group in range(groups)]
     column, cross_pairs, near_parts = lax.optimization_barrier((column, cross_pairs, near_parts))
     near_parts = [part.reshape(2, near, half) for part in near_parts]
@@ -418,8 +443,10 @@
     def rows_out(dtype):
         return pltpu.VMEM((tok_rows, half), dtype)
 
-    near_out = pltpu.VMEM((near, half), jnp.float32)
-    far_out = jax.ShapeDtypeStruct((levels,) + own_pair.shape, jnp.bfloat16)
+    def far_out(count):
+        return pltpu.VMEM((count,) + own_pair.shape, jnp.bfloat16)
+
+    low = (levels + 1) // 2
     near_pairs = HEADS // CORES * tok_rows * members * near
     far_width = members * seq_count * part_tok
     far_pairs = HEADS // CORES * tok_rows * far_width
@@ -442,46 +469,50 @@
     for group, cross_pair in zip(crossing, cross_pairs):
         (same, other), _ = lax.optimization_barrier((group, near_stat))
         far_parts += [own_pair, same, cross_pair, other]
-    attended, far_gq, level, drift, own_grad, cross_grad = call(
-        functools.partial(far_kernel, groups, head_dim, *far_plan),
+    attended, far_gq, level, drift, own_low, own_high, cross_low, cross_high = call(
+        functools.partial(far_kernel, groups, levels, head_dim, *far_plan),
         [queries, grad_out, near_sum, near_stat] + far_parts,
-        [rows_out(jnp.bfloat16)] + [rows_out(jnp.float32)] * 3 + [far_out, far_out],
+        [rows_out(jnp.bfloat16)]
+        + [rows_out(jnp.float32)] * 3
+        + [far_out(low), far_out(levels - low)] * COLUMNS,
         far_pairs,
         5,
         head_dim,
     )
-    grad_q, near_k, near_v, near_sent = call(
+    high = hop(cross_high, 1, 0)
+    grad_q, near_own, near_kept, near_sent = call(
         functools.partial(near_backward_kernel, members, head_dim),
         [bias, queries, grad_out, level, drift, far_gq] + near_parts,
-        [rows_out(jnp.bfloat16), near_out, near_out, pltpu.VMEM((2, near, half), jnp.bfloat16)],
+        [rows_out(jnp.bfloat16), pltpu.VMEM((2, near, half), jnp.float32)]
+        + [pltpu.VMEM((2, near, half), jnp.bfloat16)] * 2,
         near_pairs,
         4,
         head_dim,
     )
-    crossed, near_k = lax.optimization_barrier((hop(cross_grad, 1, 0), near_k))
-    returned = [crossed[0]]
-    for d in range(1, levels):
-        summed = own_grad[d].astype(jnp.float32) + crossed[d].astype(jnp.float32)
-        returned.append(sink(summed.astype(jnp.bfloat16), d))
+    cross_low, near_own = lax.optimization_barrier((cross_low, near_own))
+    crossed = hop(cross_low, 1, 0)
+    high, near_own = lax.optimization_barrier((high, near_own))
+
+    def add(own, cross):
+        return (own.astype(jnp.float32) + cross.astype(jnp.float32)).astype(jnp.bfloat16)
+
+    sums = [add(own_high[d - low], high[d - low]) for d in range(low, levels)]
+    attended, grad_q, near_sent, _ = lax.optimization_barrier(
+        (attended, grad_q, near_sent, crossed)
+    )
+    sums = [add(own_low[d], crossed[d]) for d in range(1, low)] + sums
+    returned = [sink(part, d) for d, part in enumerate(sums, 1)] + [crossed[0]]
     near_theirs = hop(near_sent, 0, 1)
-    attended, grad_q = join([(attended, hop(attended, 0, 1)), (grad_q, hop(grad_q, 0, 1))])
-    returned, attended, grad_q = lax.optimization_barrier((returned, attended, grad_q))
+    attended, grad_q, grad_k, grad_v = join(
+        [attended, hop(attended, 0, 1), grad_q, hop(grad_q, 0, 1), near_kept, near_theirs],
+        [(tok_rows, feat_width)] * 2 + [(near, feat_width)] * 2,
+    )
+    returned, grad_k, grad_v = lax.optimization_barrier((returned, grad_k, grad_v))
     far_sent = sum(part[1].astype(jnp.float32) for part in returned).astype(jnp.bfloat16)
-    shape = (blocks, part_tok, half)
-    grad_k, grad_v = pl.pallas_call(
-        finish_kernel,
-        in_specs=[WHOLE] * (5 + levels),
-        out_specs=[WHOLE] * 2,
-        out_shape=[jax.ShapeDtypeStruct(keys.shape, keys.dtype)] * 2,
-    )(
-        mask,
-        near_k.reshape(shape),
-        near_v.reshape(shape),
-        near_theirs.reshape((2,) + shape),
-        hop(far_sent, 0, 1),
-        *returned,
-    )
-    return (attended, grad_q, grad_k, grad_v)
+    grad_k, grad_v = finish(
+        [block, near_own, near_theirs, hop(far_sent, 0, 1)] + returned, [grad_k, grad_v]
+    )
+    return (attended, grad_q, grad_k.reshape(keys.shape), grad_v.reshape(values.shape))
 
 
 def solution(mesh):

time: 63.1 us -> 60.8 us (0.964)
  waiting for transfers between devices: 21.7 us -> 14.3 us
  local copies, waits for them, and re-layouts: 1.2 us -> 4.74 us
  starting transfers between devices: 24.4 us -> 26.6 us
  Pallas kernels: 14.5 us -> 13.3 us
    ppermute x14 -> x15, waiting for transfers between devices: 16.2 us -> 11.6 us  [hop(): return lax.ppermute(part, ('seq', 'kv'), pairs)]
    unnamed x18 -> x16, local copies, waits for them, and re-layouts: 1.19 us -> 4.73 us
    ppermute x3, waiting for transfers between devices: 5.48 us -> 2.62 us  [sink(): lax.ppermute(part, 'seq', [(s, s - COLUMNS * d) for s in range(COLUMNS *...]
    ppermute x14 -> x15, starting transfers between devices: 11.9 us -> 13.3 us  [hop(): return lax.ppermute(part, ('seq', 'kv'), pairs)]
    pallas_call x1, Pallas kernels: 2.14 us -> 0.78 us  [finish(): pl.pallas_call(finish_kernel, in_specs=[WHOLE] * len(operands) + [IN_HBM]...]
  transfers between devices with their start and end apart: 20 -> 21, of which waited for: 9 -> 9; matrix products, arithmetic and copies ran while one was open for 0% -> 1% of each run, Pallas kernels for 7% -> 7%
where the time goes in v6:
time: 60.8 us; the launch traced here: 60.4 us
  starting transfers between devices  26.6 us (44%)
  waiting for transfers between devices  14.3 us (24%)
  Pallas kernels  13.3 us (22%)
  local copies, waits for them, and re-layouts  4.74 us (8%)
  between operations  0.85 us (1%)
  other arithmetic  0.72 us (1%)
    ppermute x15, starting transfers between devices, hop(): return lax.ppermute(part, ('seq', 'kv'), pairs)  13.3 us
    ppermute x15, waiting for transfers between devices, hop(): return lax.ppermute(part, ('seq', 'kv'), pairs)  11.6 us
    pallas_call x3, Pallas kernels, call(): pl.pallas_call(kernel, in_specs=in_specs or [WHOLE] * len(operands), out_...  9.71 us
    ppermute x3, starting transfers between devices, climb(): lax.ppermute(part, 'seq', [(s, s + COLUMNS * d) for s in range(seq_count...  9.27 us
    unnamed x16, local copies, waits for them, and re-layouts  4.73 us
    ppermute x3, starting transfers between devices, sink(): lax.ppermute(part, 'seq', [(s, s - COLUMNS * d) for s in range(COLUMNS *...  4 us
    ppermute x3, waiting for transfers between devices, sink(): lax.ppermute(part, 'seq', [(s, s - COLUMNS * d) for s in range(COLUMNS *...  2.62 us
    pallas_call x1, Pallas kernels, join(): pl.pallas_call(join_kernel, in_specs=[WHOLE] * len(operands), out_specs=[...  1.54 us
  transfers between devices with their start and end apart: 21, of which 9 were waited for; matrix products, arithmetic and copies ran while one was open for 1% of the time, Pallas kernels for 7%

profile of v6, /device:TPU:0, one launch (start us, length us, event | category | flops | bytes accessed | tf_op | source)
XLA Modules:
  0.0 60.4 jit_solution(8874671409691048579)
XLA Ops:
  0.6 1.2 %shard_map.84 = (bf16[2,8,16,512]{3,2,1,0:T(8,128)(2,1)S(1)}, bf16[2,8,16,512]{3,2,1,0:T(8,128)(2,1)S(1)}, bf16[2,16,512]{2,1,0:T(8,128)(2,1)S(1)}, bf16[2,16,512]{2,1,0:T(8,128)(2,1)S(1)}, f32[8,128]{1,0:T(8,128)S(1)}) custom-call(s32[15,64]{1,0:T(8,128)} %bitcast.37, bf16[8,16,1024]{2,1,0:T(8,128)(2,1)} %keys_hbm.1, bf16[8,16,1024]{2,1,0:T(8,128)(2,1)} %values_hbm.1), custom_call_target="tpu_custom_call" | custom-call | tf_op jit(solution)/shard_map/pallas_call | solution.py:73
  2.5 2.9 %collective-permute-start.7 = (bf16[2,8,16,512]{3,2,1,0:T(8,128)(2,1)S(1)}, bf16[2,8,16,512]{3,2,1,0:T(8,128)(2,1)S(1)}, u32[]{:S(2)}, u32[]{:S(2)}) collective-permute-start(bf16[2,8,16,512]{3,2,1,0:T(8,128)(2,1)S(1)} %get-tuple-element.62), channel_id=1, source_target_pairs={{0,2},{1,3},{2,0},{3,1},{4,6},{5,7},{6,4},{7,5},{8,10},{9,11},{10,... | collective-permute-start | bytes 786440 | tf_op jit(solution)/shard_map/ppermute | solution.py:414
  5.4 1.0 %collective-permute-start.8 = (bf16[2,8,16,512]{3,2,1,0:T(8,128)(2,1)S(1)}, bf16[2,8,16,512]{3,2,1,0:T(8,128)(2,1)S(1)}, u32[]{:S(2)}, u32[]{:S(2)}) collective-permute-start(bf16[2,8,16,512]{3,2,1,0:T(8,128)(2,1)S(1)} %collective-permute-done.4), channel_id=1, source_target_pairs={{0,2},{1,3},{2,0},{3,1},{4,6},{5,7},{6,4},{7,5},{8,10},{9,11},{10,... | collective-permute-start | bytes 786440 | tf_op jit(solution)/shard_map/ppermute | solution.py:414
  6.4 5.5 %collective-permute-start.3 = (bf16[2,2,16,512]{3,2,1,0:T(8,128)(2,1)S(1)}, bf16[2,2,16,512]{3,2,1,0:T(8,128)(2,1)S(1)}, u32[]{:S(2)}, u32[]{:S(2)}) collective-permute-start(bf16[2,2,16,512]{3,2,1,0:T(8,128)(2,1)S(1)} %pad_maximum_fusion.1.refs_0_.refs_4_), channel_id=1, source_target_pairs={{0,24},{4,28},{1,25},{5,29},{2,26},{6,30},{3,27},{7,31}} | collective-permute-start | bytes 196616 | tf_op jit(solution)/shard_map/ppermute | solution.py:417
  12.0 1.3 %collective-permute-start.2 = (bf16[2,2,16,512]{3,2,1,0:T(8,128)(2,1)S(1)}, bf16[2,2,16,512]{3,2,1,0:T(8,128)(2,1)S(1)}, u32[]{:S(2)}, u32[]{:S(2)}) collective-permute-start(bf16[2,2,16,512]{3,2,1,0:T(8,128)(2,1)S(1)} %pad_maximum_fusion.1.refs_0_.refs_4_), channel_id=1, source_target_pairs={{0,16},{4,20},{8,24},{12,28},{1,17},{5,21},{9,25},{13,29},{2,18},{... | collective-permute-start | bytes 196616 | tf_op jit(solution)/shard_map/ppermute | solution.py:417
  13.3 2.5 %collective-permute-start.1 = (bf16[2,2,16,512]{3,2,1,0:T(8,128)(2,1)S(1)}, bf16[2,2,16,512]{3,2,1,0:T(8,128)(2,1)S(1)}, u32[]{:S(2)}, u32[]{:S(2)}) collective-permute-start(bf16[2,2,16,512]{3,2,1,0:T(8,128)(2,1)S(1)} %pad_maximum_fusion.1.refs_0_.refs_4_), channel_id=1, source_target_pairs={{0,8},{4,12},{8,16},{12,20},{16,24},{20,28},{1,9},{5,13},{9,17},{1... | collective-permute-start | bytes 196616 | tf_op jit(solution)/shard_map/ppermute | solution.py:417
  15.8 2.0 %collective-permute-start.6 = (bf16[2,2,16,512]{3,2,1,0:T(8,128)(2,1)S(1)}, bf16[2,2,16,512]{3,2,1,0:T(8,128)(2,1)S(1)}, u32[]{:S(2)}, u32[]{:S(2)}) collective-permute-start(bf16[2,2,16,512]{3,2,1,0:T(8,128)(2,1)S(1)} %pad_maximum_fusion.1.refs_0_.refs_4_), channel_id=1, source_target_pairs={{0,6},{1,7},{2,4},{3,5},{4,2},{5,3},{6,0},{7,1},{8,14},{9,15},{10,... | collective-permute-start | bytes 196616 | tf_op jit(solution)/shard_map/ppermute | solution.py:414
  18.3 2.9 %collective-permute-done.6.refs_6_ = bf16[2,2,16,512]{3,2,1,0:T(8,128)(2,1)S(1)} collective-permute-done((bf16[2,2,16,512]{3,2,1,0:T(8,128)(2,1)S(1)}, bf16[2,2,16,512]{3,2,1,0:T(8,128)(2,1)S(1)}, u32[]{:S(2)}, u32[]{:S(2)}) %collective-permute-start.6) | collective-permute-done | bytes 65568 | tf_op jit(solution)/shard_map/ppermute | solution.py:414
  21.2 0.8 %collective-permute-done.5.refs_2_ = bf16[2,2,16,512]{3,2,1,0:T(8,128)(2,1)S(1)} collective-permute-done((bf16[2,2,16,512]{3,2,1,0:T(8,128)(2,1)S(1)}, bf16[2,2,16,512]{3,2,1,0:T(8,128)(2,1)S(1)}, u32[]{:S(2)}, u32[]{:S(2)}) %collective-permute-start.5) | collective-permute-done | bytes 65568 | tf_op jit(solution)/shard_map/ppermute | solution.py:414
  22.0 1.2 %collective-permute-start.11 = (bf16[3,2,2,16,512]{4,3,2,1,0:T(8,128)(2,1)S(1)}, bf16[3,2,2,16,512]{4,3,2,1,0:T(8,128)(2,1)S(1)}, u32[]{:S(2)}, u32[]{:S(2)}) collective-permute-start(bf16[3,2,2,16,512]{4,3,2,1,0:T(8,128)(2,1)S(1)} %pad_maximum_fusion.refs_1_), channel_id=1, source_target_pairs={{0,6},{1,7},{2,4},{3,5},{4,2},{5,3},{6,0},{7,1},{8,14},{9,15},{10,... | collective-permute-start | bytes 589832 | tf_op jit(solution)/shard_map/ppermute | solution.py:414
  23.2 1.0 %collective-permute-start.10 = (bf16[3,2,2,16,512]{4,3,2,1,0:T(8,128)(2,1)S(1)}, bf16[3,2,2,16,512]{4,3,2,1,0:T(8,128)(2,1)S(1)}, u32[]{:S(2)}, u32[]{:S(2)}) collective-permute-start(bf16[3,2,2,16,512]{4,3,2,1,0:T(8,128)(2,1)S(1)} %pad_maximum_fusion.refs_1_), channel_id=1, source_target_pairs={{0,2},{1,3},{2,0},{3,1},{4,6},{5,7},{6,4},{7,5},{8,10},{9,11},{10,... | collective-permute-start | bytes 589832 | tf_op jit(solution)/shard_map/ppermute | solution.py:414
  24.2 1.3 %collective-permute-start.9 = (bf16[3,2,2,16,512]{4,3,2,1,0:T(8,128)(2,1)S(1)}, bf16[3,2,2,16,512]{4,3,2,1,0:T(8,128)(2,1)S(1)}, u32[]{:S(2)}, u32[]{:S(2)}) collective-permute-start(bf16[3,2,2,16,512]{4,3,2,1,0:T(8,128)(2,1)S(1)} %pad_maximum_fusion.refs_1_), channel_id=1, source_target_pairs={{0,4},{1,5},{2,6},{3,7},{4,0},{5,1},{6,2},{7,3},{8,12},{9,13},{10,... | collective-permute-start | bytes 589832 | tf_op jit(solution)/shard_map/ppermute | solution.py:414
  25.5 2.7 %shard_map.85 = (f32[512,512]{1,0:T(8,128)S(1)}, f32[512,512]{1,0:T(8,128)S(1)}, f32[512,512]{1,0:T(8,128)S(1)}, bf16[512,512]{1,0:T(8,128)(2,1)S(1)}, bf16[512,512]{1,0:T(8,128)(2,1)S(1)}) custom-call(bf16[512,1024]{1,0:T(8,128)(2,1)} %q_hbm.1, bf16[512,1024]{1,0:T(8,128)(2,1)} %g_hbm.1, bf16[2,128,512]{2,1,0:T(8,128)(2,1)S(1)} %bitcast.23, ...), custom_call_target="tpu_custom_call" | custom-call | flops 1073741824 | bytes 3145728 | tf_op jit(solution)/shard_map/pallas_call | solution.py:383
  28.2 1.2 %collective-permute-done.11.refs_7_ = bf16[3,2,2,16,512]{4,3,2,1,0:T(8,128)(2,1)S(1)} collective-permute-done((bf16[3,2,2,16,512]{4,3,2,1,0:T(8,128)(2,1)S(1)}, bf16[3,2,2,16,512]{4,3,2,1,0:T(8,128)(2,1)S(1)}, u32[]{:S(2)}, u32[]{:S(2)}) %collective-permute-start.11) | collective-permute-done | bytes 196640 | tf_op jit(solution)/shard_map/ppermute | solution.py:414
  29.5 2.0 %collective-permute-done.10.refs_5_ = bf16[3,2,2,16,512]{4,3,2,1,0:T(8,128)(2,1)S(1)} collective-permute-done((bf16[3,2,2,16,512]{4,3,2,1,0:T(8,128)(2,1)S(1)}, bf16[3,2,2,16,512]{4,3,2,1,0:T(8,128)(2,1)S(1)}, u32[]{:S(2)}, u32[]{:S(2)}) %collective-permute-start.10) | collective-permute-done | bytes 196640 | tf_op jit(solution)/shard_map/ppermute | solution.py:414
  32.0 4.5 %shard_map.86 = (bf16[512,512]{1,0:T(8,128)(2,1)S(1)}, f32[512,512]{1,0:T(8,128)S(1)}, f32[512,512]{1,0:T(8,128)S(1)}, f32[512,512]{1,0:T(8,128)S(1)}, bf16[2,2,...) custom-call(bf16[512,512]{1,0:T(8,128)(2,1)S(1)} %get-tuple-element., ...), custom_call_target="tpu_custom_call" | custom-call | flops 2684354560 | bytes 4194304 | tf_op jit(solution)/shard_map/pallas_call | solution.py:383
  36.6 2.4 %shard_map.87 = (bf16[512,512]{1,0:T(8,128)(2,1)S(1)}, f32[2,128,512]{2,1,0:T(8,128)S(1)}, bf16[2,128,512]{2,1,0:T(8,128)(2,1)S(1)}, bf16[2,128,512]{2,1,0:T(8,128)(2,1)S(1)}) custom-call(f32[512,512]{1,0:T(8,128)S(1)} %get-tuple-element.78.bias_ref, bf16[512,512]{1,0:T(8,128)(2,1)S(1)} %get-tuple-element.66.q_ref, ...), custom_call_target="tpu_custom_call" | custom-call | flops 2147483648 | bytes 6291456 | tf_op jit(solution)/shard_map/pallas_call | solution.py:383
  39.6 1.5 %collective-permute-start.16 = (bf16[2,2,2,16,512]{4,3,2,1,0:T(8,128)(2,1)S(1)}, bf16[2,2,2,16,512]{4,3,2,1,0:T(8,128)(2,1)S(1)}, u32[]{:S(2)}, u32[]{:S(2)}) collective-permute-start(bf16[2,2,2,16,512]{4,3,2,1,0:T(8,128)(2,1)S(1)} %get-tuple-element.94), channel_id=1, source_target_pairs={{0,4},{1,5},{2,6},{3,7},{4,0},{5,1},{6,2},{7,3},{8,12},{9,13},{10,... | collective-permute-start | bytes 393224 | tf_op jit(solution)/shard_map/ppermute | solution.py:414
  41.1 2.9 %collective-permute-done.12 = bf16[2,2,2,16,512]{4,3,2,1,0:T(8,128)(2,1)S(1)} collective-permute-done((bf16[2,2,2,16,512]{4,3,2,1,0:T(8,128)(2,1)S(1)}, bf16[2,2,2,16,512]{4,3,2,1,0:T(8,128)(2,1)S(1)}, u32[]{:S(2)}, u32[]{:S(2)}) %collective-permute-start.12) | collective-permute-done | bytes 131104 | tf_op jit(solution)/shard_map/ppermute | solution.py:414
  44.7 1.4 %collective-permute-start.17 = (bf16[2,2,16,512]{3,2,1,0:T(8,128)(2,1)S(1)}, bf16[2,2,16,512]{3,2,1,0:T(8,128)(2,1)S(1)}, u32[]{:S(2)}, u32[]{:S(2)}) collective-permute-start(bf16[2,2,16,512]{3,2,1,0:T(8,128)(2,1)S(1)} %fusion), channel_id=1, source_target_pairs={{8,0},{12,4},{16,8},{20,12},{24,16},{28,20},{9,1},{13,5},{17,9},{2... | collective-permute-start | bytes 196616 | tf_op jit(solution)/shard_map/ppermute | solution.py:422
  46.1 0.7 %fusion.2 = (bf16[2,2,16,512]{3,2,1,0:T(8,128)(2,1)}, bf16[2,2,16,512]{3,2,1,0:T(8,128)(2,1)S(1)}) fusion(bf16[2,2,2,16,512]{4,3,2,1,0:T(8,128)(2,1)S(1)} %collective-permute-done.16, bf16[2,2,2,16,512]{4,3,2,1,0:T(8,128)(2,1)S(1)} %get-tuple-element.98), kind=kLoop, calls=%fused_computation.6 | loop fusion | flops 262144 | bytes 393216 | tf_op jit(solution)/shard_map/convert_element_type | solution.py:497
  46.8 1.3 %collective-permute-start.19 = (bf16[2,2,16,512]{3,2,1,0:T(8,128)(2,1)}, bf16[2,2,16,512]{3,2,1,0:T(8,128)(2,1)S(1)}, u32[]{:S(2)}, u32[]{:S(2)}) collective-permute-start(bf16[2,2,16,512]{3,2,1,0:T(8,128)(2,1)} %get-tuple-element.110), channel_id=1, source_target_pairs={{24,0},{28,4},{25,1},{29,5},{26,2},{30,6},{27,3},{31,7}} | collective-permute-start | bytes 196616 | tf_op jit(solution)/shard_map/ppermute | solution.py:422
  48.1 1.3 %collective-permute-start.18 = (bf16[2,2,16,512]{3,2,1,0:T(8,128)(2,1)S(1)}, bf16[2,2,16,512]{3,2,1,0:T(8,128)(2,1)S(1)}, u32[]{:S(2)}, u32[]{:S(2)}) collective-permute-start(bf16[2,2,16,512]{3,2,1,0:T(8,128)(2,1)S(1)} %get-tuple-element.111), channel_id=1, source_target_pairs={{16,0},{20,4},{24,8},{28,12},{17,1},{21,5},{25,9},{29,13},{18,2},{... | collective-permute-start | bytes 196616 | tf_op jit(solution)/shard_map/ppermute | solution.py:422
  49.4 0.8 %copy-done.4 = bf16[512,512]{1,0:T(8,128)(2,1)} copy-done((bf16[512,512]{1,0:T(8,128)(2,1)}, bf16[512,512]{1,0:T(8,128)(2,1)S(1)}, u32[]{:S(2)}) %copy-start.4) | copy-done | bytes 524312
  50.2 0.8 %copy-done.6 = bf16[512,512]{1,0:T(8,128)(2,1)} copy-done((bf16[512,512]{1,0:T(8,128)(2,1)}, bf16[512,512]{1,0:T(8,128)(2,1)S(1)}, u32[]{:S(2)}) %copy-start.6) | copy-done | bytes 524312
  51.0 1.0 %copy-done.3 = bf16[512,512]{1,0:T(8,128)(2,1)S(1)} copy-done((bf16[512,512]{1,0:T(8,128)(2,1)S(1)}, bf16[512,512]{1,0:T(8,128)(2,1)}, u32[]{:S(2)}) %copy-start.3) | copy-done | bytes 524312
  52.1 1.0 %copy-done.5 = bf16[512,512]{1,0:T(8,128)(2,1)S(1)} copy-done((bf16[512,512]{1,0:T(8,128)(2,1)S(1)}, bf16[512,512]{1,0:T(8,128)(2,1)}, u32[]{:S(2)}) %copy-start.5) | copy-done | bytes 524312
  53.1 1.0 %copy-done.7 = bf16[512,512]{1,0:T(8,128)(2,1)S(1)} copy-done((bf16[512,512]{1,0:T(8,128)(2,1)S(1)}, bf16[512,512]{1,0:T(8,128)(2,1)}, u32[]{:S(2)}) %copy-start.7) | copy-done | bytes 524312
  54.2 1.5 %shard_map.88 = (bf16[512,1024]{1,0:T(8,128)(2,1)}, bf16[512,1024]{1,0:T(8,128)(2,1)}, bf16[128,1024]{1,0:T(8,128)(2,1)}, bf16[128,1024]{1,0:T(8,128)(2,1)}) custom-call(bf16[512,512]{1,0:T(8,128)(2,1)S(1)} %copy-done.1, bf16[512,512]{1,0:T(8,128)(2,1)S(1)} %copy-done.5, bf16[512,512]{1,0:T(8,128)(2,1)S(1)} %copy-done.3, bf16[512,512]{1,0:T(8,128)(2,1)S(1)} %copy-done.7, ...), custom_call_target="tpu_custom_call" | custom-call | tf_op jit(solution)/shard_map/pallas_call | solution.py:105
  56.4 2.0 %collective-permute-done.18.refs_1_ = bf16[2,2,16,512]{3,2,1,0:T(8,128)(2,1)S(1)} collective-permute-done((bf16[2,2,16,512]{3,2,1,0:T(8,128)(2,1)S(1)}, bf16[2,2,16,512]{3,2,1,0:T(8,128)(2,1)S(1)}, u32[]{:S(2)}, u32[]{:S(2)}) %collective-permute-start.18) | collective-permute-done | bytes 65568 | tf_op jit(solution)/shard_map/ppermute | solution.py:422
  58.4 1.2 %collective-permute-done.20.far_ref = bf16[2,16,512]{2,1,0:T(8,128)(2,1)S(1)} collective-permute-done((bf16[2,16,512]{2,1,0:T(8,128)(2,1)S(1)}, bf16[2,16,512]{2,1,0:T(8,128)(2,1)S(1)}, u32[]{:S(2)}, u32[]{:S(2)}) %collective-permute-start.20) | collective-permute-done | bytes 32800 | tf_op jit(solution)/shard_map/ppermute | solution.py:414
  59.6 0.8 %shard_map.89 = (bf16[128,1024]{1,0:T(8,128)(2,1)}, bf16[128,1024]{1,0:T(8,128)(2,1)}) custom-call(f32[8,128]{1,0:T(8,128)S(1)} %get-tuple-element.93.block_ref, f32[2,128,512]{2,1,0:T(8,128)S(1)} %get-tuple-element.96.near_ref, bf16[2,128,512]{2,1,0:T(8,128)(2,1)S(1)} %collective-permute-done.15.near_far.near_far_ref, ...), custom_call_target="tpu_custom_call", output_to_operand_aliasing={{0}: (8, {}), {1}: (9, {})} | custom-call | tf_op jit(solution)/shard_map/pallas_call | solution.py:140
  (38 shorter events, 3.7 us)
Async XLA Ops:
  1.9 3.5 %collective-permute-start.4 = (bf16[2,8,16,512]{3,2,1,0:T(8,128)(2,1)S(1)}, bf16[2,8,16,512]{3,2,1,0:T(8,128)(2,1)S(1)}, u32[]{:S(2)}, u32[]{:S(2)}) collective-permute-start(bf16[2,8,16,512]{3,2,1,0:T(8,128)(2,1)S(1)} %get-tuple-element.59), channel_id=1, source_target_pairs={{0,1},{1,0},{2,3},{3,2},{4,5},{5,4},{6,7},{7,6},{8,9},{9,8},{10,11... | collective-permute-start | bytes 786440 | tf_op jit(solution)/shard_map/ppermute | solution.py:414
  2.4 4.1 %collective-permute-start = (bf16[2,16,512]{2,1,0:T(8,128)(2,1)S(1)}, bf16[2,16,512]{2,1,0:T(8,128)(2,1)S(1)}, u32[]{:S(2)}, u32[]{:S(2)}) collective-permute-start(bf16[2,16,512]{2,1,0:T(8,128)(2,1)S(1)} %get-tuple-element.58), channel_id=1, source_target_pairs={{0,1},{1,0},{2,3},{3,2},{4,5},{5,4},{6,7},{7,6},{8,9},{9,8},{10,11... | collective-permute-start | bytes 98312 | tf_op jit(solution)/shard_map/ppermute | solution.py:414
  2.5 15.9 %collective-permute-start.7 = (bf16[2,8,16,512]{3,2,1,0:T(8,128)(2,1)S(1)}, bf16[2,8,16,512]{3,2,1,0:T(8,128)(2,1)S(1)}, u32[]{:S(2)}, u32[]{:S(2)}) collective-permute-start(bf16[2,8,16,512]{3,2,1,0:T(8,128)(2,1)S(1)} %get-tuple-element.62), channel_id=1, source_target_pairs={{0,2},{1,3},{2,0},{3,1},{4,6},{5,7},{6,4},{7,5},{8,10},{9,11},{10,... | collective-permute-start | bytes 786440 | tf_op jit(solution)/shard_map/ppermute | solution.py:414
  5.4 16.6 %collective-permute-start.8 = (bf16[2,8,16,512]{3,2,1,0:T(8,128)(2,1)S(1)}, bf16[2,8,16,512]{3,2,1,0:T(8,128)(2,1)S(1)}, u32[]{:S(2)}, u32[]{:S(2)}) collective-permute-start(bf16[2,8,16,512]{3,2,1,0:T(8,128)(2,1)S(1)} %collective-permute-done.4), channel_id=1, source_target_pairs={{0,2},{1,3},{2,0},{3,1},{4,6},{5,7},{6,4},{7,5},{8,10},{9,11},{10,... | collective-permute-start | bytes 786440 | tf_op jit(solution)/shard_map/ppermute | solution.py:414
  6.4 9.3 %collective-permute-start.3 = (bf16[2,2,16,512]{3,2,1,0:T(8,128)(2,1)S(1)}, bf16[2,2,16,512]{3,2,1,0:T(8,128)(2,1)S(1)}, u32[]{:S(2)}, u32[]{:S(2)}) collective-permute-start(bf16[2,2,16,512]{3,2,1,0:T(8,128)(2,1)S(1)} %pad_maximum_fusion.1.refs_0_.refs_4_), channel_id=1, source_target_pairs={{0,24},{4,28},{1,25},{5,29},{2,26},{6,30},{3,27},{7,31}} | collective-permute-start | bytes 196616 | tf_op jit(solution)/shard_map/ppermute | solution.py:417
  12.0 5.8 %collective-permute-start.2 = (bf16[2,2,16,512]{3,2,1,0:T(8,128)(2,1)S(1)}, bf16[2,2,16,512]{3,2,1,0:T(8,128)(2,1)S(1)}, u32[]{:S(2)}, u32[]{:S(2)}) collective-permute-start(bf16[2,2,16,512]{3,2,1,0:T(8,128)(2,1)S(1)} %pad_maximum_fusion.1.refs_0_.refs_4_), channel_id=1, source_target_pairs={{0,16},{4,20},{8,24},{12,28},{1,17},{5,21},{9,25},{13,29},{2,18},{... | collective-permute-start | bytes 196616 | tf_op jit(solution)/shard_map/ppermute | solution.py:417
  13.3 5.0 %collective-permute-start.1 = (bf16[2,2,16,512]{3,2,1,0:T(8,128)(2,1)S(1)}, bf16[2,2,16,512]{3,2,1,0:T(8,128)(2,1)S(1)}, u32[]{:S(2)}, u32[]{:S(2)}) collective-permute-start(bf16[2,2,16,512]{3,2,1,0:T(8,128)(2,1)S(1)} %pad_maximum_fusion.1.refs_0_.refs_4_), channel_id=1, source_target_pairs={{0,8},{4,12},{8,16},{12,20},{16,24},{20,28},{1,9},{5,13},{9,17},{1... | collective-permute-start | bytes 196616 | tf_op jit(solution)/shard_map/ppermute | solution.py:417
  15.8 5.5 %collective-permute-start.6 = (bf16[2,2,16,512]{3,2,1,0:T(8,128)(2,1)S(1)}, bf16[2,2,16,512]{3,2,1,0:T(8,128)(2,1)S(1)}, u32[]{:S(2)}, u32[]{:S(2)}) collective-permute-start(bf16[2,2,16,512]{3,2,1,0:T(8,128)(2,1)S(1)} %pad_maximum_fusion.1.refs_0_.refs_4_), channel_id=1, source_target_pairs={{0,6},{1,7},{2,4},{3,5},{4,2},{5,3},{6,0},{7,1},{8,14},{9,15},{10,... | collective-permute-start | bytes 196616 | tf_op jit(solution)/shard_map/ppermute | solution.py:414
  17.8 4.3 %collective-permute-start.5 = (bf16[2,2,16,512]{3,2,1,0:T(8,128)(2,1)S(1)}, bf16[2,2,16,512]{3,2,1,0:T(8,128)(2,1)S(1)}, u32[]{:S(2)}, u32[]{:S(2)}) collective-permute-start(bf16[2,2,16,512]{3,2,1,0:T(8,128)(2,1)S(1)} %pad_maximum_fusion.1.refs_0_.refs_4_), channel_id=1, source_target_pairs={{0,4},{1,5},{2,6},{3,7},{4,0},{5,1},{6,2},{7,3},{8,12},{9,13},{10,... | collective-permute-start | bytes 196616 | tf_op jit(solution)/shard_map/ppermute | solution.py:414
  22.0 7.5 %collective-permute-start.11 = (bf16[3,2,2,16,512]{4,3,2,1,0:T(8,128)(2,1)S(1)}, bf16[3,2,2,16,512]{4,3,2,1,0:T(8,128)(2,1)S(1)}, u32[]{:S(2)}, u32[]{:S(2)}) collective-permute-start(bf16[3,2,2,16,512]{4,3,2,1,0:T(8,128)(2,1)S(1)} %pad_maximum_fusion.refs_1_), channel_id=1, source_target_pairs={{0,6},{1,7},{2,4},{3,5},{4,2},{5,3},{6,0},{7,1},{8,14},{9,15},{10,... | collective-permute-start | bytes 589832 | tf_op jit(solution)/shard_map/ppermute | solution.py:414
  23.2 8.3 %collective-permute-start.10 = (bf16[3,2,2,16,512]{4,3,2,1,0:T(8,128)(2,1)S(1)}, bf16[3,2,2,16,512]{4,3,2,1,0:T(8,128)(2,1)S(1)}, u32[]{:S(2)}, u32[]{:S(2)}) collective-permute-start(bf16[3,2,2,16,512]{4,3,2,1,0:T(8,128)(2,1)S(1)} %pad_maximum_fusion.refs_1_), channel_id=1, source_target_pairs={{0,2},{1,3},{2,0},{3,1},{4,6},{5,7},{6,4},{7,5},{8,10},{9,11},{10,... | collective-permute-start | bytes 589832 | tf_op jit(solution)/shard_map/ppermute | solution.py:414
  24.2 7.8 %collective-permute-start.9 = (bf16[3,2,2,16,512]{4,3,2,1,0:T(8,128)(2,1)S(1)}, bf16[3,2,2,16,512]{4,3,2,1,0:T(8,128)(2,1)S(1)}, u32[]{:S(2)}, u32[]{:S(2)}) collective-permute-start(bf16[3,2,2,16,512]{4,3,2,1,0:T(8,128)(2,1)S(1)} %pad_maximum_fusion.refs_1_), channel_id=1, source_target_pairs={{0,4},{1,5},{2,6},{3,7},{4,0},{5,1},{6,2},{7,3},{8,12},{9,13},{10,... | collective-permute-start | bytes 589832 | tf_op jit(solution)/shard_map/ppermute | solution.py:414
  36.6 7.5 %copy-start = (bf16[512,512]{1,0:T(8,128)(2,1)}, bf16[512,512]{1,0:T(8,128)(2,1)S(1)}, u32[]{:S(2)}) copy-start(bf16[512,512]{1,0:T(8,128)(2,1)S(1)} %get-tuple-element.87.att_ref) | copy-start | bytes 1572868
  39.0 10.4 %copy-start.2 = (bf16[512,512]{1,0:T(8,128)(2,1)}, bf16[512,512]{1,0:T(8,128)(2,1)S(1)}, u32[]{:S(2)}) copy-start(bf16[512,512]{1,0:T(8,128)(2,1)S(1)} %get-tuple-element.88.gq_ref) | copy-start | bytes 1572868
  39.1 5.0 %collective-permute-start.12 = (bf16[2,2,2,16,512]{4,3,2,1,0:T(8,128)(2,1)S(1)}, bf16[2,2,2,16,512]{4,3,2,1,0:T(8,128)(2,1)S(1)}, u32[]{:S(2)}, u32[]{:S(2)}) collective-permute-start(bf16[2,2,2,16,512]{4,3,2,1,0:T(8,128)(2,1)S(1)} %get-tuple-element.86), channel_id=1, source_target_pairs={{0,4},{1,5},{2,6},{3,7},{4,0},{5,1},{6,2},{7,3},{8,12},{9,13},{10,... | collective-permute-start | bytes 393224 | tf_op jit(solution)/shard_map/ppermute | solution.py:414
  39.6 6.5 %collective-permute-start.16 = (bf16[2,2,2,16,512]{4,3,2,1,0:T(8,128)(2,1)S(1)}, bf16[2,2,2,16,512]{4,3,2,1,0:T(8,128)(2,1)S(1)}, u32[]{:S(2)}, u32[]{:S(2)}) collective-permute-start(bf16[2,2,2,16,512]{4,3,2,1,0:T(8,128)(2,1)S(1)} %get-tuple-element.94), channel_id=1, source_target_pairs={{0,4},{1,5},{2,6},{3,7},{4,0},{5,1},{6,2},{7,3},{8,12},{9,13},{10,... | collective-permute-start | bytes 393224 | tf_op jit(solution)/shard_map/ppermute | solution.py:414
  44.1 4.0 %collective-permute-start.15 = (bf16[2,128,512]{2,1,0:T(8,128)(2,1)S(1)}, bf16[2,128,512]{2,1,0:T(8,128)(2,1)S(1)}, u32[]{:S(2)}, u32[]{:S(2)}) collective-permute-start(bf16[2,128,512]{2,1,0:T(8,128)(2,1)S(1)} %get-tuple-element.90), channel_id=1, source_target_pairs={{0,1},{1,0},{2,3},{3,2},{4,5},{5,4},{6,7},{7,6},{8,9},{9,8},{10,11... | collective-permute-start | bytes 786440 | tf_op jit(solution)/shard_map/ppermute | solution.py:414
  44.1 5.3 %collective-permute-start.13 = (bf16[512,512]{1,0:T(8,128)(2,1)S(1)}, bf16[512,512]{1,0:T(8,128)(2,1)S(1)}, u32[]{:S(2)}, u32[]{:S(2)}) collective-permute-start(bf16[512,512]{1,0:T(8,128)(2,1)S(1)} %get-tuple-element.87.att_ref), channel_id=1, source_target_pairs={{0,1},{1,0},{2,3},{3,2},{4,5},{5,4},{6,7},{7,6},{8,9},{9,8},{10,11... | collective-permute-start | bytes 1572872 | tf_op jit(solution)/shard_map/ppermute | solution.py:414
  44.6 6.4 %copy-start.1 = (bf16[512,512]{1,0:T(8,128)(2,1)S(1)}, bf16[512,512]{1,0:T(8,128)(2,1)}, u32[]{:S(2)}) copy-start(bf16[512,512]{1,0:T(8,128)(2,1)} %copy-done) | copy-start | bytes 1572868
  44.6 5.6 %collective-permute-start.14 = (bf16[512,512]{1,0:T(8,128)(2,1)S(1)}, bf16[512,512]{1,0:T(8,128)(2,1)S(1)}, u32[]{:S(2)}, u32[]{:S(2)}) collective-permute-start(bf16[512,512]{1,0:T(8,128)(2,1)S(1)} %get-tuple-element.88.gq_ref), channel_id=1, source_target_pairs={{0,1},{1,0},{2,3},{3,2},{4,5},{5,4},{6,7},{7,6},{8,9},{9,8},{10,11... | collective-permute-start | bytes 1572872 | tf_op jit(solution)/shard_map/ppermute | solution.py:414
  44.7 11.0 %collective-permute-start.17 = (bf16[2,2,16,512]{3,2,1,0:T(8,128)(2,1)S(1)}, bf16[2,2,16,512]{3,2,1,0:T(8,128)(2,1)S(1)}, u32[]{:S(2)}, u32[]{:S(2)}) collective-permute-start(bf16[2,2,16,512]{3,2,1,0:T(8,128)(2,1)S(1)} %fusion), channel_id=1, source_target_pairs={{8,0},{12,4},{16,8},{20,12},{24,16},{28,20},{9,1},{13,5},{17,9},{2... | collective-permute-start | bytes 196616 | tf_op jit(solution)/shard_map/ppermute | solution.py:422
  46.8 9.6 %collective-permute-start.19 = (bf16[2,2,16,512]{3,2,1,0:T(8,128)(2,1)}, bf16[2,2,16,512]{3,2,1,0:T(8,128)(2,1)S(1)}, u32[]{:S(2)}, u32[]{:S(2)}) collective-permute-start(bf16[2,2,16,512]{3,2,1,0:T(8,128)(2,1)} %get-tuple-element.110), channel_id=1, source_target_pairs={{24,0},{28,4},{25,1},{29,5},{26,2},{30,6},{27,3},{31,7}} | collective-permute-start | bytes 196616 | tf_op jit(solution)/shard_map/ppermute | solution.py:422
  48.1 10.3 %collective-permute-start.18 = (bf16[2,2,16,512]{3,2,1,0:T(8,128)(2,1)S(1)}, bf16[2,2,16,512]{3,2,1,0:T(8,128)(2,1)S(1)}, u32[]{:S(2)}, u32[]{:S(2)}) collective-permute-start(bf16[2,2,16,512]{3,2,1,0:T(8,128)(2,1)S(1)} %get-tuple-element.111), channel_id=1, source_target_pairs={{16,0},{20,4},{24,8},{28,12},{17,1},{21,5},{25,9},{29,13},{18,2},{... | collective-permute-start | bytes 196616 | tf_op jit(solution)/shard_map/ppermute | solution.py:422
  49.4 0.8 %copy-start.4 = (bf16[512,512]{1,0:T(8,128)(2,1)}, bf16[512,512]{1,0:T(8,128)(2,1)S(1)}, u32[]{:S(2)}) copy-start(bf16[512,512]{1,0:T(8,128)(2,1)S(1)} %collective-permute-done.13.att_far) | copy-start | bytes 1572868
  50.2 0.8 %copy-start.6 = (bf16[512,512]{1,0:T(8,128)(2,1)}, bf16[512,512]{1,0:T(8,128)(2,1)S(1)}, u32[]{:S(2)}) copy-start(bf16[512,512]{1,0:T(8,128)(2,1)S(1)} %collective-permute-done.14.gq_far) | copy-start | bytes 1572868
  51.0 1.0 %copy-start.3 = (bf16[512,512]{1,0:T(8,128)(2,1)S(1)}, bf16[512,512]{1,0:T(8,128)(2,1)}, u32[]{:S(2)}) copy-start(bf16[512,512]{1,0:T(8,128)(2,1)} %copy-done.2) | copy-start | bytes 1572868
  52.1 1.0 %copy-start.5 = (bf16[512,512]{1,0:T(8,128)(2,1)S(1)}, bf16[512,512]{1,0:T(8,128)(2,1)}, u32[]{:S(2)}) copy-start(bf16[512,512]{1,0:T(8,128)(2,1)} %copy-done.4) | copy-start | bytes 1572868
  53.1 1.0 %copy-start.7 = (bf16[512,512]{1,0:T(8,128)(2,1)S(1)}, bf16[512,512]{1,0:T(8,128)(2,1)}, u32[]{:S(2)}) copy-start(bf16[512,512]{1,0:T(8,128)(2,1)} %copy-done.6) | copy-start | bytes 1572868
  58.4 1.3 %collective-permute-start.20 = (bf16[2,16,512]{2,1,0:T(8,128)(2,1)S(1)}, bf16[2,16,512]{2,1,0:T(8,128)(2,1)S(1)}, u32[]{:S(2)}, u32[]{:S(2)}) collective-permute-start(bf16[2,16,512]{2,1,0:T(8,128)(2,1)S(1)} %fusion.3), channel_id=1, source_target_pairs={{0,1},{1,0},{2,3},{3,2},{4,5},{5,4},{6,7},{7,6},{8,9},{9,8},{10,11... | collective-permute-start | bytes 98312 | tf_op jit(solution)/shard_map/ppermute | solution.py:414
